TPU v7x, 256 devices: a whole 4x4x8 slice. The times are simulated.
256 devices in a mesh: gz: 2 (over y_lo), gy: 8 (over x, core), gx: 16 (over z, y_hi).
Axes of the slice: x: 4, y: 4 (y_hi: 2, y_lo: 2; y = y_hi * 2 + y_lo), z: 8, core: 2. Of those that a mesh axis runs over, the one named last changes fastest.
Arguments:
- patches: bfloat16 [4, 32, 64, 128, 128], P('gz', 'gy', 'gx'), may hold values from -6 to 6
- prior_patches: bfloat16 [32, 64, 128, 128], P('gy', 'gx'), may hold values from -6 to 6
- node_patch: int32 [4, 128, 256], P(None, 'gy', 'gx'), may hold values from 0 to 35, as said below
- node_weight: float32 [4, 128, 256], P(None, 'gy', 'gx'), may hold values from 0.1 to 0.5
- edges: int32 [4, 128, 256], P(None, 'gy', 'gx'), may hold values from 0 to 1, as said below
- flow_weight: float32 [4, 128, 256], P('gz', 'gy', 'gx'), may hold values from 0.1 to 1
- start_offset: float32 [4, 2, 128, 256], P('gz', None, 'gy', 'gx'), may hold values from -6 to 6
Outputs:
- flow_field: float32 [4, 2, 32, 64], P('gz', None, 'gy', 'gx')
- displacement: float32 [4, 2, 128, 256], P('gz', None, 'gy', 'gx')
Inputs may be any that keep to these rules, and one draw needn't show every extreme that they name: `node_patch`: for the node in row i and column j of its block of 16 x 16 nodes, every entry is (r + a) * 6 + c + b with r = 1 + i * 4 // 16, c = 1 + j * 4 // 16 and a, b each one of -1, 0, 1. `edges`: entry 1 of a node equals entry 0 of the node in the previous column, entry 3 equals entry 2 of the node in the previous row; springs that would leave the grid are 0.
All inputs are finite; a program needn't handle non-finite values.
Results may differ from a plain program's by a relative error of at most 0.0003.
Values may be sent and summed in bfloat16 or wider, within the bound.
No kernel may reach another device: no remote copies, remote signals or barrier semaphores. Data moves between devices by JAX's collectives and lax.ppermute only.
A program may use at most 64 MiB of HBM per device.

v0:
```python
import functools
import math

import jax
import jax.numpy as jnp
import ml_dtypes
import numpy as np
from jax import lax
from jax.experimental import pallas as pl
from jax.experimental.pallas import tpu as pltpu
from jax.sharding import PartitionSpec as P

STEPS = 3
STEP_SIZE = 0.35
N = 128
H = N // 2
F32 = jnp.float32
BF16 = jnp.bfloat16
GROUP = 32
EDGE = 3
VMEM_LIMIT = 40 * 1024 * 1024


def split_const(values):
    high = values.astype(ml_dtypes.bfloat16)
    low = (values - high.astype(np.float64)).astype(ml_dtypes.bfloat16)
    return high, low


@functools.lru_cache(maxsize=None)
def tables():
    pixel = np.arange(N)
    phase = 2.0 * np.pi / N * (np.outer(np.arange(H), pixel) % N)
    cosine, sine = np.cos(phase), np.sin(phase)
    sine[0] = np.cos(np.pi * pixel)
    norm = np.full(H, math.sqrt(2.0 / N))
    norm[0] = math.sqrt(1.0 / N)
    basis = np.concatenate([cosine * norm[:, None], sine * norm[:, None]])
    root = basis / np.sqrt(np.concatenate([norm, norm]))[:, None]
    wide = np.zeros((2 * N, 2 * N))
    wide[:N, 0:H], wide[:N, N : N + H] = root[:H].T, root[H:].T
    wide[N:, H:N], wide[N:, N + H :] = root[:H].T, root[H:].T
    back = np.zeros((2 * N, 2 * N))
    back[0:H, :N], back[N : N + H, :N] = basis[:H], basis[H:]
    back[H:N, N:], back[N + H :, N:] = basis[:H], basis[H:]
    offset = ((pixel + H) % N - H).astype(np.float64)
    moment = (basis * offset[None, :]) @ basis.T
    stacked = []
    for left in (root, moment):
        high, low = split_const(left)
        stacked.append(np.block([[high, high], [low, low]]))
    return (*split_const(wide), stacked[0], stacked[1], *split_const(back))


def dot(left, right):
    return jnp.dot(left, right, preferred_element_type=F32)


def halves(values):
    high = values.astype(BF16)
    return high, (values - high.astype(F32)).astype(BF16)


def left_product(stacked, values):
    high, low = halves(values)
    both = dot(stacked, jnp.concatenate([high, low], axis=0))
    return both[:N] + both[N:]


def spectrum(pixels, wide_high, wide_low, rows):
    return left_product(rows, dot(pixels, wide_high) + dot(pixels, wide_low))


def cross(prev, cur):
    lane = lax.broadcasted_iota(jnp.int32, (H, N), 1) % H == 0

    def part(start, stop, first_row):
        def quarter(whole, row, col):
            return whole[row + start : row + stop, col : col + N]

        pcc, pcs, psc, pss = (quarter(prev, r, c) for r in (0, H) for c in (0, N))
        qcc, qcs, qsc, qss = (quarter(cur, r, c) for r in (0, H) for c in (0, N))
        edge = lane[start:stop]
        u1, u2, u3, u4 = pcc * qcc, pss * qss, pcs * qcs, psc * qsc
        v1, v2, v3, v4 = pcc * qcs, pss * qsc, pcs * qcc, psc * qss
        w1, w2, w3, w4 = pcc * qsc, pss * qcs, pcs * qss, psc * qcc
        z = pcc * qss + pss * qcc - pcs * qsc - psc * qcs
        even, odd = u2 + u3, w3 - w2
        cc = u1 + u4 + jnp.where(edge, 0.0, even)
        cs = jnp.where(edge, even, (v1 - v3) + (v4 - v2))
        sc = (w1 - w4) + jnp.where(edge, 0.0, odd)
        ss = jnp.where(edge, odd, z)
        if first_row:
            top = lax.broadcasted_iota(jnp.int32, (stop - start, N), 0) == 0
            cc = jnp.where(top, u1 + jnp.where(edge, 0.0, u3), cc)
            cs = jnp.where(top, jnp.where(edge, u3, v1 - v3), cs)
            sc = jnp.where(top, u4 + jnp.where(edge, 0.0, u2), sc)
            ss = jnp.where(top, jnp.where(edge, u2, v4 - v2), ss)
        return jnp.concatenate([cc, cs], axis=1), jnp.concatenate([sc, ss], axis=1)

    first, rest = part(0, 8, True), part(8, H, False)
    return jnp.concatenate([first[0], rest[0], first[1], rest[1]], axis=0)


def moments(prev, cur, moment, back_high, back_low):
    values = cross(prev, cur)
    along_y = jnp.sum(values * left_product(moment, values), axis=0, keepdims=True)
    along_y = along_y[:, :N] + along_y[:, N:]
    high, low = halves(values)
    pixels = dot(high, back_high) + dot(low, back_high) + dot(high, back_low)
    return along_y, jnp.sum(pixels * pixels, axis=0, keepdims=True)


def placed_flows(along_y, power, section, first_col):
    lane = lax.broadcasted_iota(jnp.int32, (8, N), 1)
    offset = ((lane + H) % N - H).astype(F32)
    pad = jnp.zeros((2, N), F32)
    flows = jnp.zeros((8, N), F32)
    stacked_y = jnp.concatenate([pad, *along_y, pad], axis=0)
    for side in range(2):
        columns = jnp.concatenate([pad, *[p[:, side * N : (side + 1) * N] for p in power], pad], axis=0)
        energy = jnp.sum(columns, axis=1, keepdims=True) * (1.0 / (N * N)) + 1e-6
        mine = (lane < H) if side == 0 else (lane >= H)
        flow_y = jnp.sum(jnp.where(mine, stacked_y, 0.0), axis=1, keepdims=True) * (1.0 / (N * N)) / energy
        flow_x = jnp.sum(columns * offset, axis=1, keepdims=True) * (1.0 / (N * N)) / energy
        slot = section * 16 + 2 + first_col + side
        flows = jnp.where(lane == slot, flow_y, flows)
        flows = jnp.where(lane == slot + 8, flow_x, flows)
    return flows


def position(flags_ref):
    return [flags_ref[i] for i in range(7)]


def pair_of(ref, index):
    return jnp.concatenate([ref[(*index, 0)], ref[(*index, 1)]], axis=1)


def local_kernel(flags_ref, patches_ref, start_ref, weight_ref, edges_ref, nodes_ref, share_ref,
                 wide_high, wide_low, rows, moment, back_high, back_low, spec_ref, flows_ref, static_ref, sums_y, sums_x):
    odd = flags_ref[1]
    forward = (wide_high[...], wide_low[...], rows[...])
    inverse = (moment[...], back_high[...], back_low[...])
    static_ref[...] = jnp.zeros_like(static_ref)
    fields = [start_ref[s, c] for s in range(2) for c in range(2)]
    fields += [weight_ref[0], weight_ref[1], edges_ref[0].astype(F32), edges_ref[2].astype(F32)]
    fields += [nodes_ref[k].astype(F32) for k in range(4)] + [share_ref[k] for k in range(4)]
    for at, field in enumerate(fields):
        row, lane = at // 4 * 16, at % 4 * GROUP + EDGE
        static_ref[row : row + 16, lane : lane + 16] = field

    @pl.loop(0, 8)
    def _(unit):
        half, py = unit // 4, unit % 4
        first = 2 * (half ^ odd)
        pair = [jnp.concatenate([patches_ref[s, py, first], patches_ref[s, py, first + 1]], axis=1) for s in range(2)]
        prev, cur = (spectrum(p, *forward) for p in pair)
        spec_ref[half, py] = prev
        along_y, power = moments(prev, cur, *inverse)
        sums_y[unit] = along_y
        sums_x[unit] = power

    flows = jnp.zeros((8, N), F32)
    for half in range(2):
        flows += placed_flows([sums_y[half * 4 + i] for i in range(4)], [sums_x[half * 4 + i] for i in range(4)], 1, 2 * (half ^ odd))
    flows_ref[...] = flows


def chained_kernel(half, flags_ref, prior_ref, recv_ref, spec_ref, before_ref, static_ref,
                   wide_high, wide_low, rows, moment, back_high, back_low, out_ref, *field_ref):
    at_start, odd = flags_ref[0] == 0, flags_ref[1]
    forward = (wide_high[...], wide_low[...], rows[...])
    inverse = (moment[...], back_high[...], back_low[...])
    first = 2 * (half ^ odd)
    sums = []
    for py in range(4):
        own = jnp.concatenate([prior_ref[py, first], prior_ref[py, first + 1]], axis=1)
        other = jnp.concatenate([recv_ref[py, 0], recv_ref[py, 1]], axis=1)
        pixels = jnp.where(at_start, own, other)
        sums.append(moments(spectrum(pixels, *forward), spec_ref[py], *inverse))
    flows = before_ref[0:8, :] + placed_flows([s[0] for s in sums], [s[1] for s in sums], 0, first)
    out_ref[0:8, :] = flows
    out_ref[8:, :] = static_ref[...]
    if field_ref:
        for s in range(2):
            for c in range(2):
                lane = s * 16 + c * 8 + 2
                field_ref[0][s, c] = flows[2:6, lane : lane + 4]


def columns_kernel(flags_ref, own_ref, near_ref, far_ref, low_ref, high_ref):
    _, odd, has_left, has_right, odd_row, _, _ = position(flags_ref)
    own, near, far = own_ref[...], near_ref[...], far_ref[...]
    left = jnp.where(odd == 1, near, far) * has_left.astype(F32)
    right = jnp.where(odd == 1, far, near) * has_right.astype(F32)

    lane = lax.broadcasted_iota(jnp.int32, (8, N), 1) % 8
    flows = jnp.where(lane < 2, pltpu.roll(left[:8], N - 4, 1), jnp.where(lane < 6, own[:8], pltpu.roll(right[:8], 4, 1)))
    lane = lax.broadcasted_iota(jnp.int32, (64, N), 1) % GROUP
    nodes = jnp.where(lane < EDGE, pltpu.roll(left[8:], N - 16, 1),
                      jnp.where(lane < EDGE + 16, own[8:], jnp.where(lane < 2 * EDGE + 16, pltpu.roll(right[8:], 16, 1), 0.0)))
    top = jnp.concatenate([flows] + [nodes[16 * f : 16 * f + 8] for f in range(4)], axis=0)
    bottom = jnp.concatenate([flows] + [nodes[16 * f + 8 : 16 * f + 16] for f in range(4)], axis=0)
    low_ref[...] = top
    high_ref[...] = bottom


def shifted_rows(values, by):
    return pltpu.roll(values, by % values.shape[0], 0)


def nodes_kernel(flags_ref, top_ref, bottom_ref, near_ref, far_ref, spread_ref, out_ref):
    _, _, _, _, odd_row, has_up, has_down = position(flags_ref)
    top, bottom, near, far = top_ref[...], bottom_ref[...], near_ref[...], far_ref[...]
    above = jnp.where(odd_row == 1, near, far) * has_up.astype(F32)
    below = jnp.where(odd_row == 1, far, near) * has_down.astype(F32)

    row = lax.broadcasted_iota(jnp.int32, (8, N), 0)
    window = jnp.where(row < 2, pltpu.roll(above[:8], 4, 0), jnp.where(row < 6, top[:8], pltpu.roll(below[:8], 4, 0)))

    def field(at):
        part = slice(8 + 8 * at, 16 + 8 * at)
        return jnp.concatenate([above[part], top[part], bottom[part], below[part]], axis=0)

    moved, mixed, patch, share = (field(at) for at in range(4))

    narrow = window[:, : 4 * 8]
    part1 = narrow.astype(BF16)
    rest = narrow - part1.astype(F32)
    part2 = rest.astype(BF16)
    part3 = (rest - part2.astype(F32)).astype(BF16)
    spread = dot(jnp.concatenate([part1, part2, part3], axis=1), spread_ref[...])
    upper = row < 4
    lines = [[jnp.broadcast_to(spread[r : r + 1, b * N : (b + 1) * N], (8, N)) for b in range(3)] for r in range(8)]

    def patch_row(r):
        return lines[min(max(r, 0), 7)]

    rows4 = lax.broadcasted_iota(jnp.int32, (32, N), 0)
    lanes4 = lax.broadcasted_iota(jnp.int32, (32, N), 1)
    base = (1 + (rows4 + 8) % 16 // 4) * 6 + 1 + (lanes4 % GROUP + 16 - EDGE) % 16 // 4
    step = patch - base.astype(F32)

    def over_groups(values):
        values = values + pltpu.roll(values, GROUP, 1)
        return values + pltpu.roll(values, 2 * GROUP, 1)

    target = jnp.zeros((32, N), F32)
    for a in range(-1, 2):
        for b in range(-1, 2):
            weight = over_groups(jnp.where(step == float(6 * a + b), share, 0.0))
            moving = jnp.concatenate([jnp.where(upper, patch_row(2 * t + a)[b + 1], patch_row(2 * t + 1 + a)[b + 1]) for t in range(4)], axis=0)
            target = target + weight * moving

    group = lanes4 // GROUP
    stiff_pair = jnp.where(group < 2, mixed, 0.0)
    only0 = jnp.where(group == 0, mixed, 0.0)
    only1 = jnp.where(group == 1, mixed, 0.0)
    stiffness = only0 + pltpu.roll(only0, GROUP, 1) + pltpu.roll(only1, GROUP, 1) + pltpu.roll(only1, 2 * GROUP, 1)
    right = over_groups(jnp.where(group == 2, mixed, 0.0))
    down = over_groups(jnp.where(group == 3, mixed, 0.0))
    left = pltpu.roll(right, 1, 1)
    up = shifted_rows(down, 1)
    for _ in range(STEPS):
        springs = right * (pltpu.roll(moved, N - 1, 1) - moved) + left * (pltpu.roll(moved, 1, 1) - moved)
        springs = springs + down * (shifted_rows(moved, -1) - moved) + up * (shifted_rows(moved, 1) - moved)
        moved = moved + STEP_SIZE * (stiffness * (target - moved) + springs)
    for s in range(2):
        for c in range(2):
            lane = (2 * s + c) * GROUP + EDGE
            out_ref[s, c] = moved[8:24, lane : lane + 16]


@functools.lru_cache(maxsize=None)
def spread_table():
    table = np.zeros((3, 32, 3 * N))
    for b in range(3):
        for lane in range(N):
            group, node = lane // GROUP, lane % GROUP - EDGE
            col = node // 4 + 2 + b - 1
            if 0 <= col < 8 and node < 19:
                table[:, group * 8 + col, b * N + lane] = 1.0
    return table.reshape(96, 3 * N).astype(ml_dtypes.bfloat16)


def call(kernel, inputs, out_shapes, scratch=(), flops=0, moved=0):
    return pl.pallas_call(
        kernel,
        out_shape=out_shapes,
        in_specs=[pl.BlockSpec(memory_space=pltpu.SMEM)] + [pl.BlockSpec(memory_space=pltpu.VMEM)] * (len(inputs) - 1),
        out_specs=jax.tree.map(lambda _: pl.BlockSpec(memory_space=pltpu.VMEM), out_shapes),
        scratch_shapes=scratch,
        compiler_params=pltpu.CompilerParams(vmem_limit_bytes=VMEM_LIMIT),
        cost_estimate=pl.CostEstimate(flops=flops, bytes_accessed=moved, transcendentals=0),
    )(*inputs)


def f32(*shape):
    return jax.ShapeDtypeStruct(shape, F32)


def near_partner(count):
    return [(i, i ^ 1) for i in range(count)]


def far_partner(count):
    pairs = []
    for i in range(count):
        other = i + 1 if i % 2 else i - 1
        pairs.append((i, other if 0 <= other < count else i))
    return pairs


def body(patches, prior_patches, node_patch, node_weight, edges, flow_weight, start_offset):
    gz, gy, gx = (lax.axis_index(a) for a in ("gz", "gy", "gx"))
    rows, cols = lax.axis_size("gy"), lax.axis_size("gx")
    odd = gx % 2
    flags = jnp.stack([gz, odd, gx > 0, gx < cols - 1, gy % 2, gy > 0, gy < rows - 1]).astype(jnp.int32)
    consts = [jnp.asarray(t) for t in tables()]
    along_z = [(0, 1)]

    last = patches[1]
    arriving = []
    for half in range(2):
        chunk = lax.dynamic_slice_in_dim(last, 2 * (half ^ odd), 2, axis=1)
        arriving.append(lax.ppermute(chunk, "gz", along_z))

    spec, flows, static = call(
        local_kernel,
        [flags, patches, start_offset, flow_weight, edges, node_patch, node_weight, *consts],
        [f32(2, 4, N, 2 * N), f32(8, N), f32(64, N)],
        scratch=[pltpu.VMEM((8, 1, N), F32), pltpu.VMEM((8, 1, 2 * N), F32)],
        flops=5_000_000_000, moved=4_000_000,
    )
    (first,) = call(
        functools.partial(chained_kernel, 0),
        [flags, prior_patches, arriving[0], spec[0], flows, static, *consts],
        [f32(72, N)], flops=1_000_000_000, moved=2_000_000,
    )
    from_far = lax.ppermute(first, "gx", far_partner(cols))
    own, flow_field = call(
        functools.partial(chained_kernel, 1),
        [flags, prior_patches, arriving[1], spec[1], first, static, *consts],
        [f32(72, N), f32(2, 2, 4, 4)], flops=1_000_000_000, moved=2_000_000,
    )
    from_near = lax.ppermute(own, "gx", near_partner(cols))
    top, bottom = call(columns_kernel, [flags, own, from_near, from_far], [f32(40, N), f32(40, N)])
    odd_row = flags[4] == 1
    to_near = jnp.where(odd_row, top, bottom)
    to_far = jnp.where(odd_row, bottom, top)
    row_near = lax.ppermute(to_near, "gy", near_partner(rows))
    row_far = lax.ppermute(to_far, "gy", far_partner(rows))
    displacement = call(
        nodes_kernel, [flags, top, bottom, row_near, row_far, jnp.asarray(spread_table())], f32(2, 2, 16, 16))
    return flow_field, displacement


def solution(mesh):
    return jax.shard_map(
        body,
        mesh=mesh,
        in_specs=(
            P("gz", "gy", "gx", None, None),
            P("gy", "gx", None, None),
            P(None, "gy", "gx"),
            P(None, "gy", "gx"),
            P(None, "gy", "gx"),
            P("gz", "gy", "gx"),
            P("gz", None, "gy", "gx"),
        ),
        out_specs=(P("gz", None, "gy", "gx"), P("gz", None, "gy", "gx")),
        check_vma=False,
    )
```

profile of v0, /device:TPU:129, one launch (start us, length us, event | category | flops | bytes accessed | tf_op | source)
XLA Modules:
  0.0 44.3 jit_solution(499961409797130231)
XLA Ops:
  0.7 1.0 %slice-done = bf16[1,4,4,128,128]{4,3,2,1,0:T(8,128)(2,1)S(1)} async-done(((bf16[2,4,4,128,128]{4,3,2,1,0:T(8,128)(2,1)}), bf16[1,4,4,128,128]{4,3,2,1,0:T(8,128)(2,1)S(1)}, s32[]{:S(2)}) %slice-start) | async-done | bytes 524312 | tf_op jit(solution)/shard_map/slice | solution.py:323
  1.7 0.0 copy-start.9
  1.7 0.0 copy-start.10
  1.8 3.3 %collective-permute-start.1 = (bf16[4,2,128,128]{3,2,1,0:T(8,128)(2,1)S(1)}, bf16[4,2,128,128]{3,2,1,0:T(8,128)(2,1)S(1)}, u32[]{:S(2)}, u32[]{:S(2)}) collective-permute-start(bf16[4,2,128,128]{3,2,1,0:T(8,128)(2,1)S(1)} %get-tuple-element.18), channel_id=1, source_target_pairs={{0,128},{1,129},{2,130},{3,131},{4,132},{5,133},{6,134},{7,135},{8... | collective-permute-start | bytes 786440 | tf_op jit(solution)/shard_map/ppermute | solution.py:327
  5.1 0.0 copy-start.3
  5.1 0.0 copy-start.4
  5.2 1.3 %collective-permute-start = (bf16[4,2,128,128]{3,2,1,0:T(8,128)(2,1)S(1)}, bf16[4,2,128,128]{3,2,1,0:T(8,128)(2,1)S(1)}, u32[]{:S(2)}, u32[]{:S(2)}) collective-permute-start(bf16[4,2,128,128]{3,2,1,0:T(8,128)(2,1)S(1)} %get-tuple-element.19), channel_id=1, source_target_pairs={{0,128},{1,129},{2,130},{3,131},{4,132},{5,133},{6,134},{7,135},{8... | collective-permute-start | bytes 786440 | tf_op jit(solution)/shard_map/ppermute | solution.py:327
  6.5 0.1 stack.47.flags_ref
  6.7 0.0 copy-start.11
  6.7 0.9 %copy-done.11 = bf16[256,256]{1,0:T(8,128)(2,1)S(1)} copy-done((bf16[256,256]{1,0:T(8,128)(2,1)S(1)}, bf16[256,256]{1,0:T(8,128)(2,1)}, u32[]{:S(2)}) %copy-start.11) | copy-done | bytes 131096
  7.6 0.9 %copy-done.13 = bf16[256,256]{1,0:T(8,128)(2,1)S(1)} copy-done((bf16[256,256]{1,0:T(8,128)(2,1)S(1)}, bf16[256,256]{1,0:T(8,128)(2,1)}, u32[]{:S(2)}) %copy-start.13) | copy-done | bytes 131096
  8.5 0.9 %copy-done.15 = bf16[256,256]{1,0:T(8,128)(2,1)S(1)} copy-done((bf16[256,256]{1,0:T(8,128)(2,1)S(1)}, bf16[256,256]{1,0:T(8,128)(2,1)}, u32[]{:S(2)}) %copy-start.15) | copy-done | bytes 131096
  9.4 6.8 %shard_map.149 = (f32[2,4,128,256]{3,2,1,0:T(8,128)S(1)}, f32[8,128]{1,0:T(8,128)S(1)}, f32[64,128]{1,0:T(8,128)S(1)}) custom-call(s32[7]{0:T(128)S(1)} %stack.47.flags_ref, bf16[2,4,4,128,128]{4,3,2,1,0:T(8,128)(2,1)S(1)} %copy-done, f32[2,2,16,16]{3,2,1,0:T(8,128)S(1)} %copy-done.3, f32[2,16,16]{2,1,0:T(8,128)S(1)} %copy-done.7, ...), custom_call_target="tpu_custom_call" | custom-call | flops 5000000000 | bytes 4000000 | tf_op jit(solution)/shard_map/pallas_call | solution.py:288
  16.2 0.0 copy-start.12
  16.2 0.0 copy-start.14
  16.2 0.0 copy-start.16
  16.3 0.1 slice_bitcast_fusion
  16.3 0.9 %copy-done.2 = bf16[4,4,128,128]{3,2,1,0:T(8,128)(2,1)S(1)} copy-done((bf16[4,4,128,128]{3,2,1,0:T(8,128)(2,1)S(1)}, bf16[4,4,128,128]{3,2,1,0:T(8,128)(2,1)}, u32[]{:S(2)}) %copy-start.2) | copy-done | bytes 524312
  17.2 0.0 copy-done.12
  17.3 0.0 copy-done.14
  17.3 0.0 copy-done.16
  17.4 2.7 %shard_map.150.before_ref = f32[72,128]{1,0:T(8,128)S(1)} custom-call(s32[7]{0:T(128)S(1)} %stack.47.flags_ref, bf16[4,4,128,128]{3,2,1,0:T(8,128)(2,1)S(1)} %copy-done.2, bf16[4,2,128,128]{3,2,1,0:T(8,128)(2,1)S(1)} %collective-permute-done.1.recv_ref, f32[4,128,256]{2,1,0:T(8,128)S(1)} %get-tuple-element.16.spec_ref, ...), custom_call_target="tpu_custom_call" | custom-call | flops 1000000000 | bytes 2000000 | tf_op jit(solution)/shard_map/pallas_call | solution.py:288
  20.1 3.4 %shard_map.151 = (f32[72,128]{1,0:T(8,128)S(1)}, f32[2,2,4,4]{3,2,1,0:T(4,128)}) custom-call(s32[7]{0:T(128)S(1)} %stack.47.flags_ref, bf16[4,4,128,128]{3,2,1,0:T(8,128)(2,1)S(1)} %copy-done.2, bf16[4,2,128,128]{3,2,1,0:T(8,128)(2,1)S(1)} %collective-permute-done.recv_ref, f32[4,128,256]{2,1,0:T(8,128)S(1)} %get-tuple-element.17.spec_ref, ...), custom_call_target="tpu_custom_call" | custom-call | flops 1000000000 | bytes 2000000 | tf_op jit(solution)/shard_map/pallas_call | solution.py:288
  23.5 2.6 %collective-permute-start.2 = (f32[72,128]{1,0:T(8,128)S(1)}, f32[72,128]{1,0:T(8,128)S(1)}, u32[]{:S(2)}, u32[]{:S(2)}) collective-permute-start(f32[72,128]{1,0:T(8,128)S(1)} %get-tuple-element.13.own_ref), channel_id=1, source_target_pairs={{0,1},{1,0},{2,3},{3,2},{4,5},{5,4},{6,7},{7,6},{8,9},{9,8},{10,11... | collective-permute-start | bytes 110600 | tf_op jit(solution)/shard_map/ppermute | solution.py:347
  26.2 1.9 %collective-permute-start.3 = (f32[72,128]{1,0:T(8,128)S(1)}, f32[72,128]{1,0:T(8,128)S(1)}, u32[]{:S(2)}, u32[]{:S(2)}) collective-permute-start(f32[72,128]{1,0:T(8,128)S(1)} %shard_map.150.before_ref), channel_id=1, source_target_pairs={{0,0},{1,2},{2,1},{3,4},{4,3},{5,6},{6,5},{7,8},{8,7},{9,10},{10,9... | collective-permute-start | bytes 110600 | tf_op jit(solution)/shard_map/ppermute | solution.py:341
  28.1 0.0 copy-start.1
  28.1 6.4 %collective-permute-done.3.far_ref = f32[72,128]{1,0:T(8,128)S(1)} collective-permute-done((f32[72,128]{1,0:T(8,128)S(1)}, f32[72,128]{1,0:T(8,128)S(1)}, u32[]{:S(2)}, u32[]{:S(2)}) %collective-permute-start.3) | collective-permute-done | bytes 36896 | tf_op jit(solution)/shard_map/ppermute | solution.py:341
  34.5 0.6 %shard_map.152 = (f32[40,128]{1,0:T(8,128)S(1)}, f32[40,128]{1,0:T(8,128)S(1)}) custom-call(s32[7]{0:T(128)S(1)} %stack.47.flags_ref, f32[72,128]{1,0:T(8,128)S(1)} %get-tuple-element.13.own_ref, f32[72,128]{1,0:T(8,128)S(1)} %collective-permute-done.2.near_ref, f32[72,128]{1,0:T(8,128)S(1)} %collective-permute-done.3.far_ref), custom_call_target="tpu_custom_call" | custom-call | tf_op jit(solution)/shard_map/pallas_call | solution.py:288
  35.1 2.5 %collective-permute-start.4 = (f32[40,128]{1,0:T(8,128)S(1)}, f32[40,128]{1,0:T(8,128)S(1)}, u32[]{:S(2)}, u32[]{:S(2)}) collective-permute-start(f32[40,128]{1,0:T(8,128)S(1)} %get-tuple-element.21), channel_id=1, source_target_pairs={{0,16},{16,0},{32,48},{48,32},{64,80},{80,64},{96,112},{112,96},{1... | collective-permute-start | bytes 61448 | tf_op jit(solution)/shard_map/ppermute | solution.py:352
  37.6 3.0 %collective-permute-start.5 = (f32[40,128]{1,0:T(8,128)S(1)}, f32[40,128]{1,0:T(8,128)S(1)}, u32[]{:S(2)}, u32[]{:S(2)}) collective-permute-start(f32[40,128]{1,0:T(8,128)S(1)} %get-tuple-element.20), channel_id=1, source_target_pairs={{0,0},{16,32},{32,16},{48,64},{64,48},{80,96},{96,80},{112,112},{1... | collective-permute-start | bytes 61448 | tf_op jit(solution)/shard_map/ppermute | solution.py:353
  40.6 2.1 %collective-permute-done.5.far_ref = f32[40,128]{1,0:T(8,128)S(1)} collective-permute-done((f32[40,128]{1,0:T(8,128)S(1)}, f32[40,128]{1,0:T(8,128)S(1)}, u32[]{:S(2)}, u32[]{:S(2)}) %collective-permute-start.5) | collective-permute-done | bytes 20512 | tf_op jit(solution)/shard_map/ppermute | solution.py:353
  42.7 1.6 %shard_map.153 = f32[2,2,16,16]{3,2,1,0:T(8,128)} custom-call(s32[7]{0:T(128)S(1)} %stack.47.flags_ref, f32[40,128]{1,0:T(8,128)S(1)} %get-tuple-element.14.top_ref, f32[40,128]{1,0:T(8,128)S(1)} %get-tuple-element.15.bottom_ref, f32[40,128]{1,0:T(8,128)S(1)} %collective-permute-done.4.near_ref, f32[40,128]{1,0:T(8,128)S(1)} %collective-permute-done.5.far_ref, ...), custom_call_target="tpu_custom_call" | custom-call | tf_op jit(solution)/shard_map/pallas_call | solution.py:288
  (25 shorter events, 0.1 us)
Async XLA Ops:
  0.6 1.0 %slice-start = ((bf16[2,4,4,128,128]{4,3,2,1,0:T(8,128)(2,1)}), bf16[1,4,4,128,128]{4,3,2,1,0:T(8,128)(2,1)S(1)}, s32[]{:S(2)}) async-start(bf16[2,4,4,128,128]{4,3,2,1,0:T(8,128)(2,1)} %patches_ref.1), calls=%async_computation | async-start | bytes 1048576 | tf_op jit(solution)/shard_map/slice | solution.py:323
  0.7 5.9 %copy-start = (bf16[2,4,4,128,128]{4,3,2,1,0:T(8,128)(2,1)S(1)}, bf16[2,4,4,128,128]{4,3,2,1,0:T(8,128)(2,1)}, u32[]{:S(2)}) copy-start(bf16[2,4,4,128,128]{4,3,2,1,0:T(8,128)(2,1)} %patches_ref.1) | copy-start | bytes 3145732
  1.7 4.9 %copy-start.5 = (s32[4,16,16]{2,1,0:T(8,128)S(1)}, s32[4,16,16]{2,1,0:T(8,128)}, u32[]{:S(2)}) copy-start(s32[4,16,16]{2,1,0:T(8,128)} %nodes_ref.1) | copy-start | bytes 12292
  1.7 4.9 %copy-start.6 = (f32[4,16,16]{2,1,0:T(8,128)S(1)}, f32[4,16,16]{2,1,0:T(8,128)}, u32[]{:S(2)}) copy-start(f32[4,16,16]{2,1,0:T(8,128)} %share_ref.1) | copy-start | bytes 12292
  1.7 4.9 %copy-start.7 = (f32[2,16,16]{2,1,0:T(8,128)S(1)}, f32[2,16,16]{2,1,0:T(8,128)}, u32[]{:S(2)}) copy-start(f32[2,16,16]{2,1,0:T(8,128)} %weight_ref.1) | copy-start | bytes 6148
  1.7 4.9 %copy-start.8 = (bf16[256,256]{1,0:T(8,128)(2,1)S(1)}, bf16[256,256]{1,0:T(8,128)(2,1)}, u32[]{:S(2)}) copy-start(bf16[256,256]{1,0:T(8,128)(2,1)} %constant.55.clone.wide_high) | copy-start | bytes 393220
  1.7 4.9 %copy-start.9 = (bf16[256,256]{1,0:T(8,128)(2,1)S(1)}, bf16[256,256]{1,0:T(8,128)(2,1)}, u32[]{:S(2)}) copy-start(bf16[256,256]{1,0:T(8,128)(2,1)} %constant.56.clone.wide_low) | copy-start | bytes 393220
  1.7 4.9 %copy-start.10 = (bf16[256,256]{1,0:T(8,128)(2,1)S(1)}, bf16[256,256]{1,0:T(8,128)(2,1)}, u32[]{:S(2)}) copy-start(bf16[256,256]{1,0:T(8,128)(2,1)} %constant.57.clone.rows) | copy-start | bytes 393220
  1.8 14.6 %collective-permute-start.1 = (bf16[4,2,128,128]{3,2,1,0:T(8,128)(2,1)S(1)}, bf16[4,2,128,128]{3,2,1,0:T(8,128)(2,1)S(1)}, u32[]{:S(2)}, u32[]{:S(2)}) collective-permute-start(bf16[4,2,128,128]{3,2,1,0:T(8,128)(2,1)S(1)} %get-tuple-element.18), channel_id=1, source_target_pairs={{0,128},{1,129},{2,130},{3,131},{4,132},{5,133},{6,134},{7,135},{8... | collective-permute-start | bytes 786440 | tf_op jit(solution)/shard_map/ppermute | solution.py:327
  5.1 1.5 %copy-start.3 = (f32[2,2,16,16]{3,2,1,0:T(8,128)S(1)}, f32[2,2,16,16]{3,2,1,0:T(8,128)}, u32[]{:S(2)}) copy-start(f32[2,2,16,16]{3,2,1,0:T(8,128)} %start_ref.1) | copy-start | bytes 12292
  5.1 1.5 %copy-start.4 = (s32[4,16,16]{2,1,0:T(8,128)S(1)}, s32[4,16,16]{2,1,0:T(8,128)}, u32[]{:S(2)}) copy-start(s32[4,16,16]{2,1,0:T(8,128)} %edges_ref.1) | copy-start | bytes 12292
  5.2 15.0 %collective-permute-start = (bf16[4,2,128,128]{3,2,1,0:T(8,128)(2,1)S(1)}, bf16[4,2,128,128]{3,2,1,0:T(8,128)(2,1)S(1)}, u32[]{:S(2)}, u32[]{:S(2)}) collective-permute-start(bf16[4,2,128,128]{3,2,1,0:T(8,128)(2,1)S(1)} %get-tuple-element.19), channel_id=1, source_target_pairs={{0,128},{1,129},{2,130},{3,131},{4,132},{5,133},{6,134},{7,135},{8... | collective-permute-start | bytes 786440 | tf_op jit(solution)/shard_map/ppermute | solution.py:327
  6.7 0.9 %copy-start.11 = (bf16[256,256]{1,0:T(8,128)(2,1)S(1)}, bf16[256,256]{1,0:T(8,128)(2,1)}, u32[]{:S(2)}) copy-start(bf16[256,256]{1,0:T(8,128)(2,1)} %constant.58.clone.moment) | copy-start | bytes 393220
  7.6 0.9 %copy-start.13 = (bf16[256,256]{1,0:T(8,128)(2,1)S(1)}, bf16[256,256]{1,0:T(8,128)(2,1)}, u32[]{:S(2)}) copy-start(bf16[256,256]{1,0:T(8,128)(2,1)} %constant.59.clone.back_high) | copy-start | bytes 393220
  8.5 0.9 %copy-start.15 = (bf16[256,256]{1,0:T(8,128)(2,1)S(1)}, bf16[256,256]{1,0:T(8,128)(2,1)}, u32[]{:S(2)}) copy-start(bf16[256,256]{1,0:T(8,128)(2,1)} %constant.60.clone.back_low) | copy-start | bytes 393220
  16.2 1.0 %copy-start.2 = (bf16[4,4,128,128]{3,2,1,0:T(8,128)(2,1)S(1)}, bf16[4,4,128,128]{3,2,1,0:T(8,128)(2,1)}, u32[]{:S(2)}) copy-start(bf16[4,4,128,128]{3,2,1,0:T(8,128)(2,1)} %prior_ref.3) | copy-start | bytes 1572868
  16.2 1.1 %copy-start.12 = (bf16[256,256]{1,0:T(8,128)(2,1)S(1)}, bf16[256,256]{1,0:T(8,128)(2,1)}, u32[]{:S(2)}) copy-start(bf16[256,256]{1,0:T(8,128)(2,1)} %constant.58.clone.moment) | copy-start | bytes 393220
  16.2 1.1 %copy-start.14 = (bf16[256,256]{1,0:T(8,128)(2,1)S(1)}, bf16[256,256]{1,0:T(8,128)(2,1)}, u32[]{:S(2)}) copy-start(bf16[256,256]{1,0:T(8,128)(2,1)} %constant.59.clone.back_high) | copy-start | bytes 393220
  16.2 1.1 %copy-start.16 = (bf16[256,256]{1,0:T(8,128)(2,1)S(1)}, bf16[256,256]{1,0:T(8,128)(2,1)}, u32[]{:S(2)}) copy-start(bf16[256,256]{1,0:T(8,128)(2,1)} %constant.60.clone.back_low) | copy-start | bytes 393220
  23.5 4.6 %collective-permute-start.2 = (f32[72,128]{1,0:T(8,128)S(1)}, f32[72,128]{1,0:T(8,128)S(1)}, u32[]{:S(2)}, u32[]{:S(2)}) collective-permute-start(f32[72,128]{1,0:T(8,128)S(1)} %get-tuple-element.13.own_ref), channel_id=1, source_target_pairs={{0,1},{1,0},{2,3},{3,2},{4,5},{5,4},{6,7},{7,6},{8,9},{9,8},{10,11... | collective-permute-start | bytes 110600 | tf_op jit(solution)/shard_map/ppermute | solution.py:347
  26.2 8.3 %collective-permute-start.3 = (f32[72,128]{1,0:T(8,128)S(1)}, f32[72,128]{1,0:T(8,128)S(1)}, u32[]{:S(2)}, u32[]{:S(2)}) collective-permute-start(f32[72,128]{1,0:T(8,128)S(1)} %shard_map.150.before_ref), channel_id=1, source_target_pairs={{0,0},{1,2},{2,1},{3,4},{4,3},{5,6},{6,5},{7,8},{8,7},{9,10},{10,9... | collective-permute-start | bytes 110600 | tf_op jit(solution)/shard_map/ppermute | solution.py:341
  28.1 14.6 %copy-start.1 = (bf16[96,384]{1,0:T(8,128)(2,1)S(1)}, bf16[96,384]{1,0:T(8,128)(2,1)}, u32[]{:S(2)}) copy-start(bf16[96,384]{1,0:T(8,128)(2,1)} %constant.61.clone.spread_ref) | copy-start | bytes 221188
  35.1 5.5 %collective-permute-start.4 = (f32[40,128]{1,0:T(8,128)S(1)}, f32[40,128]{1,0:T(8,128)S(1)}, u32[]{:S(2)}, u32[]{:S(2)}) collective-permute-start(f32[40,128]{1,0:T(8,128)S(1)} %get-tuple-element.21), channel_id=1, source_target_pairs={{0,16},{16,0},{32,48},{48,32},{64,80},{80,64},{96,112},{112,96},{1... | collective-permute-start | bytes 61448 | tf_op jit(solution)/shard_map/ppermute | solution.py:352
  37.6 5.1 %collective-permute-start.5 = (f32[40,128]{1,0:T(8,128)S(1)}, f32[40,128]{1,0:T(8,128)S(1)}, u32[]{:S(2)}, u32[]{:S(2)}) collective-permute-start(f32[40,128]{1,0:T(8,128)S(1)} %get-tuple-element.20), channel_id=1, source_target_pairs={{0,0},{16,32},{32,16},{48,64},{64,48},{80,96},{96,80},{112,112},{1... | collective-permute-start | bytes 61448 | tf_op jit(solution)/shard_map/ppermute | solution.py:353
where the time goes:
time: 44.6 us; the launch traced here: 44.3 us
  Pallas kernels  15.2 us (34%)
  starting transfers between devices  14.7 us (33%)
  waiting for transfers between devices  8.43 us (19%)
  local copies, waits for them, and re-layouts  5 us (11%)
  between operations  0.96 us (2%)
    pallas_call x5, Pallas kernels, call(): pl.pallas_call(kernel, out_shape=out_shapes, in_specs=[pl.BlockSpec(memor...  15.2 us
    ppermute x1, waiting for transfers between devices, body(): from_far = lax.ppermute(first, 'gx', far_partner(cols))  6.36 us
    ppermute x2, starting transfers between devices, body(): arriving.append(lax.ppermute(chunk, 'gz', along_z))  4.65 us
    unnamed x34, local copies, waits for them, and re-layouts  3.78 us
    ppermute x1, starting transfers between devices, body(): row_far = lax.ppermute(to_far, 'gy', far_partner(rows))  3.02 us
    ppermute x1, starting transfers between devices, body(): from_near = lax.ppermute(own, 'gx', near_partner(cols))  2.62 us
    ppermute x1, starting transfers between devices, body(): row_near = lax.ppermute(to_near, 'gy', near_partner(rows))  2.48 us
    ppermute x1, waiting for transfers between devices, body(): row_far = lax.ppermute(to_far, 'gy', far_partner(rows))  2.06 us
  transfers between devices with their start and end apart: 6, of which 2 were waited for; matrix products, arithmetic and copies ran while one was open for 0% of the time, Pallas kernels for 22%

commit v1 on v0

--- a/solution.py
+++ b/solution.py
@@ -18,7 +18,7 @@
 BF16 = jnp.bfloat16
 GROUP = 32
 EDGE = 3
-VMEM_LIMIT = 40 * 1024 * 1024
+VMEM_LIMIT = 24 * 1024 * 1024
 
 
 def split_const(values):
@@ -49,7 +49,7 @@
     for left in (root, moment):
         high, low = split_const(left)
         stacked.append(np.block([[high, high], [low, low]]))
-    return (*split_const(wide), stacked[0], stacked[1], *split_const(back))
+    return np.stack([*split_const(wide), stacked[0], stacked[1], *split_const(back)])
 
 
 def dot(left, right):
@@ -129,19 +129,11 @@
     return flows
 
 
-def position(flags_ref):
-    return [flags_ref[i] for i in range(7)]
-
-
-def pair_of(ref, index):
-    return jnp.concatenate([ref[(*index, 0)], ref[(*index, 1)]], axis=1)
-
-
 def local_kernel(flags_ref, patches_ref, start_ref, weight_ref, edges_ref, nodes_ref, share_ref,
-                 wide_high, wide_low, rows, moment, back_high, back_low, spec_ref, flows_ref, static_ref, sums_y, sums_x):
+                 table_ref, spec_ref, flows_ref, static_ref, current, sums_y, sums_x):
     odd = flags_ref[1]
-    forward = (wide_high[...], wide_low[...], rows[...])
-    inverse = (moment[...], back_high[...], back_low[...])
+    forward = [table_ref[i] for i in range(3)]
+    inverse = [table_ref[i] for i in range(3, 6)]
     static_ref[...] = jnp.zeros_like(static_ref)
     fields = [start_ref[s, c] for s in range(2) for c in range(2)]
     fields += [weight_ref[0], weight_ref[1], edges_ref[0].astype(F32), edges_ref[2].astype(F32)]
@@ -150,14 +142,14 @@
         row, lane = at // 4 * 16, at % 4 * GROUP + EDGE
         static_ref[row : row + 16, lane : lane + 16] = field
 
-    @pl.loop(0, 8)
-    def _(unit):
+    for unit in range(8):
         half, py = unit // 4, unit % 4
         first = 2 * (half ^ odd)
-        pair = [jnp.concatenate([patches_ref[s, py, first], patches_ref[s, py, first + 1]], axis=1) for s in range(2)]
-        prev, cur = (spectrum(p, *forward) for p in pair)
-        spec_ref[half, py] = prev
-        along_y, power = moments(prev, cur, *inverse)
+        for section, result in ((0, spec_ref.at[half, py]), (1, current.at[unit])):
+            pixels = jnp.concatenate([patches_ref[section, py, first], patches_ref[section, py, first + 1]], axis=1)
+            result[...] = spectrum(pixels, *forward)
+    for unit in range(8):
+        along_y, power = moments(spec_ref[unit // 4, unit % 4], current[unit], *inverse)
         sums_y[unit] = along_y
         sums_x[unit] = power
 
@@ -167,18 +159,17 @@
     flows_ref[...] = flows
 
 
-def chained_kernel(half, flags_ref, prior_ref, recv_ref, spec_ref, before_ref, static_ref,
-                   wide_high, wide_low, rows, moment, back_high, back_low, out_ref, *field_ref):
+def chained_kernel(half, flags_ref, prior_ref, recv_ref, spec_ref, before_ref, static_ref, table_ref, out_ref, *rest):
+    *field_ref, previous = rest
     at_start, odd = flags_ref[0] == 0, flags_ref[1]
-    forward = (wide_high[...], wide_low[...], rows[...])
-    inverse = (moment[...], back_high[...], back_low[...])
+    forward = [table_ref[i] for i in range(3)]
+    inverse = [table_ref[i] for i in range(3, 6)]
     first = 2 * (half ^ odd)
-    sums = []
     for py in range(4):
         own = jnp.concatenate([prior_ref[py, first], prior_ref[py, first + 1]], axis=1)
         other = jnp.concatenate([recv_ref[py, 0], recv_ref[py, 1]], axis=1)
-        pixels = jnp.where(at_start, own, other)
-        sums.append(moments(spectrum(pixels, *forward), spec_ref[py], *inverse))
+        previous[py] = spectrum(jnp.where(at_start, own, other), *forward)
+    sums = [moments(previous[py], spec_ref[py], *inverse) for py in range(4)]
     flows = before_ref[0:8, :] + placed_flows([s[0] for s in sums], [s[1] for s in sums], 0, first)
     out_ref[0:8, :] = flows
     out_ref[8:, :] = static_ref[...]
@@ -189,32 +180,44 @@
                 field_ref[0][s, c] = flows[2:6, lane : lane + 4]
 
 
-def columns_kernel(flags_ref, own_ref, near_ref, far_ref, low_ref, high_ref):
-    _, odd, has_left, has_right, odd_row, _, _ = position(flags_ref)
-    own, near, far = own_ref[...], near_ref[...], far_ref[...]
-    left = jnp.where(odd == 1, near, far) * has_left.astype(F32)
-    right = jnp.where(odd == 1, far, near) * has_right.astype(F32)
-
+def beside(base, values, on_right):
     lane = lax.broadcasted_iota(jnp.int32, (8, N), 1) % 8
-    flows = jnp.where(lane < 2, pltpu.roll(left[:8], N - 4, 1), jnp.where(lane < 6, own[:8], pltpu.roll(right[:8], 4, 1)))
+    left = jnp.where(lane < 2, pltpu.roll(values[:8], N - 4, 1), base[:8])
+    right = jnp.where(lane >= 6, pltpu.roll(values[:8], 4, 1), base[:8])
+    flows = jnp.where(on_right, right, left)
     lane = lax.broadcasted_iota(jnp.int32, (64, N), 1) % GROUP
-    nodes = jnp.where(lane < EDGE, pltpu.roll(left[8:], N - 16, 1),
-                      jnp.where(lane < EDGE + 16, own[8:], jnp.where(lane < 2 * EDGE + 16, pltpu.roll(right[8:], 16, 1), 0.0)))
+    left = jnp.where(lane < EDGE, pltpu.roll(values[8:], N - 16, 1), base[8:])
+    right = jnp.where((lane >= EDGE + 16) & (lane < 2 * EDGE + 16), pltpu.roll(values[8:], 16, 1), base[8:])
+    return flows, jnp.where(on_right, right, left)
+
+
+def far_columns_kernel(flags_ref, static_ref, far_ref, out_ref):
+    base = jnp.concatenate([jnp.zeros((8, N), F32), static_ref[...]], axis=0)
+    flows, nodes = beside(base, far_ref[...] * flags_ref[2].astype(F32), flags_ref[1] == 1)
+    out_ref[0:8, :] = flows
+    out_ref[8:, :] = nodes
+
+
+def near_columns_kernel(flags_ref, own_ref, partial_ref, near_ref, to_near_ref, to_far_ref):
+    base = jnp.concatenate([partial_ref[0:8, :] + own_ref[0:8, :], partial_ref[8:, :]], axis=0)
+    flows, nodes = beside(base, near_ref[...], flags_ref[1] == 0)
     top = jnp.concatenate([flows] + [nodes[16 * f : 16 * f + 8] for f in range(4)], axis=0)
     bottom = jnp.concatenate([flows] + [nodes[16 * f + 8 : 16 * f + 16] for f in range(4)], axis=0)
-    low_ref[...] = top
-    high_ref[...] = bottom
+    odd = flags_ref[3] == 1
+    to_near_ref[...] = jnp.where(odd, top, bottom)
+    to_far_ref[...] = jnp.where(odd, bottom, top)
 
 
 def shifted_rows(values, by):
     return pltpu.roll(values, by % values.shape[0], 0)
 
 
-def nodes_kernel(flags_ref, top_ref, bottom_ref, near_ref, far_ref, spread_ref, out_ref):
-    _, _, _, _, odd_row, has_up, has_down = position(flags_ref)
-    top, bottom, near, far = top_ref[...], bottom_ref[...], near_ref[...], far_ref[...]
-    above = jnp.where(odd_row == 1, near, far) * has_up.astype(F32)
-    below = jnp.where(odd_row == 1, far, near) * has_down.astype(F32)
+def nodes_kernel(flags_ref, to_near_ref, to_far_ref, near_ref, far_ref, spread_ref, out_ref):
+    odd = flags_ref[3] == 1
+    near, far = near_ref[...], far_ref[...] * flags_ref[4].astype(F32)
+    above, below = jnp.where(odd, near, far), jnp.where(odd, far, near)
+    top = jnp.where(odd, to_near_ref[...], to_far_ref[...])
+    bottom = jnp.where(odd, to_far_ref[...], to_near_ref[...])
 
     row = lax.broadcasted_iota(jnp.int32, (8, N), 0)
     window = jnp.where(row < 2, pltpu.roll(above[:8], 4, 0), jnp.where(row < 6, top[:8], pltpu.roll(below[:8], 4, 0)))
@@ -315,44 +318,43 @@
 def body(patches, prior_patches, node_patch, node_weight, edges, flow_weight, start_offset):
     gz, gy, gx = (lax.axis_index(a) for a in ("gz", "gy", "gx"))
     rows, cols = lax.axis_size("gy"), lax.axis_size("gx")
-    odd = gx % 2
-    flags = jnp.stack([gz, odd, gx > 0, gx < cols - 1, gy % 2, gy > 0, gy < rows - 1]).astype(jnp.int32)
-    consts = [jnp.asarray(t) for t in tables()]
-    along_z = [(0, 1)]
-
-    last = patches[1]
+    odd, odd_row = gx % 2, gy % 2
+    has_far = (gx > 0) & (gx < cols - 1)
+    has_far_row = (gy > 0) & (gy < rows - 1)
+    flags = jnp.stack([gz, odd, has_far, odd_row, has_far_row]).astype(jnp.int32)
+    table = jnp.asarray(tables())
+
     arriving = []
     for half in range(2):
-        chunk = lax.dynamic_slice_in_dim(last, 2 * (half ^ odd), 2, axis=1)
-        arriving.append(lax.ppermute(chunk, "gz", along_z))
+        chunk = lax.dynamic_slice_in_dim(patches[1], 2 * (half ^ odd), 2, axis=1)
+        arriving.append(lax.ppermute(chunk, "gz", [(0, 1)]))
 
     spec, flows, static = call(
         local_kernel,
-        [flags, patches, start_offset, flow_weight, edges, node_patch, node_weight, *consts],
+        [flags, patches, start_offset, flow_weight, edges, node_patch, node_weight, table],
         [f32(2, 4, N, 2 * N), f32(8, N), f32(64, N)],
-        scratch=[pltpu.VMEM((8, 1, N), F32), pltpu.VMEM((8, 1, 2 * N), F32)],
+        scratch=[pltpu.VMEM((8, N, 2 * N), F32), pltpu.VMEM((8, 1, N), F32), pltpu.VMEM((8, 1, 2 * N), F32)],
         flops=5_000_000_000, moved=4_000_000,
     )
+    scratch = [pltpu.VMEM((4, N, 2 * N), F32)]
     (first,) = call(
         functools.partial(chained_kernel, 0),
-        [flags, prior_patches, arriving[0], spec[0], flows, static, *consts],
-        [f32(72, N)], flops=1_000_000_000, moved=2_000_000,
+        [flags, prior_patches, arriving[0], spec[0], flows, static, table],
+        [f32(72, N)], scratch, flops=2_000_000_000, moved=2_000_000,
     )
     from_far = lax.ppermute(first, "gx", far_partner(cols))
+    partial = call(far_columns_kernel, [flags, static, from_far], f32(72, N), flops=5_000_000_000, moved=2_000_000)
     own, flow_field = call(
         functools.partial(chained_kernel, 1),
-        [flags, prior_patches, arriving[1], spec[1], first, static, *consts],
-        [f32(72, N), f32(2, 2, 4, 4)], flops=1_000_000_000, moved=2_000_000,
+        [flags, prior_patches, arriving[1], spec[1], first, static, table],
+        [f32(72, N), f32(2, 2, 4, 4)], scratch, flops=2_000_000_000, moved=2_000_000,
     )
     from_near = lax.ppermute(own, "gx", near_partner(cols))
-    top, bottom = call(columns_kernel, [flags, own, from_near, from_far], [f32(40, N), f32(40, N)])
-    odd_row = flags[4] == 1
-    to_near = jnp.where(odd_row, top, bottom)
-    to_far = jnp.where(odd_row, bottom, top)
+    to_near, to_far = call(near_columns_kernel, [flags, own, partial, from_near], [f32(40, N), f32(40, N)])
     row_near = lax.ppermute(to_near, "gy", near_partner(rows))
     row_far = lax.ppermute(to_far, "gy", far_partner(rows))
     displacement = call(
-        nodes_kernel, [flags, top, bottom, row_near, row_far, jnp.asarray(spread_table())], f32(2, 2, 16, 16))
+        nodes_kernel, [flags, to_near, to_far, row_near, row_far, jnp.asarray(spread_table())], f32(2, 2, 16, 16))
     return flow_field, displacement
 
 

time: 44.6 us -> 36.9 us (0.83)
  the two profiles are of different devices: /device:TPU:129 before, /device:TPU:125 now
where the time goes in v1:
time: 36.9 us; the launch traced here: 36.5 us
  starting transfers between devices  14.9 us (40%)
  Pallas kernels  10.3 us (28%)
  waiting for transfers between devices  7.42 us (20%)
  local copies, waits for them, and re-layouts  2.97 us (8%)
  between operations  0.85 us (2%)
    pallas_call x6, Pallas kernels, call(): pl.pallas_call(kernel, out_shape=out_shapes, in_specs=[pl.BlockSpec(memor...  10.3 us
    ppermute x1, starting transfers between devices, body(): from_far = lax.ppermute(first, 'gx', far_partner(cols))  5.43 us
    ppermute x1, starting transfers between devices, body(): row_near = lax.ppermute(to_near, 'gy', near_partner(rows))  4.21 us
    ppermute x1, waiting for transfers between devices, body(): from_near = lax.ppermute(own, 'gx', near_partner(cols))  3.33 us
    ppermute x1, starting transfers between devices, body(): row_far = lax.ppermute(to_far, 'gy', far_partner(rows))  2.72 us
    ppermute x2, starting transfers between devices, body(): arriving.append(lax.ppermute(chunk, 'gz', [(0, 1)]))  2.58 us
    ppermute x1, waiting for transfers between devices, body(): row_far = lax.ppermute(to_far, 'gy', far_partner(rows))  2.35 us
    unnamed x18, local copies, waits for them, and re-layouts  1.76 us
  transfers between devices with their start and end apart: 6, of which 4 were waited for; matrix products, arithmetic and copies ran while one was open for 0% of the time, Pallas kernels for 22%

profile of v1, /device:TPU:125, one launch (start us, length us, event | category | flops | bytes accessed | tf_op | source)
XLA Modules:
  0.0 36.5 jit_solution(16004862155573478701)
XLA Ops:
  0.6 0.0 slice-start
  0.7 0.0 copy-start
  0.7 1.0 %slice-done = bf16[1,4,4,128,128]{4,3,2,1,0:T(8,128)(2,1)S(1)} async-done(((bf16[2,4,4,128,128]{4,3,2,1,0:T(8,128)(2,1)}), bf16[1,4,4,128,128]{4,3,2,1,0:T(8,128)(2,1)S(1)}, s32[]{:S(2)}) %slice-start) | async-done | bytes 524312 | tf_op jit(solution)/shard_map/slice | solution.py:329
  1.7 0.0 copy-start.3
  1.8 1.3 %collective-permute-start.1 = (bf16[4,2,128,128]{3,2,1,0:T(8,128)(2,1)S(1)}, bf16[4,2,128,128]{3,2,1,0:T(8,128)(2,1)S(1)}, u32[]{:S(2)}, u32[]{:S(2)}) collective-permute-start(bf16[4,2,128,128]{3,2,1,0:T(8,128)(2,1)S(1)} %get-tuple-element.18), channel_id=1, source_target_pairs={{0,128},{1,129},{2,130},{3,131},{4,132},{5,133},{6,134},{7,135},{8... | collective-permute-start | bytes 786440 | tf_op jit(solution)/shard_map/ppermute | solution.py:330
  3.1 1.3 %collective-permute-start = (bf16[4,2,128,128]{3,2,1,0:T(8,128)(2,1)S(1)}, bf16[4,2,128,128]{3,2,1,0:T(8,128)(2,1)S(1)}, u32[]{:S(2)}, u32[]{:S(2)}) collective-permute-start(bf16[4,2,128,128]{3,2,1,0:T(8,128)(2,1)S(1)} %get-tuple-element.19), channel_id=1, source_target_pairs={{0,128},{1,129},{2,130},{3,131},{4,132},{5,133},{6,134},{7,135},{8... | collective-permute-start | bytes 786440 | tf_op jit(solution)/shard_map/ppermute | solution.py:330
  4.4 0.0 copy-start.7
  4.4 0.1 stack.31.flags_ref
  4.5 0.0 copy-done
  4.5 0.0 copy-done.5
  4.5 0.0 copy-done.3
  4.5 0.6 %copy-done.7 = f32[2,16,16]{2,1,0:T(8,128)S(1)} copy-done((f32[2,16,16]{2,1,0:T(8,128)S(1)}, f32[2,16,16]{2,1,0:T(8,128)}, u32[]{:S(2)}) %copy-start.7) | copy-done | bytes 2072
  5.1 1.1 %copy-done.8 = bf16[6,256,256]{2,1,0:T(8,128)(2,1)S(1)} copy-done((bf16[6,256,256]{2,1,0:T(8,128)(2,1)S(1)}, bf16[6,256,256]{2,1,0:T(8,128)(2,1)}, u32[]{:S(2)}) %copy-start.8) | copy-done | bytes 786456
  6.2 3.1 %shard_map.104 = (f32[2,4,128,256]{3,2,1,0:T(8,128)S(1)}, f32[8,128]{1,0:T(8,128)S(1)}, f32[64,128]{1,0:T(8,128)S(1)}) custom-call(s32[5]{0:T(128)S(1)} %stack.31.flags_ref, bf16[2,4,4,128,128]{4,3,2,1,0:T(8,128)(2,1)S(1)} %copy-done, f32[2,2,16,16]{3,2,1,0:T(8,128)S(1)} %copy-done.3, f32[2,16,16]{2,1,0:T(8,128)S(1)} %copy-done.7, ...), custom_call_target="tpu_custom_call" | custom-call | flops 5000000000 | bytes 4000000 | tf_op jit(solution)/shard_map/pallas_call | solution.py:291
  9.3 0.0 copy-start.2
  9.3 0.1 slice_bitcast_fusion
  9.4 1.4 %collective-permute-done.1.recv_ref = bf16[4,2,128,128]{3,2,1,0:T(8,128)(2,1)S(1)} collective-permute-done((bf16[4,2,128,128]{3,2,1,0:T(8,128)(2,1)S(1)}, bf16[4,2,128,128]{3,2,1,0:T(8,128)(2,1)S(1)}, u32[]{:S(2)}, u32[]{:S(2)}) %collective-permute-start.1) | collective-permute-done | bytes 262176 | tf_op jit(solution)/shard_map/ppermute | solution.py:330
  10.8 1.8 %shard_map.105.before_ref = f32[72,128]{1,0:T(8,128)S(1)} custom-call(s32[5]{0:T(128)S(1)} %stack.31.flags_ref, bf16[4,4,128,128]{3,2,1,0:T(8,128)(2,1)S(1)} %copy-done.2, bf16[4,2,128,128]{3,2,1,0:T(8,128)(2,1)S(1)} %collective-permute-done.1.recv_ref, f32[4,128,256]{2,1,0:T(8,128)S(1)} %get-tuple-element.16.spec_ref, ...), custom_call_target="tpu_custom_call" | custom-call | flops 2000000000 | bytes 2000000 | tf_op jit(solution)/shard_map/pallas_call | solution.py:291
  12.7 5.4 %collective-permute-start.2 = (f32[72,128]{1,0:T(8,128)S(1)}, f32[72,128]{1,0:T(8,128)S(1)}, u32[]{:S(2)}, u32[]{:S(2)}) collective-permute-start(f32[72,128]{1,0:T(8,128)S(1)} %shard_map.105.before_ref), channel_id=1, source_target_pairs={{0,0},{1,2},{2,1},{3,4},{4,3},{5,6},{6,5},{7,8},{8,7},{9,10},{10,9... | collective-permute-start | bytes 110600 | tf_op jit(solution)/shard_map/ppermute | solution.py:345
  18.1 0.0 collective-permute-done.recv_ref
  18.1 2.5 %shard_map.106 = (f32[72,128]{1,0:T(8,128)S(1)}, f32[2,2,4,4]{3,2,1,0:T(4,128)}) custom-call(s32[5]{0:T(128)S(1)} %stack.31.flags_ref, bf16[4,4,128,128]{3,2,1,0:T(8,128)(2,1)S(1)} %copy-done.2, bf16[4,2,128,128]{3,2,1,0:T(8,128)(2,1)S(1)} %collective-permute-done.recv_ref, f32[4,128,256]{2,1,0:T(8,128)S(1)} %get-tuple-element.17.spec_ref, ...), custom_call_target="tpu_custom_call" | custom-call | flops 2000000000 | bytes 2000000 | tf_op jit(solution)/shard_map/pallas_call | solution.py:291
  20.7 0.0 collective-permute-start.3
  20.7 0.3 collective-permute-done.2.far_ref
  21.0 0.6 %shard_map.107.partial_ref = f32[72,128]{1,0:T(8,128)S(1)} custom-call(s32[5]{0:T(128)S(1)} %stack.31.flags_ref, f32[64,128]{1,0:T(8,128)S(1)} %get-tuple-element.11.static_ref, f32[72,128]{1,0:T(8,128)S(1)} %collective-permute-done.2.far_ref), custom_call_target="tpu_custom_call" | custom-call | flops 5000000000 | bytes 2000000 | tf_op jit(solution)/shard_map/pallas_call | solution.py:291
  21.6 0.0 copy-start.1
  21.6 3.3 %collective-permute-done.3.near_ref = f32[72,128]{1,0:T(8,128)S(1)} collective-permute-done((f32[72,128]{1,0:T(8,128)S(1)}, f32[72,128]{1,0:T(8,128)S(1)}, u32[]{:S(2)}, u32[]{:S(2)}) %collective-permute-start.3) | collective-permute-done | bytes 36896 | tf_op jit(solution)/shard_map/ppermute | solution.py:352
  25.0 0.6 %shard_map.108 = (f32[40,128]{1,0:T(8,128)S(1)}, f32[40,128]{1,0:T(8,128)S(1)}) custom-call(s32[5]{0:T(128)S(1)} %stack.31.flags_ref, f32[72,128]{1,0:T(8,128)S(1)} %get-tuple-element.13.own_ref, f32[72,128]{1,0:T(8,128)S(1)} %shard_map.107.partial_ref, f32[72,128]{1,0:T(8,128)S(1)} %collective-permute-done.3.near_ref), custom_call_target="tpu_custom_call" | custom-call | tf_op jit(solution)/shard_map/pallas_call | solution.py:291
  25.6 4.2 %collective-permute-start.4 = (f32[40,128]{1,0:T(8,128)S(1)}, f32[40,128]{1,0:T(8,128)S(1)}, u32[]{:S(2)}, u32[]{:S(2)}) collective-permute-start(f32[40,128]{1,0:T(8,128)S(1)} %get-tuple-element.14.to_near_ref), channel_id=1, source_target_pairs={{0,16},{16,0},{32,48},{48,32},{64,80},{80,64},{96,112},{112,96},{1... | collective-permute-start | bytes 61448 | tf_op jit(solution)/shard_map/ppermute | solution.py:354
  29.8 2.7 %collective-permute-start.5 = (f32[40,128]{1,0:T(8,128)S(1)}, f32[40,128]{1,0:T(8,128)S(1)}, u32[]{:S(2)}, u32[]{:S(2)}) collective-permute-start(f32[40,128]{1,0:T(8,128)S(1)} %get-tuple-element.15.to_far_ref), channel_id=1, source_target_pairs={{0,0},{16,32},{32,16},{48,64},{64,48},{80,96},{96,80},{112,112},{1... | collective-permute-start | bytes 61448 | tf_op jit(solution)/shard_map/ppermute | solution.py:355
  32.6 0.0 collective-permute-done.4.near_ref
  32.6 2.3 %collective-permute-done.5.far_ref = f32[40,128]{1,0:T(8,128)S(1)} collective-permute-done((f32[40,128]{1,0:T(8,128)S(1)}, f32[40,128]{1,0:T(8,128)S(1)}, u32[]{:S(2)}, u32[]{:S(2)}) %collective-permute-start.5) | collective-permute-done | bytes 20512 | tf_op jit(solution)/shard_map/ppermute | solution.py:355
  34.9 1.6 %shard_map.109 = f32[2,2,16,16]{3,2,1,0:T(8,128)} custom-call(s32[5]{0:T(128)S(1)} %stack.31.flags_ref, f32[40,128]{1,0:T(8,128)S(1)} %get-tuple-element.14.to_near_ref, f32[40,128]{1,0:T(8,128)S(1)} %get-tuple-element.15.to_far_ref, f32[40,128]{1,0:T(8,128)S(1)} %collective-permute-done.4.near_ref, f32[40,128]{1,0:T(8,128)S(1)} %collective-permute-done.5.far_ref, ...), custom_call_target="tpu_custom_call" | custom-call | tf_op jit(solution)/shard_map/pallas_call | solution.py:291
  (9 shorter events, 0.1 us)
Async XLA Ops:
  0.6 1.0 %slice-start = ((bf16[2,4,4,128,128]{4,3,2,1,0:T(8,128)(2,1)}), bf16[1,4,4,128,128]{4,3,2,1,0:T(8,128)(2,1)S(1)}, s32[]{:S(2)}) async-start(bf16[2,4,4,128,128]{4,3,2,1,0:T(8,128)(2,1)} %patches_ref.1), calls=%async_computation | async-start | bytes 1048576 | tf_op jit(solution)/shard_map/slice | solution.py:329
  0.7 3.8 %copy-start = (bf16[2,4,4,128,128]{4,3,2,1,0:T(8,128)(2,1)S(1)}, bf16[2,4,4,128,128]{4,3,2,1,0:T(8,128)(2,1)}, u32[]{:S(2)}) copy-start(bf16[2,4,4,128,128]{4,3,2,1,0:T(8,128)(2,1)} %patches_ref.1) | copy-start | bytes 3145732
  1.7 2.8 %copy-start.4 = (s32[4,16,16]{2,1,0:T(8,128)S(1)}, s32[4,16,16]{2,1,0:T(8,128)}, u32[]{:S(2)}) copy-start(s32[4,16,16]{2,1,0:T(8,128)} %edges_ref.1) | copy-start | bytes 12292
  1.7 2.8 %copy-start.5 = (s32[4,16,16]{2,1,0:T(8,128)S(1)}, s32[4,16,16]{2,1,0:T(8,128)}, u32[]{:S(2)}) copy-start(s32[4,16,16]{2,1,0:T(8,128)} %nodes_ref.1) | copy-start | bytes 12292
  1.7 2.8 %copy-start.6 = (f32[4,16,16]{2,1,0:T(8,128)S(1)}, f32[4,16,16]{2,1,0:T(8,128)}, u32[]{:S(2)}) copy-start(f32[4,16,16]{2,1,0:T(8,128)} %share_ref.1) | copy-start | bytes 12292
  1.7 2.8 %copy-start.3 = (f32[2,2,16,16]{3,2,1,0:T(8,128)S(1)}, f32[2,2,16,16]{3,2,1,0:T(8,128)}, u32[]{:S(2)}) copy-start(f32[2,2,16,16]{3,2,1,0:T(8,128)} %start_ref.1) | copy-start | bytes 12292
  1.8 9.1 %collective-permute-start.1 = (bf16[4,2,128,128]{3,2,1,0:T(8,128)(2,1)S(1)}, bf16[4,2,128,128]{3,2,1,0:T(8,128)(2,1)S(1)}, u32[]{:S(2)}, u32[]{:S(2)}) collective-permute-start(bf16[4,2,128,128]{3,2,1,0:T(8,128)(2,1)S(1)} %get-tuple-element.18), channel_id=1, source_target_pairs={{0,128},{1,129},{2,130},{3,131},{4,132},{5,133},{6,134},{7,135},{8... | collective-permute-start | bytes 786440 | tf_op jit(solution)/shard_map/ppermute | solution.py:330
  3.1 15.1 %collective-permute-start = (bf16[4,2,128,128]{3,2,1,0:T(8,128)(2,1)S(1)}, bf16[4,2,128,128]{3,2,1,0:T(8,128)(2,1)S(1)}, u32[]{:S(2)}, u32[]{:S(2)}) collective-permute-start(bf16[4,2,128,128]{3,2,1,0:T(8,128)(2,1)S(1)} %get-tuple-element.19), channel_id=1, source_target_pairs={{0,128},{1,129},{2,130},{3,131},{4,132},{5,133},{6,134},{7,135},{8... | collective-permute-start | bytes 786440 | tf_op jit(solution)/shard_map/ppermute | solution.py:330
  4.4 0.7 %copy-start.7 = (f32[2,16,16]{2,1,0:T(8,128)S(1)}, f32[2,16,16]{2,1,0:T(8,128)}, u32[]{:S(2)}) copy-start(f32[2,16,16]{2,1,0:T(8,128)} %weight_ref.1) | copy-start | bytes 6148
  5.1 1.1 %copy-start.8 = (bf16[6,256,256]{2,1,0:T(8,128)(2,1)S(1)}, bf16[6,256,256]{2,1,0:T(8,128)(2,1)}, u32[]{:S(2)}) copy-start(bf16[6,256,256]{2,1,0:T(8,128)(2,1)} %constant.45.clone.table_ref) | copy-start | bytes 2359300
  9.3 1.5 %copy-start.2 = (bf16[4,4,128,128]{3,2,1,0:T(8,128)(2,1)S(1)}, bf16[4,4,128,128]{3,2,1,0:T(8,128)(2,1)}, u32[]{:S(2)}) copy-start(bf16[4,4,128,128]{3,2,1,0:T(8,128)(2,1)} %prior_ref.3) | copy-start | bytes 1572868
  12.7 8.3 %collective-permute-start.2 = (f32[72,128]{1,0:T(8,128)S(1)}, f32[72,128]{1,0:T(8,128)S(1)}, u32[]{:S(2)}, u32[]{:S(2)}) collective-permute-start(f32[72,128]{1,0:T(8,128)S(1)} %shard_map.105.before_ref), channel_id=1, source_target_pairs={{0,0},{1,2},{2,1},{3,4},{4,3},{5,6},{6,5},{7,8},{8,7},{9,10},{10,9... | collective-permute-start | bytes 110600 | tf_op jit(solution)/shard_map/ppermute | solution.py:345
  20.7 4.3 %collective-permute-start.3 = (f32[72,128]{1,0:T(8,128)S(1)}, f32[72,128]{1,0:T(8,128)S(1)}, u32[]{:S(2)}, u32[]{:S(2)}) collective-permute-start(f32[72,128]{1,0:T(8,128)S(1)} %get-tuple-element.13.own_ref), channel_id=1, source_target_pairs={{0,1},{1,0},{2,3},{3,2},{4,5},{5,4},{6,7},{7,6},{8,9},{9,8},{10,11... | collective-permute-start | bytes 110600 | tf_op jit(solution)/shard_map/ppermute | solution.py:352
  21.6 13.3 %copy-start.1 = (bf16[96,384]{1,0:T(8,128)(2,1)S(1)}, bf16[96,384]{1,0:T(8,128)(2,1)}, u32[]{:S(2)}) copy-start(bf16[96,384]{1,0:T(8,128)(2,1)} %constant.46.clone.spread_ref) | copy-start | bytes 221188
  25.6 6.9 %collective-permute-start.4 = (f32[40,128]{1,0:T(8,128)S(1)}, f32[40,128]{1,0:T(8,128)S(1)}, u32[]{:S(2)}, u32[]{:S(2)}) collective-permute-start(f32[40,128]{1,0:T(8,128)S(1)} %get-tuple-element.14.to_near_ref), channel_id=1, source_target_pairs={{0,16},{16,0},{32,48},{48,32},{64,80},{80,64},{96,112},{112,96},{1... | collective-permute-start | bytes 61448 | tf_op jit(solution)/shard_map/ppermute | solution.py:354
  29.8 5.1 %collective-permute-start.5 = (f32[40,128]{1,0:T(8,128)S(1)}, f32[40,128]{1,0:T(8,128)S(1)}, u32[]{:S(2)}, u32[]{:S(2)}) collective-permute-start(f32[40,128]{1,0:T(8,128)S(1)} %get-tuple-element.15.to_far_ref), channel_id=1, source_target_pairs={{0,0},{16,32},{32,16},{48,64},{64,48},{80,96},{96,80},{112,112},{1... | collective-permute-start | bytes 61448 | tf_op jit(solution)/shard_map/ppermute | solution.py:355

commit v2 on v1

--- a/solution.py
+++ b/solution.py
@@ -129,42 +129,50 @@
     return flows
 
 
-def local_kernel(flags_ref, patches_ref, start_ref, weight_ref, edges_ref, nodes_ref, share_ref,
-                 table_ref, spec_ref, flows_ref, static_ref, current, sums_y, sums_x):
+def local_kernel(flags_ref, patches_ref, table_ref, spec0_ref, spec1_ref, flows_ref, later_ref, current, sums_y, sums_x):
     odd = flags_ref[1]
     forward = [table_ref[i] for i in range(3)]
     inverse = [table_ref[i] for i in range(3, 6)]
-    static_ref[...] = jnp.zeros_like(static_ref)
+    for py in range(4):
+        for j in range(2):
+            later_ref[py, j] = patches_ref[1, py, 2 * (1 ^ odd) + j]
+    previous = [ref.at[py] for ref in (spec0_ref, spec1_ref) for py in range(4)]
+    for unit in range(8):
+        first = 2 * ((unit // 4) ^ odd)
+        for section, result in ((0, previous[unit]), (1, current.at[unit])):
+            pixels = jnp.concatenate([patches_ref[section, unit % 4, first], patches_ref[section, unit % 4, first + 1]], axis=1)
+            result[...] = spectrum(pixels, *forward)
+    for unit in range(8):
+        along_y, power = moments(previous[unit][...], current[unit], *inverse)
+        sums_y[unit] = along_y
+        sums_x[unit] = power
+
+    flows = jnp.zeros((8, N), F32)
+    for half in range(2):
+        flows += placed_flows([sums_y[half * 4 + i] for i in range(4)], [sums_x[half * 4 + i] for i in range(4)], 1, 2 * (half ^ odd))
+    flows_ref[...] = flows
+
+
+def pack_nodes(out_ref, start_ref, weight_ref, edges_ref, nodes_ref, share_ref):
+    out_ref[8:, :] = jnp.zeros((64, N), F32)
     fields = [start_ref[s, c] for s in range(2) for c in range(2)]
     fields += [weight_ref[0], weight_ref[1], edges_ref[0].astype(F32), edges_ref[2].astype(F32)]
     fields += [nodes_ref[k].astype(F32) for k in range(4)] + [share_ref[k] for k in range(4)]
     for at, field in enumerate(fields):
-        row, lane = at // 4 * 16, at % 4 * GROUP + EDGE
-        static_ref[row : row + 16, lane : lane + 16] = field
-
-    for unit in range(8):
-        half, py = unit // 4, unit % 4
-        first = 2 * (half ^ odd)
-        for section, result in ((0, spec_ref.at[half, py]), (1, current.at[unit])):
-            pixels = jnp.concatenate([patches_ref[section, py, first], patches_ref[section, py, first + 1]], axis=1)
-            result[...] = spectrum(pixels, *forward)
-    for unit in range(8):
-        along_y, power = moments(spec_ref[unit // 4, unit % 4], current[unit], *inverse)
-        sums_y[unit] = along_y
-        sums_x[unit] = power
-
-    flows = jnp.zeros((8, N), F32)
-    for half in range(2):
-        flows += placed_flows([sums_y[half * 4 + i] for i in range(4)], [sums_x[half * 4 + i] for i in range(4)], 1, 2 * (half ^ odd))
-    flows_ref[...] = flows
-
-
-def chained_kernel(half, flags_ref, prior_ref, recv_ref, spec_ref, before_ref, static_ref, table_ref, out_ref, *rest):
-    *field_ref, previous = rest
+        row, lane = 8 + at // 4 * 16, at % 4 * GROUP + EDGE
+        out_ref[row : row + 16, lane : lane + 16] = field
+
+
+def chained_kernel(half, flags_ref, prior_ref, recv_ref, spec_ref, before_ref, table_ref, *rest):
+    *node_refs, out_ref, previous = rest
     at_start, odd = flags_ref[0] == 0, flags_ref[1]
     forward = [table_ref[i] for i in range(3)]
     inverse = [table_ref[i] for i in range(3, 6)]
     first = 2 * (half ^ odd)
+    if half == 0:
+        pack_nodes(out_ref, *node_refs)
+    else:
+        out_ref[8:, :] = before_ref[8:, :]
     for py in range(4):
         own = jnp.concatenate([prior_ref[py, first], prior_ref[py, first + 1]], axis=1)
         other = jnp.concatenate([recv_ref[py, 0], recv_ref[py, 1]], axis=1)
@@ -172,12 +180,6 @@
     sums = [moments(previous[py], spec_ref[py], *inverse) for py in range(4)]
     flows = before_ref[0:8, :] + placed_flows([s[0] for s in sums], [s[1] for s in sums], 0, first)
     out_ref[0:8, :] = flows
-    out_ref[8:, :] = static_ref[...]
-    if field_ref:
-        for s in range(2):
-            for c in range(2):
-                lane = s * 16 + c * 8 + 2
-                field_ref[0][s, c] = flows[2:6, lane : lane + 4]
 
 
 def beside(base, values, on_right):
@@ -191,16 +193,19 @@
     return flows, jnp.where(on_right, right, left)
 
 
-def far_columns_kernel(flags_ref, static_ref, far_ref, out_ref):
-    base = jnp.concatenate([jnp.zeros((8, N), F32), static_ref[...]], axis=0)
+def far_columns_kernel(flags_ref, far_ref, own_ref, out_ref, field_ref):
+    base = own_ref[...]
     flows, nodes = beside(base, far_ref[...] * flags_ref[2].astype(F32), flags_ref[1] == 1)
     out_ref[0:8, :] = flows
     out_ref[8:, :] = nodes
-
-
-def near_columns_kernel(flags_ref, own_ref, partial_ref, near_ref, to_near_ref, to_far_ref):
-    base = jnp.concatenate([partial_ref[0:8, :] + own_ref[0:8, :], partial_ref[8:, :]], axis=0)
-    flows, nodes = beside(base, near_ref[...], flags_ref[1] == 0)
+    for s in range(2):
+        for c in range(2):
+            lane = s * 16 + c * 8 + 2
+            field_ref[s, c] = own_ref[2:6, lane : lane + 4]
+
+
+def near_columns_kernel(flags_ref, partial_ref, near_ref, to_near_ref, to_far_ref):
+    flows, nodes = beside(partial_ref[...], near_ref[...], flags_ref[1] == 0)
     top = jnp.concatenate([flows] + [nodes[16 * f : 16 * f + 8] for f in range(4)], axis=0)
     bottom = jnp.concatenate([flows] + [nodes[16 * f + 8 : 16 * f + 16] for f in range(4)], axis=0)
     odd = flags_ref[3] == 1
@@ -288,10 +293,11 @@
 
 
 def call(kernel, inputs, out_shapes, scratch=(), flops=0, moved=0):
+    memory = [pltpu.SMEM] + [pltpu.VMEM] * (len(inputs) - 1)
     return pl.pallas_call(
         kernel,
         out_shape=out_shapes,
-        in_specs=[pl.BlockSpec(memory_space=pltpu.SMEM)] + [pl.BlockSpec(memory_space=pltpu.VMEM)] * (len(inputs) - 1),
+        in_specs=[pl.BlockSpec(memory_space=m) for m in memory],
         out_specs=jax.tree.map(lambda _: pl.BlockSpec(memory_space=pltpu.VMEM), out_shapes),
         scratch_shapes=scratch,
         compiler_params=pltpu.CompilerParams(vmem_limit_bytes=VMEM_LIMIT),
@@ -322,35 +328,36 @@
     has_far = (gx > 0) & (gx < cols - 1)
     has_far_row = (gy > 0) & (gy < rows - 1)
     flags = jnp.stack([gz, odd, has_far, odd_row, has_far_row]).astype(jnp.int32)
+
+    def to_next_section(values):
+        return lax.ppermute(values, "gz", [(0, 1)])
+
+    early = to_next_section(lax.dynamic_slice_in_dim(patches[1], 2 * odd, 2, axis=1))
     table = jnp.asarray(tables())
-
-    arriving = []
-    for half in range(2):
-        chunk = lax.dynamic_slice_in_dim(patches[1], 2 * (half ^ odd), 2, axis=1)
-        arriving.append(lax.ppermute(chunk, "gz", [(0, 1)]))
-
-    spec, flows, static = call(
+    half_spec = f32(4, N, 2 * N)
+    spec0, spec1, flows, later = call(
         local_kernel,
-        [flags, patches, start_offset, flow_weight, edges, node_patch, node_weight, table],
-        [f32(2, 4, N, 2 * N), f32(8, N), f32(64, N)],
-        scratch=[pltpu.VMEM((8, N, 2 * N), F32), pltpu.VMEM((8, 1, N), F32), pltpu.VMEM((8, 1, 2 * N), F32)],
+        [flags, patches, table],
+        [half_spec, half_spec, f32(8, N), jax.ShapeDtypeStruct((4, 2, N, N), BF16)],
+        [pltpu.VMEM((8, N, 2 * N), F32), pltpu.VMEM((8, 1, N), F32), pltpu.VMEM((8, 1, 2 * N), F32)],
         flops=5_000_000_000, moved=4_000_000,
     )
+    late = to_next_section(later)
     scratch = [pltpu.VMEM((4, N, 2 * N), F32)]
     (first,) = call(
         functools.partial(chained_kernel, 0),
-        [flags, prior_patches, arriving[0], spec[0], flows, static, table],
+        [flags, prior_patches, early, spec0, flows, table, start_offset, flow_weight, edges, node_patch, node_weight],
         [f32(72, N)], scratch, flops=2_000_000_000, moved=2_000_000,
     )
     from_far = lax.ppermute(first, "gx", far_partner(cols))
-    partial = call(far_columns_kernel, [flags, static, from_far], f32(72, N), flops=5_000_000_000, moved=2_000_000)
-    own, flow_field = call(
-        functools.partial(chained_kernel, 1),
-        [flags, prior_patches, arriving[1], spec[1], first, static, table],
-        [f32(72, N), f32(2, 2, 4, 4)], scratch, flops=2_000_000_000, moved=2_000_000,
+    (own,) = call(
+        functools.partial(chained_kernel, 1), [flags, prior_patches, late, spec1, first, table],
+        [f32(72, N)], scratch, flops=2_000_000_000, moved=2_000_000,
     )
+    partial, flow_field = call(
+        far_columns_kernel, [flags, from_far, own], [f32(72, N), f32(2, 2, 4, 4)], flops=5_000_000_000, moved=2_000_000)
     from_near = lax.ppermute(own, "gx", near_partner(cols))
-    to_near, to_far = call(near_columns_kernel, [flags, own, partial, from_near], [f32(40, N), f32(40, N)])
+    to_near, to_far = call(near_columns_kernel, [flags, partial, from_near], [f32(40, N), f32(40, N)])
     row_near = lax.ppermute(to_near, "gy", near_partner(rows))
     row_far = lax.ppermute(to_far, "gy", far_partner(rows))
     displacement = call(

time: 36.9 us -> 35 us (0.949)
  starting transfers between devices: 14.9 us -> 13.9 us
  local copies, waits for them, and re-layouts: 2.97 us -> 2.3 us
    ppermute x1, waiting for transfers between devices: 3.33 us -> 2.15 us  [body(): from_near = lax.ppermute(own, 'gx', near_partner(cols))]
    ppermute x1, starting transfers between devices: 4.21 us -> 3.06 us  [body(): row_near = lax.ppermute(to_near, 'gy', near_partner(rows))]
    ppermute x2, waiting for transfers between devices: 1.4 us -> 2.07 us  [to_next_section(): return lax.ppermute(values, 'gz', [(0, 1)])]
    ppermute x1, waiting for transfers between devices: 0.33 us -> 0.92 us  [body(): from_far = lax.ppermute(first, 'gx', far_partner(cols))]
    unnamed x18, local copies, waits for them, and re-layouts: 1.76 us -> 1.17 us
  transfers between devices with their start and end apart: 6 -> 6, of which waited for: 4 -> 4; matrix products, arithmetic and copies ran while one was open for 0% -> 0% of each run, Pallas kernels for 22% -> 23%
where the time goes in v2:
time: 35 us; the launch traced here: 34.8 us
  starting transfers between devices  13.9 us (40%)
  Pallas kernels  10.3 us (29%)
  waiting for transfers between devices  7.49 us (21%)
  local copies, waits for them, and re-layouts  2.3 us (7%)
  between operations  0.83 us (2%)
    pallas_call x6, Pallas kernels, call(): pl.pallas_call(kernel, out_shape=out_shapes, in_specs=[pl.BlockSpec(memor...  10.3 us
    ppermute x1, starting transfers between devices, body(): from_far = lax.ppermute(first, 'gx', far_partner(cols))  5.43 us
    ppermute x1, starting transfers between devices, body(): row_near = lax.ppermute(to_near, 'gy', near_partner(rows))  3.06 us
    ppermute x1, starting transfers between devices, body(): row_far = lax.ppermute(to_far, 'gy', far_partner(rows))  2.72 us
    ppermute x2, starting transfers between devices, to_next_section(): return lax.ppermute(values, 'gz', [(0, 1)])  2.58 us
    ppermute x1, waiting for transfers between devices, body(): row_far = lax.ppermute(to_far, 'gy', far_partner(rows))  2.35 us
    ppermute x1, waiting for transfers between devices, body(): from_near = lax.ppermute(own, 'gx', near_partner(cols))  2.15 us
    ppermute x2, waiting for transfers between devices, to_next_section(): return lax.ppermute(values, 'gz', [(0, 1)])  2.07 us
  transfers between devices with their start and end apart: 6, of which 4 were waited for; matrix products, arithmetic and copies ran while one was open for 0% of the time, Pallas kernels for 23%

profile of v2, /device:TPU:125, one launch (start us, length us, event | category | flops | bytes accessed | tf_op | source)
XLA Modules:
  0.0 34.8 jit_solution(13617205898922096143)
XLA Ops:
  0.6 0.0 slice-start
  0.7 0.0 copy-start
  0.7 1.0 %slice-done = bf16[1,4,4,128,128]{4,3,2,1,0:T(8,128)(2,1)S(1)} async-done(((bf16[2,4,4,128,128]{4,3,2,1,0:T(8,128)(2,1)}), bf16[1,4,4,128,128]{4,3,2,1,0:T(8,128)(2,1)S(1)}, s32[]{:S(2)}) %slice-start) | async-done | bytes 524312 | tf_op jit(solution)/shard_map/slice | solution.py:335
  1.7 1.3 %collective-permute-start = (bf16[4,2,128,128]{3,2,1,0:T(8,128)(2,1)S(1)}, bf16[4,2,128,128]{3,2,1,0:T(8,128)(2,1)S(1)}, u32[]{:S(2)}, u32[]{:S(2)}) collective-permute-start(bf16[4,2,128,128]{3,2,1,0:T(8,128)(2,1)S(1)} %dynamic-slice_bitcast_fusion), channel_id=1, source_target_pairs={{0,128},{1,129},{2,130},{3,131},{4,132},{5,133},{6,134},{7,135},{8... | collective-permute-start | bytes 786440 | tf_op jit(solution)/shard_map/ppermute | solution.py:333
  3.0 0.1 stack.31.flags_ref
  3.1 0.0 copy-done
  3.1 1.1 %copy-done.8 = bf16[6,256,256]{2,1,0:T(8,128)(2,1)S(1)} copy-done((bf16[6,256,256]{2,1,0:T(8,128)(2,1)S(1)}, bf16[6,256,256]{2,1,0:T(8,128)(2,1)}, u32[]{:S(2)}) %copy-start.8) | copy-done | bytes 786456
  4.3 0.0 copy-start.6
  4.3 0.0 copy-start.7
  4.3 3.1 %shard_map.104 = (f32[4,128,256]{2,1,0:T(8,128)S(1)}, f32[4,128,256]{2,1,0:T(8,128)S(1)}, f32[8,128]{1,0:T(8,128)S(1)}, bf16[4,2,128,128]{3,2,1,0:T(8,128)(2,1)S(1)}) custom-call(s32[5]{0:T(128)S(1)} %stack.31.flags_ref, bf16[2,4,4,128,128]{4,3,2,1,0:T(8,128)(2,1)S(1)} %copy-done, bf16[6,256,256]{2,1,0:T(8,128)(2,1)S(1)} %copy-done.8), custom_call_target="tpu_custom_call" | custom-call | flops 5000000000 | bytes 4000000 | tf_op jit(solution)/shard_map/pallas_call | solution.py:297
  7.4 1.3 %collective-permute-start.2 = (bf16[4,2,128,128]{3,2,1,0:T(8,128)(2,1)S(1)}, bf16[4,2,128,128]{3,2,1,0:T(8,128)(2,1)S(1)}, u32[]{:S(2)}, u32[]{:S(2)}) collective-permute-start(bf16[4,2,128,128]{3,2,1,0:T(8,128)(2,1)S(1)} %get-tuple-element.12), channel_id=1, source_target_pairs={{0,128},{1,129},{2,130},{3,131},{4,132},{5,133},{6,134},{7,135},{8... | collective-permute-start | bytes 786440 | tf_op jit(solution)/shard_map/ppermute | solution.py:333
  8.7 2.1 %collective-permute-done.recv_ref = bf16[4,2,128,128]{3,2,1,0:T(8,128)(2,1)S(1)} collective-permute-done((bf16[4,2,128,128]{3,2,1,0:T(8,128)(2,1)S(1)}, bf16[4,2,128,128]{3,2,1,0:T(8,128)(2,1)S(1)}, u32[]{:S(2)}, u32[]{:S(2)}) %collective-permute-start) | collective-permute-done | bytes 262176 | tf_op jit(solution)/shard_map/ppermute | solution.py:333
  10.8 0.0 copy-done.2
  10.8 0.0 copy-done.3
  10.8 0.0 copy-done.4
  10.8 0.0 copy-done.5
  10.8 0.0 copy-done.6
  10.8 0.0 copy-done.7
  10.8 1.8 %shard_map.105.before_ref = f32[72,128]{1,0:T(8,128)S(1)} custom-call(s32[5]{0:T(128)S(1)} %stack.31.flags_ref, bf16[4,4,128,128]{3,2,1,0:T(8,128)(2,1)S(1)} %copy-done.2, bf16[4,2,128,128]{3,2,1,0:T(8,128)(2,1)S(1)} %collective-permute-done.recv_ref, f32[4,128,256]{2,1,0:T(8,128)S(1)} %get-tuple-element.10.spec_ref, ...), custom_call_target="tpu_custom_call" | custom-call | flops 2000000000 | bytes 2000000 | tf_op jit(solution)/shard_map/pallas_call | solution.py:297
  12.7 5.4 %collective-permute-start.1 = (f32[72,128]{1,0:T(8,128)S(1)}, f32[72,128]{1,0:T(8,128)S(1)}, u32[]{:S(2)}, u32[]{:S(2)}) collective-permute-start(f32[72,128]{1,0:T(8,128)S(1)} %shard_map.105.before_ref), channel_id=1, source_target_pairs={{0,0},{1,2},{2,1},{3,4},{4,3},{5,6},{6,5},{7,8},{8,7},{9,10},{10,9... | collective-permute-start | bytes 110600 | tf_op jit(solution)/shard_map/ppermute | solution.py:352
  18.1 0.0 collective-permute-done.2.recv_ref
  18.1 1.8 %shard_map.106.own_ref = f32[72,128]{1,0:T(8,128)S(1)} custom-call(s32[5]{0:T(128)S(1)} %stack.31.flags_ref, bf16[4,4,128,128]{3,2,1,0:T(8,128)(2,1)S(1)} %copy-done.2, bf16[4,2,128,128]{3,2,1,0:T(8,128)(2,1)S(1)} %collective-permute-done.2.recv_ref, f32[4,128,256]{2,1,0:T(8,128)S(1)} %get-tuple-element.13.spec_ref, f32[72,128]{1,0:T(8,128)S(1)} %shard_map.105.before_ref, ...), custom_call_target="tpu_custom_call" | custom-call | flops 2000000000 | bytes 2000000 | tf_op jit(solution)/shard_map/pallas_call | solution.py:297
  20.0 0.1 collective-permute-start.3
  20.1 0.9 %collective-permute-done.1.far_ref = f32[72,128]{1,0:T(8,128)S(1)} collective-permute-done((f32[72,128]{1,0:T(8,128)S(1)}, f32[72,128]{1,0:T(8,128)S(1)}, u32[]{:S(2)}, u32[]{:S(2)}) %collective-permute-start.1) | collective-permute-done | bytes 36896 | tf_op jit(solution)/shard_map/ppermute | solution.py:352
  21.0 1.2 %shard_map.107 = (f32[72,128]{1,0:T(8,128)S(1)}, f32[2,2,4,4]{3,2,1,0:T(4,128)}) custom-call(s32[5]{0:T(128)S(1)} %stack.31.flags_ref, f32[72,128]{1,0:T(8,128)S(1)} %collective-permute-done.1.far_ref, f32[72,128]{1,0:T(8,128)S(1)} %shard_map.106.own_ref), custom_call_target="tpu_custom_call" | custom-call | flops 5000000000 | bytes 2000000 | tf_op jit(solution)/shard_map/pallas_call | solution.py:297
  22.2 2.1 %collective-permute-done.3.near_ref = f32[72,128]{1,0:T(8,128)S(1)} collective-permute-done((f32[72,128]{1,0:T(8,128)S(1)}, f32[72,128]{1,0:T(8,128)S(1)}, u32[]{:S(2)}, u32[]{:S(2)}) %collective-permute-start.3) | collective-permute-done | bytes 36896 | tf_op jit(solution)/shard_map/ppermute | solution.py:359
  24.4 0.6 %shard_map.108 = (f32[40,128]{1,0:T(8,128)S(1)}, f32[40,128]{1,0:T(8,128)S(1)}) custom-call(s32[5]{0:T(128)S(1)} %stack.31.flags_ref, f32[72,128]{1,0:T(8,128)S(1)} %get-tuple-element.15.partial_ref, f32[72,128]{1,0:T(8,128)S(1)} %collective-permute-done.3.near_ref), custom_call_target="tpu_custom_call" | custom-call | tf_op jit(solution)/shard_map/pallas_call | solution.py:297
  25.0 3.1 %collective-permute-start.4 = (f32[40,128]{1,0:T(8,128)S(1)}, f32[40,128]{1,0:T(8,128)S(1)}, u32[]{:S(2)}, u32[]{:S(2)}) collective-permute-start(f32[40,128]{1,0:T(8,128)S(1)} %get-tuple-element.16.to_near_ref), channel_id=1, source_target_pairs={{0,16},{16,0},{32,48},{48,32},{64,80},{80,64},{96,112},{112,96},{1... | collective-permute-start | bytes 61448 | tf_op jit(solution)/shard_map/ppermute | solution.py:361
  28.1 2.7 %collective-permute-start.5 = (f32[40,128]{1,0:T(8,128)S(1)}, f32[40,128]{1,0:T(8,128)S(1)}, u32[]{:S(2)}, u32[]{:S(2)}) collective-permute-start(f32[40,128]{1,0:T(8,128)S(1)} %get-tuple-element.17.to_far_ref), channel_id=1, source_target_pairs={{0,0},{16,32},{32,16},{48,64},{64,48},{80,96},{96,80},{112,112},{1... | collective-permute-start | bytes 61448 | tf_op jit(solution)/shard_map/ppermute | solution.py:362
  30.8 0.0 collective-permute-done.4.near_ref
  30.8 2.3 %collective-permute-done.5.far_ref = f32[40,128]{1,0:T(8,128)S(1)} collective-permute-done((f32[40,128]{1,0:T(8,128)S(1)}, f32[40,128]{1,0:T(8,128)S(1)}, u32[]{:S(2)}, u32[]{:S(2)}) %collective-permute-start.5) | collective-permute-done | bytes 20512 | tf_op jit(solution)/shard_map/ppermute | solution.py:362
  33.2 1.6 %shard_map.109 = f32[2,2,16,16]{3,2,1,0:T(8,128)} custom-call(s32[5]{0:T(128)S(1)} %stack.31.flags_ref, f32[40,128]{1,0:T(8,128)S(1)} %get-tuple-element.16.to_near_ref, f32[40,128]{1,0:T(8,128)S(1)} %get-tuple-element.17.to_far_ref, f32[40,128]{1,0:T(8,128)S(1)} %collective-permute-done.4.near_ref, f32[40,128]{1,0:T(8,128)S(1)} %collective-permute-done.5.far_ref, ...), custom_call_target="tpu_custom_call" | custom-call | tf_op jit(solution)/shard_map/pallas_call | solution.py:297
  (8 shorter events, 0.0 us)
Async XLA Ops:
  0.6 1.0 %slice-start = ((bf16[2,4,4,128,128]{4,3,2,1,0:T(8,128)(2,1)}), bf16[1,4,4,128,128]{4,3,2,1,0:T(8,128)(2,1)S(1)}, s32[]{:S(2)}) async-start(bf16[2,4,4,128,128]{4,3,2,1,0:T(8,128)(2,1)} %patches_ref.1), calls=%async_computation | async-start | bytes 1048576 | tf_op jit(solution)/shard_map/slice | solution.py:335
  0.7 2.5 %copy-start = (bf16[2,4,4,128,128]{4,3,2,1,0:T(8,128)(2,1)S(1)}, bf16[2,4,4,128,128]{4,3,2,1,0:T(8,128)(2,1)}, u32[]{:S(2)}) copy-start(bf16[2,4,4,128,128]{4,3,2,1,0:T(8,128)(2,1)} %patches_ref.1) | copy-start | bytes 3145732
  1.7 9.1 %collective-permute-start = (bf16[4,2,128,128]{3,2,1,0:T(8,128)(2,1)S(1)}, bf16[4,2,128,128]{3,2,1,0:T(8,128)(2,1)S(1)}, u32[]{:S(2)}, u32[]{:S(2)}) collective-permute-start(bf16[4,2,128,128]{3,2,1,0:T(8,128)(2,1)S(1)} %dynamic-slice_bitcast_fusion), channel_id=1, source_target_pairs={{0,128},{1,129},{2,130},{3,131},{4,132},{5,133},{6,134},{7,135},{8... | collective-permute-start | bytes 786440 | tf_op jit(solution)/shard_map/ppermute | solution.py:333
  3.1 1.1 %copy-start.8 = (bf16[6,256,256]{2,1,0:T(8,128)(2,1)S(1)}, bf16[6,256,256]{2,1,0:T(8,128)(2,1)}, u32[]{:S(2)}) copy-start(bf16[6,256,256]{2,1,0:T(8,128)(2,1)} %constant.43.clone.table_ref) | copy-start | bytes 2359300
  4.3 6.5 %copy-start.2 = (bf16[4,4,128,128]{3,2,1,0:T(8,128)(2,1)S(1)}, bf16[4,4,128,128]{3,2,1,0:T(8,128)(2,1)}, u32[]{:S(2)}) copy-start(bf16[4,4,128,128]{3,2,1,0:T(8,128)(2,1)} %prior_ref.3) | copy-start | bytes 1572868
  4.3 6.5 %copy-start.3 = (f32[2,2,16,16]{3,2,1,0:T(8,128)S(1)}, f32[2,2,16,16]{3,2,1,0:T(8,128)}, u32[]{:S(2)}) copy-start(f32[2,2,16,16]{3,2,1,0:T(8,128)} %rest_0_.1) | copy-start | bytes 12292
  4.3 6.5 %copy-start.4 = (s32[4,16,16]{2,1,0:T(8,128)S(1)}, s32[4,16,16]{2,1,0:T(8,128)}, u32[]{:S(2)}) copy-start(s32[4,16,16]{2,1,0:T(8,128)} %rest_2_.1) | copy-start | bytes 12292
  4.3 6.5 %copy-start.5 = (s32[4,16,16]{2,1,0:T(8,128)S(1)}, s32[4,16,16]{2,1,0:T(8,128)}, u32[]{:S(2)}) copy-start(s32[4,16,16]{2,1,0:T(8,128)} %rest_3_.1) | copy-start | bytes 12292
  4.3 6.5 %copy-start.6 = (f32[4,16,16]{2,1,0:T(8,128)S(1)}, f32[4,16,16]{2,1,0:T(8,128)}, u32[]{:S(2)}) copy-start(f32[4,16,16]{2,1,0:T(8,128)} %rest_4_.1) | copy-start | bytes 12292
  4.3 6.5 %copy-start.7 = (f32[2,16,16]{2,1,0:T(8,128)S(1)}, f32[2,16,16]{2,1,0:T(8,128)}, u32[]{:S(2)}) copy-start(f32[2,16,16]{2,1,0:T(8,128)} %rest_1_.1) | copy-start | bytes 6148
  7.4 10.7 %collective-permute-start.2 = (bf16[4,2,128,128]{3,2,1,0:T(8,128)(2,1)S(1)}, bf16[4,2,128,128]{3,2,1,0:T(8,128)(2,1)S(1)}, u32[]{:S(2)}, u32[]{:S(2)}) collective-permute-start(bf16[4,2,128,128]{3,2,1,0:T(8,128)(2,1)S(1)} %get-tuple-element.12), channel_id=1, source_target_pairs={{0,128},{1,129},{2,130},{3,131},{4,132},{5,133},{6,134},{7,135},{8... | collective-permute-start | bytes 786440 | tf_op jit(solution)/shard_map/ppermute | solution.py:333
  12.7 8.3 %collective-permute-start.1 = (f32[72,128]{1,0:T(8,128)S(1)}, f32[72,128]{1,0:T(8,128)S(1)}, u32[]{:S(2)}, u32[]{:S(2)}) collective-permute-start(f32[72,128]{1,0:T(8,128)S(1)} %shard_map.105.before_ref), channel_id=1, source_target_pairs={{0,0},{1,2},{2,1},{3,4},{4,3},{5,6},{6,5},{7,8},{8,7},{9,10},{10,9... | collective-permute-start | bytes 110600 | tf_op jit(solution)/shard_map/ppermute | solution.py:352
  20.0 4.4 %collective-permute-start.3 = (f32[72,128]{1,0:T(8,128)S(1)}, f32[72,128]{1,0:T(8,128)S(1)}, u32[]{:S(2)}, u32[]{:S(2)}) collective-permute-start(f32[72,128]{1,0:T(8,128)S(1)} %shard_map.106.own_ref), channel_id=1, source_target_pairs={{0,1},{1,0},{2,3},{3,2},{4,5},{5,4},{6,7},{7,6},{8,9},{9,8},{10,11... | collective-permute-start | bytes 110600 | tf_op jit(solution)/shard_map/ppermute | solution.py:359
  22.2 10.9 %copy-start.1 = (bf16[96,384]{1,0:T(8,128)(2,1)S(1)}, bf16[96,384]{1,0:T(8,128)(2,1)}, u32[]{:S(2)}) copy-start(bf16[96,384]{1,0:T(8,128)(2,1)} %constant.44.clone.spread_ref) | copy-start | bytes 221188
  25.0 5.8 %collective-permute-start.4 = (f32[40,128]{1,0:T(8,128)S(1)}, f32[40,128]{1,0:T(8,128)S(1)}, u32[]{:S(2)}, u32[]{:S(2)}) collective-permute-start(f32[40,128]{1,0:T(8,128)S(1)} %get-tuple-element.16.to_near_ref), channel_id=1, source_target_pairs={{0,16},{16,0},{32,48},{48,32},{64,80},{80,64},{96,112},{112,96},{1... | collective-permute-start | bytes 61448 | tf_op jit(solution)/shard_map/ppermute | solution.py:361
  28.1 5.1 %collective-permute-start.5 = (f32[40,128]{1,0:T(8,128)S(1)}, f32[40,128]{1,0:T(8,128)S(1)}, u32[]{:S(2)}, u32[]{:S(2)}) collective-permute-start(f32[40,128]{1,0:T(8,128)S(1)} %get-tuple-element.17.to_far_ref), channel_id=1, source_target_pairs={{0,0},{16,32},{32,16},{48,64},{64,48},{80,96},{96,80},{112,112},{1... | collective-permute-start | bytes 61448 | tf_op jit(solution)/shard_map/ppermute | solution.py:362

commit v3 on v2

--- a/solution.py
+++ b/solution.py
@@ -129,83 +129,52 @@
     return flows
 
 
-def local_kernel(flags_ref, patches_ref, table_ref, spec0_ref, spec1_ref, flows_ref, later_ref, current, sums_y, sums_x):
-    odd = flags_ref[1]
-    forward = [table_ref[i] for i in range(3)]
-    inverse = [table_ref[i] for i in range(3, 6)]
-    for py in range(4):
-        for j in range(2):
-            later_ref[py, j] = patches_ref[1, py, 2 * (1 ^ odd) + j]
-    previous = [ref.at[py] for ref in (spec0_ref, spec1_ref) for py in range(4)]
-    for unit in range(8):
-        first = 2 * ((unit // 4) ^ odd)
-        for section, result in ((0, previous[unit]), (1, current.at[unit])):
-            pixels = jnp.concatenate([patches_ref[section, unit % 4, first], patches_ref[section, unit % 4, first + 1]], axis=1)
-            result[...] = spectrum(pixels, *forward)
-    for unit in range(8):
-        along_y, power = moments(previous[unit][...], current[unit], *inverse)
-        sums_y[unit] = along_y
-        sums_x[unit] = power
-
-    flows = jnp.zeros((8, N), F32)
-    for half in range(2):
-        flows += placed_flows([sums_y[half * 4 + i] for i in range(4)], [sums_x[half * 4 + i] for i in range(4)], 1, 2 * (half ^ odd))
-    flows_ref[...] = flows
-
-
-def pack_nodes(out_ref, start_ref, weight_ref, edges_ref, nodes_ref, share_ref):
-    out_ref[8:, :] = jnp.zeros((64, N), F32)
-    fields = [start_ref[s, c] for s in range(2) for c in range(2)]
-    fields += [weight_ref[0], weight_ref[1], edges_ref[0].astype(F32), edges_ref[2].astype(F32)]
-    fields += [nodes_ref[k].astype(F32) for k in range(4)] + [share_ref[k] for k in range(4)]
-    for at, field in enumerate(fields):
-        row, lane = 8 + at // 4 * 16, at % 4 * GROUP + EDGE
-        out_ref[row : row + 16, lane : lane + 16] = field
-
-
-def chained_kernel(half, flags_ref, prior_ref, recv_ref, spec_ref, before_ref, table_ref, *rest):
-    *node_refs, out_ref, previous = rest
-    at_start, odd = flags_ref[0] == 0, flags_ref[1]
-    forward = [table_ref[i] for i in range(3)]
-    inverse = [table_ref[i] for i in range(3, 6)]
-    first = 2 * (half ^ odd)
-    if half == 0:
-        pack_nodes(out_ref, *node_refs)
-    else:
-        out_ref[8:, :] = before_ref[8:, :]
-    for py in range(4):
-        own = jnp.concatenate([prior_ref[py, first], prior_ref[py, first + 1]], axis=1)
-        other = jnp.concatenate([recv_ref[py, 0], recv_ref[py, 1]], axis=1)
-        previous[py] = spectrum(jnp.where(at_start, own, other), *forward)
-    sums = [moments(previous[py], spec_ref[py], *inverse) for py in range(4)]
-    flows = before_ref[0:8, :] + placed_flows([s[0] for s in sums], [s[1] for s in sums], 0, first)
-    out_ref[0:8, :] = flows
-
-
-def beside(base, values, on_right):
+def column_flows(sums_y, sums_x, first_unit, section, first_col):
+    units = range(first_unit, first_unit + 4)
+    return placed_flows([sums_y[u] for u in units], [sums_x[u] for u in units], section, first_col)
+
+
+def group_lanes(rows):
+    return lax.broadcasted_iota(jnp.int32, (rows, N), 1) % GROUP
+
+
+def edge_columns(nodes, on_right):
+    lane = group_lanes(16)
+    edge = jnp.zeros((16, N), F32)
+    for at in range(4):
+        field, to = nodes[16 * at : 16 * at + 16], EDGE * at
+        side = jnp.where(on_right, pltpu.roll(field, (to - 16) % N, 1), pltpu.roll(field, (to - EDGE) % N, 1))
+        edge = jnp.where((lane >= to) & (lane < to + EDGE), side, edge)
+    return edge
+
+
+def beside(flows, nodes, message, on_right):
     lane = lax.broadcasted_iota(jnp.int32, (8, N), 1) % 8
-    left = jnp.where(lane < 2, pltpu.roll(values[:8], N - 4, 1), base[:8])
-    right = jnp.where(lane >= 6, pltpu.roll(values[:8], 4, 1), base[:8])
-    flows = jnp.where(on_right, right, left)
-    lane = lax.broadcasted_iota(jnp.int32, (64, N), 1) % GROUP
-    left = jnp.where(lane < EDGE, pltpu.roll(values[8:], N - 16, 1), base[8:])
-    right = jnp.where((lane >= EDGE + 16) & (lane < 2 * EDGE + 16), pltpu.roll(values[8:], 16, 1), base[8:])
-    return flows, jnp.where(on_right, right, left)
-
-
-def far_columns_kernel(flags_ref, far_ref, own_ref, out_ref, field_ref):
-    base = own_ref[...]
-    flows, nodes = beside(base, far_ref[...] * flags_ref[2].astype(F32), flags_ref[1] == 1)
+    left = jnp.where(lane < 2, pltpu.roll(message[:8], N - 4, 1), flows)
+    right = jnp.where(lane >= 6, pltpu.roll(message[:8], 4, 1), flows)
+    lane, edge = group_lanes(16), message[8:]
+    first = jnp.where(on_right, EDGE + 16, 0)
+    place = (lane >= first) & (lane < first + EDGE)
+    fields = []
+    for at in range(4):
+        side = jnp.where(on_right, pltpu.roll(edge, (EDGE + 16 - EDGE * at) % N, 1), pltpu.roll(edge, -EDGE * at % N, 1))
+        fields.append(jnp.where(place, side, nodes[16 * at : 16 * at + 16]))
+    return jnp.where(on_right, right, left), jnp.concatenate(fields, axis=0)
+
+
+def own_kernel(flags_ref, flows_ref, middle_ref, edge_ref, out_ref):
+    out_ref[0:8, :] = flows_ref[0:8, :] + middle_ref[...] * flags_ref[0].astype(F32)
+    out_ref[8:, :] = edge_ref[...]
+
+
+def far_columns_kernel(flags_ref, own_ref, nodes_ref, far_ref, out_ref):
+    flows, nodes = beside(own_ref[0:8, :], nodes_ref[...], far_ref[...] * flags_ref[2].astype(F32), flags_ref[1] == 1)
     out_ref[0:8, :] = flows
     out_ref[8:, :] = nodes
-    for s in range(2):
-        for c in range(2):
-            lane = s * 16 + c * 8 + 2
-            field_ref[s, c] = own_ref[2:6, lane : lane + 4]
 
 
 def near_columns_kernel(flags_ref, partial_ref, near_ref, to_near_ref, to_far_ref):
-    flows, nodes = beside(partial_ref[...], near_ref[...], flags_ref[1] == 0)
+    flows, nodes = beside(partial_ref[0:8, :], partial_ref[8:, :], near_ref[...], flags_ref[1] == 0)
     top = jnp.concatenate([flows] + [nodes[16 * f : 16 * f + 8] for f in range(4)], axis=0)
     bottom = jnp.concatenate([flows] + [nodes[16 * f + 8 : 16 * f + 16] for f in range(4)], axis=0)
     odd = flags_ref[3] == 1
@@ -213,11 +182,75 @@
     to_far_ref[...] = jnp.where(odd, bottom, top)
 
 
+def local_kernel(flags_ref, table_hbm, patches_hbm, prior_hbm, start_hbm, weight_hbm, edges_hbm, nodes_hbm, share_hbm,
+                 spec_ref, flows_ref, field_ref, far_edge_ref, near_edge_ref, table_ref, patches_ref, prior_ref, start_ref, weight_ref, edges_ref, nodes_ref, share_ref,
+                 before, sums_y, sums_x, sems):
+    at_start, odd = flags_ref[0] == 0, flags_ref[1]
+    pairs = [(table_hbm, table_ref), (patches_hbm, patches_ref), (prior_hbm, prior_ref), (start_hbm, start_ref),
+             (weight_hbm, weight_ref), (edges_hbm, edges_ref), (nodes_hbm, nodes_ref), (share_hbm, share_ref)]
+    copies = [pltpu.make_async_copy(source, target, sems.at[i]) for i, (source, target) in enumerate(pairs)]
+    for copy in copies:
+        copy.start()
+    field_ref[...] = jnp.zeros((64, N), F32)
+    for copy in copies[:2]:
+        copy.wait()
+    forward = [table_ref[i] for i in range(3)]
+    inverse = [table_ref[i] for i in range(3, 6)]
+    units = [(half, py) for half in range(2) for py in range(4)]
+
+    def pixels(ref, index, first):
+        return jnp.concatenate([ref[(*index, first)], ref[(*index, first + 1)]], axis=1)
+
+    for half, py in units:
+        for section in range(2):
+            spec_ref[2 * section + half, py] = spectrum(pixels(patches_ref, (section, py), 2 * (half ^ odd)), *forward)
+    for copy in copies[2:]:
+        copy.wait()
+    for unit, (half, py) in enumerate(units):
+        before[unit] = spectrum(pixels(prior_ref, (py,), 2 * (half ^ odd)), *forward)
+    for unit, (half, py) in enumerate(units):
+        chain = [before[unit], spec_ref[half, py], spec_ref[2 + half, py]]
+        for section in range(2):
+            along_y, power = moments(chain[section], chain[section + 1], *inverse)
+            sums_y[8 * section + unit] = along_y
+            sums_x[8 * section + unit] = power
+
+    flows = [sum(column_flows(sums_y, sums_x, 8 * s + 4 * half, s, 2 * (half ^ odd)) for half in range(2)) for s in range(2)]
+    flows_ref[...] = jnp.where(at_start, flows[0], 0.0) + flows[1]
+
+    fields = [start_ref[s, c] for s in range(2) for c in range(2)]
+    fields += [weight_ref[0], weight_ref[1], edges_ref[0].astype(F32), edges_ref[2].astype(F32)]
+    fields += [nodes_ref[k].astype(F32) for k in range(4)] + [share_ref[k] for k in range(4)]
+    for at, field in enumerate(fields):
+        row, lane = at // 4 * 16, at % 4 * GROUP + EDGE
+        field_ref[row : row + 16, lane : lane + 16] = field
+    nodes = field_ref[...]
+    far_edge_ref[...] = edge_columns(nodes, odd == 1)
+    near_edge_ref[...] = edge_columns(nodes, odd == 0)
+
+
+def middle_kernel(flags_ref, recv_ref, spec_ref, flows_ref, edge_ref, table_ref, out_ref, middle_ref, other, sums_y, sums_x):
+    gz, odd = flags_ref[0], flags_ref[1]
+    forward = [table_ref[i] for i in range(3)]
+    inverse = [table_ref[i] for i in range(3, 6)]
+    own = 3 * (1 - gz)
+    for py in range(4):
+        other[py] = spectrum(jnp.concatenate([recv_ref[py, 0], recv_ref[py, 1]], axis=1), *forward)
+    for py in range(4):
+        mine, theirs = spec_ref[own, py], other[py]
+        prev, cur = jnp.where(gz == 0, mine, theirs), jnp.where(gz == 0, theirs, mine)
+        sums_y[py], sums_x[py] = moments(prev, cur, *inverse)
+    flows = column_flows(sums_y, sums_x, 0, 0, 2 * (1 - gz ^ odd))
+    middle_ref[...] = flows
+    out_ref[0:8, :] = flows_ref[...] + jnp.where(gz == 0, 0.0, flows)
+    out_ref[8:, :] = edge_ref[...]
+
+
 def shifted_rows(values, by):
     return pltpu.roll(values, by % values.shape[0], 0)
 
 
-def nodes_kernel(flags_ref, to_near_ref, to_far_ref, near_ref, far_ref, spread_ref, out_ref):
+def nodes_kernel(flags_ref, to_near_ref, to_far_ref, far_ref, near_ref, spread_ref, field_ref, out_ref):
     odd = flags_ref[3] == 1
     near, far = near_ref[...], far_ref[...] * flags_ref[4].astype(F32)
     above, below = jnp.where(odd, near, far), jnp.where(odd, far, near)
@@ -276,6 +309,8 @@
         moved = moved + STEP_SIZE * (stiffness * (target - moved) + springs)
     for s in range(2):
         for c in range(2):
+            lane = s * 16 + c * 8 + 2
+            field_ref[s, c] = top[2:6, lane : lane + 4]
             lane = (2 * s + c) * GROUP + EDGE
             out_ref[s, c] = moved[8:24, lane : lane + 16]
 
@@ -292,8 +327,9 @@
     return table.reshape(96, 3 * N).astype(ml_dtypes.bfloat16)
 
 
-def call(kernel, inputs, out_shapes, scratch=(), flops=0, moved=0):
-    memory = [pltpu.SMEM] + [pltpu.VMEM] * (len(inputs) - 1)
+def call(kernel, inputs, out_shapes, scratch=(), flops=0, moved=0, from_hbm=()):
+    from_hbm = [pltpu.with_memory_space_constraint(a, pltpu.HBM) for a in from_hbm]
+    memory = [pltpu.SMEM] + [pltpu.VMEM] * (len(inputs) - 1) + [pltpu.HBM] * len(from_hbm)
     return pl.pallas_call(
         kernel,
         out_shape=out_shapes,
@@ -302,7 +338,7 @@
         scratch_shapes=scratch,
         compiler_params=pltpu.CompilerParams(vmem_limit_bytes=VMEM_LIMIT),
         cost_estimate=pl.CostEstimate(flops=flops, bytes_accessed=moved, transcendentals=0),
-    )(*inputs)
+    )(*inputs, *from_hbm)
 
 
 def f32(*shape):
@@ -328,40 +364,35 @@
     has_far = (gx > 0) & (gx < cols - 1)
     has_far_row = (gy > 0) & (gy < rows - 1)
     flags = jnp.stack([gz, odd, has_far, odd_row, has_far_row]).astype(jnp.int32)
-
-    def to_next_section(values):
-        return lax.ppermute(values, "gz", [(0, 1)])
-
-    early = to_next_section(lax.dynamic_slice_in_dim(patches[1], 2 * odd, 2, axis=1))
     table = jnp.asarray(tables())
-    half_spec = f32(4, N, 2 * N)
-    spec0, spec1, flows, later = call(
-        local_kernel,
-        [flags, patches, table],
-        [half_spec, half_spec, f32(8, N), jax.ShapeDtypeStruct((4, 2, N, N), BF16)],
-        [pltpu.VMEM((8, N, 2 * N), F32), pltpu.VMEM((8, 1, N), F32), pltpu.VMEM((8, 1, 2 * N), F32)],
-        flops=5_000_000_000, moved=4_000_000,
+
+    first_col = 2 * (odd ^ gz)
+    chunk = lax.dynamic_slice(patches, (1 - gz, 0, first_col, 0, 0), (1, 4, 2, N, N))[0]
+    received = lax.ppermute(chunk, "gz", [(0, 1), (1, 0)])
+    sums = [pltpu.VMEM((16, 1, N), F32), pltpu.VMEM((16, 1, 2 * N), F32)]
+    arrays = [patches, prior_patches, start_offset, flow_weight, edges, node_patch, node_weight]
+    spec, flows, nodes, far_edge, near_edge, table = call(
+        local_kernel, [flags],
+        [f32(4, 4, N, 2 * N), f32(8, N), f32(64, N), f32(16, N), f32(16, N), jax.ShapeDtypeStruct(table.shape, table.dtype)],
+        [*(pltpu.VMEM(a.shape, a.dtype) for a in arrays), pltpu.VMEM((8, N, 2 * N), F32), *sums, pltpu.SemaphoreType.DMA((8,))],
+        flops=8_000_000_000, moved=4_000_000, from_hbm=[table, *arrays],
     )
-    late = to_next_section(later)
-    scratch = [pltpu.VMEM((4, N, 2 * N), F32)]
-    (first,) = call(
-        functools.partial(chained_kernel, 0),
-        [flags, prior_patches, early, spec0, flows, table, start_offset, flow_weight, edges, node_patch, node_weight],
-        [f32(72, N)], scratch, flops=2_000_000_000, moved=2_000_000,
+    to_far, middle = call(
+        middle_kernel, [flags, received, spec, flows, far_edge, table],
+        [f32(24, N), f32(8, N)], [pltpu.VMEM((4, N, 2 * N), F32), *sums],
+        flops=2_000_000_000, moved=2_000_000,
     )
-    from_far = lax.ppermute(first, "gx", far_partner(cols))
-    (own,) = call(
-        functools.partial(chained_kernel, 1), [flags, prior_patches, late, spec1, first, table],
-        [f32(72, N)], scratch, flops=2_000_000_000, moved=2_000_000,
-    )
-    partial, flow_field = call(
-        far_columns_kernel, [flags, from_far, own], [f32(72, N), f32(2, 2, 4, 4)], flops=5_000_000_000, moved=2_000_000)
-    from_near = lax.ppermute(own, "gx", near_partner(cols))
+    own_middle = lax.ppermute(middle, "gz", [(0, 1), (1, 0)])
+    from_far = lax.ppermute(to_far, "gx", far_partner(cols))
+    to_near = call(own_kernel, [flags, to_far, own_middle, near_edge], f32(24, N), flops=1_000_000_000, moved=1_000_000)
+    from_near = lax.ppermute(to_near, "gx", near_partner(cols))
+    partial = call(far_columns_kernel, [flags, to_near, nodes, from_far], f32(72, N), flops=5_000_000_000, moved=2_000_000)
     to_near, to_far = call(near_columns_kernel, [flags, partial, from_near], [f32(40, N), f32(40, N)])
+    row_far = lax.ppermute(to_far, "gy", far_partner(rows))
     row_near = lax.ppermute(to_near, "gy", near_partner(rows))
-    row_far = lax.ppermute(to_far, "gy", far_partner(rows))
-    displacement = call(
-        nodes_kernel, [flags, to_near, to_far, row_near, row_far, jnp.asarray(spread_table())], f32(2, 2, 16, 16))
+    flow_field, displacement = call(
+        nodes_kernel, [flags, to_near, to_far, row_far, row_near, jnp.asarray(spread_table())],
+        [f32(2, 2, 4, 4), f32(2, 2, 16, 16)])
     return flow_field, displacement
 
 

time: 35 us -> 32.7 us (0.934)
  the two profiles are of different devices: /device:TPU:125 before, /device:TPU:165 now
where the time goes in v3:
time: 32.7 us; the launch traced here: 32.5 us
  starting transfers between devices  13.6 us (42%)
  Pallas kernels  11.7 us (36%)
  waiting for transfers between devices  5.42 us (17%)
  local copies, waits for them, and re-layouts  1.07 us (3%)
  between operations  0.73 us (2%)
    pallas_call x6, Pallas kernels, call(): pl.pallas_call(kernel, out_shape=out_shapes, in_specs=[pl.BlockSpec(memor...  11.7 us
    ppermute x1, starting transfers between devices, body(): from_far = lax.ppermute(to_far, 'gx', far_partner(cols))  4.96 us
    ppermute x1, starting transfers between devices, body(): row_near = lax.ppermute(to_near, 'gy', near_partner(rows))  3.34 us
    ppermute x1, starting transfers between devices, body(): row_far = lax.ppermute(to_far, 'gy', far_partner(rows))  2.72 us
    ppermute x1, waiting for transfers between devices, body(): row_far = lax.ppermute(to_far, 'gy', far_partner(rows))  2.35 us
    ppermute x1, waiting for transfers between devices, body(): from_near = lax.ppermute(to_near, 'gx', near_partner(cols))  2.21 us
    ppermute x1, starting transfers between devices, body(): received = lax.ppermute(chunk, 'gz', [(0, 1), (1, 0)])  1.38 us
    squeeze x1, local copies, waits for them, and re-layouts, body(): lax.dynamic_slice(patches, (1 - gz, 0, first_col, 0, 0), (1, 4, 2, N, N))[0]  0.98 us
  transfers between devices with their start and end apart: 6, of which 3 were waited for; matrix products, arithmetic and copies ran while one was open for 0% of the time, Pallas kernels for 23%

profile of v3, /device:TPU:165, one launch (start us, length us, event | category | flops | bytes accessed | tf_op | source)
XLA Modules:
  0.0 32.5 jit_solution(8840286853805105022)
XLA Ops:
  0.6 1.0 %dynamic-slice_bitcast_fusion = bf16[4,2,128,128]{3,2,1,0:T(8,128)(2,1)S(1)} fusion(bf16[2,4,4,128,128]{4,3,2,1,0:T(8,128)(2,1)} %patches_hbm.1, s32[]{:T(128)S(6)} %select_n.19, s32[]{:T(128)S(6)} %select_n.20), kind=kLoop, calls=%fused_computation | loop fusion | bytes 524296 | tf_op jit(solution)/shard_map/squeeze | solution.py:370
  1.6 1.4 %collective-permute-start = (bf16[4,2,128,128]{3,2,1,0:T(8,128)(2,1)S(1)}, bf16[4,2,128,128]{3,2,1,0:T(8,128)(2,1)S(1)}, u32[]{:S(2)}, u32[]{:S(2)}) collective-permute-start(bf16[4,2,128,128]{3,2,1,0:T(8,128)(2,1)S(1)} %dynamic-slice_bitcast_fusion), channel_id=1, source_target_pairs={{0,128},{128,0},{1,129},{129,1},{2,130},{130,2},{3,131},{131,3},{4... | collective-permute-start | bytes 786440 | tf_op jit(solution)/shard_map/ppermute | solution.py:371
  3.0 0.1 stack.31.flags_ref
  3.1 6.4 %shard_map.104 = (f32[4,4,128,256]{3,2,1,0:T(8,128)S(1)}, f32[8,128]{1,0:T(8,128)S(1)}, f32[64,128]{1,0:T(8,128)S(1)}, f32[16,128]{1,0:T(8,128)S(1)}, f32[16,128...) custom-call(s32[5]{0:T(128)S(1)} %stack.31.flags_ref, bf16[6,256,256]{2,1,0:T(8,128)(2,1)} %constant.45.clone.table_hbm, ...), custom_call_target="tpu_custom_call" | custom-call | flops 8000000000 | bytes 4000000 | tf_op jit(solution)/shard_map/pallas_call | solution.py:333
  9.5 0.0 collective-permute-done.recv_ref
  9.5 1.9 %shard_map.105 = (f32[24,128]{1,0:T(8,128)S(1)}, f32[8,128]{1,0:T(8,128)S(1)}) custom-call(s32[5]{0:T(128)S(1)} %stack.31.flags_ref, bf16[4,2,128,128]{3,2,1,0:T(8,128)(2,1)S(1)} %collective-permute-done.recv_ref, f32[4,4,128,256]{3,2,1,0:T(8,128)S(1)} %get-tuple-element.12.spec_ref, f32[8,128]{1,0:T(8,128)S(1)} %get-tuple-element.13.flows_ref, ...), custom_call_target="tpu_custom_call" | custom-call | flops 2000000000 | bytes 2000000 | tf_op jit(solution)/shard_map/pallas_call | solution.py:333
  11.4 0.7 %collective-permute-start.1 = (f32[8,128]{1,0:T(8,128)S(1)}, f32[8,128]{1,0:T(8,128)S(1)}, u32[]{:S(2)}, u32[]{:S(2)}) collective-permute-start(f32[8,128]{1,0:T(8,128)S(1)} %get-tuple-element.17), channel_id=1, source_target_pairs={{0,128},{128,0},{1,129},{129,1},{2,130},{130,2},{3,131},{131,3},{4... | collective-permute-start | bytes 12296 | tf_op jit(solution)/shard_map/ppermute | solution.py:385
  12.2 5.0 %collective-permute-start.2 = (f32[24,128]{1,0:T(8,128)S(1)}, f32[24,128]{1,0:T(8,128)S(1)}, u32[]{:S(2)}, u32[]{:S(2)}) collective-permute-start(f32[24,128]{1,0:T(8,128)S(1)} %get-tuple-element.16.flows_ref), channel_id=1, source_target_pairs={{0,0},{1,2},{2,1},{3,4},{4,3},{5,6},{6,5},{7,8},{8,7},{9,10},{10,9... | collective-permute-start | bytes 36872 | tf_op jit(solution)/shard_map/ppermute | solution.py:386
  17.1 0.0 collective-permute-done.1.middle_ref
  17.2 0.5 %shard_map.106.own_ref = f32[24,128]{1,0:T(8,128)S(1)} custom-call(s32[5]{0:T(128)S(1)} %stack.31.flags_ref, f32[24,128]{1,0:T(8,128)S(1)} %get-tuple-element.16.flows_ref, f32[8,128]{1,0:T(8,128)S(1)} %collective-permute-done.1.middle_ref, f32[16,128]{1,0:T(8,128)S(1)} %get-tuple-element.18.edge_ref), custom_call_target="tpu_custom_call" | custom-call | flops 1000000000 | bytes 1000000 | tf_op jit(solution)/shard_map/pallas_call | solution.py:333
  17.7 0.4 %collective-permute-start.3 = (f32[24,128]{1,0:T(8,128)S(1)}, f32[24,128]{1,0:T(8,128)S(1)}, u32[]{:S(2)}, u32[]{:S(2)}) collective-permute-start(f32[24,128]{1,0:T(8,128)S(1)} %shard_map.106.own_ref), channel_id=1, source_target_pairs={{0,1},{1,0},{2,3},{3,2},{4,5},{5,4},{6,7},{7,6},{8,9},{9,8},{10,11... | collective-permute-start | bytes 36872 | tf_op jit(solution)/shard_map/ppermute | solution.py:388
  18.2 0.8 %collective-permute-done.2.far_ref = f32[24,128]{1,0:T(8,128)S(1)} collective-permute-done((f32[24,128]{1,0:T(8,128)S(1)}, f32[24,128]{1,0:T(8,128)S(1)}, u32[]{:S(2)}, u32[]{:S(2)}) %collective-permute-start.2) | collective-permute-done | bytes 12320 | tf_op jit(solution)/shard_map/ppermute | solution.py:386
  19.0 0.0 copy-start
  19.0 0.6 %shard_map.107.partial_ref = f32[72,128]{1,0:T(8,128)S(1)} custom-call(s32[5]{0:T(128)S(1)} %stack.31.flags_ref, f32[24,128]{1,0:T(8,128)S(1)} %shard_map.106.own_ref, f32[64,128]{1,0:T(8,128)S(1)} %get-tuple-element.19.nodes_ref, f32[24,128]{1,0:T(8,128)S(1)} %collective-permute-done.2.far_ref), custom_call_target="tpu_custom_call" | custom-call | flops 5000000000 | bytes 2000000 | tf_op jit(solution)/shard_map/pallas_call | solution.py:333
  19.6 2.2 %collective-permute-done.3.near_ref = f32[24,128]{1,0:T(8,128)S(1)} collective-permute-done((f32[24,128]{1,0:T(8,128)S(1)}, f32[24,128]{1,0:T(8,128)S(1)}, u32[]{:S(2)}, u32[]{:S(2)}) %collective-permute-start.3) | collective-permute-done | bytes 12320 | tf_op jit(solution)/shard_map/ppermute | solution.py:388
  21.8 0.6 %shard_map.108 = (f32[40,128]{1,0:T(8,128)S(1)}, f32[40,128]{1,0:T(8,128)S(1)}) custom-call(s32[5]{0:T(128)S(1)} %stack.31.flags_ref, f32[72,128]{1,0:T(8,128)S(1)} %shard_map.107.partial_ref, f32[24,128]{1,0:T(8,128)S(1)} %collective-permute-done.3.near_ref), custom_call_target="tpu_custom_call" | custom-call | tf_op jit(solution)/shard_map/pallas_call | solution.py:333
  22.5 3.3 %collective-permute-start.5 = (f32[40,128]{1,0:T(8,128)S(1)}, f32[40,128]{1,0:T(8,128)S(1)}, u32[]{:S(2)}, u32[]{:S(2)}) collective-permute-start(f32[40,128]{1,0:T(8,128)S(1)} %get-tuple-element.20.to_near_ref), channel_id=1, source_target_pairs={{0,16},{16,0},{32,48},{48,32},{64,80},{80,64},{96,112},{112,96},{1... | collective-permute-start | bytes 61448 | tf_op jit(solution)/shard_map/ppermute | solution.py:392
  25.8 2.7 %collective-permute-start.4 = (f32[40,128]{1,0:T(8,128)S(1)}, f32[40,128]{1,0:T(8,128)S(1)}, u32[]{:S(2)}, u32[]{:S(2)}) collective-permute-start(f32[40,128]{1,0:T(8,128)S(1)} %get-tuple-element.21.to_far_ref), channel_id=1, source_target_pairs={{0,0},{16,32},{32,16},{48,64},{64,48},{80,96},{96,80},{112,112},{1... | collective-permute-start | bytes 61448 | tf_op jit(solution)/shard_map/ppermute | solution.py:391
  28.5 0.0 collective-permute-done.5.near_ref
  28.6 2.3 %collective-permute-done.4.far_ref = f32[40,128]{1,0:T(8,128)S(1)} collective-permute-done((f32[40,128]{1,0:T(8,128)S(1)}, f32[40,128]{1,0:T(8,128)S(1)}, u32[]{:S(2)}, u32[]{:S(2)}) %collective-permute-start.4) | collective-permute-done | bytes 20512 | tf_op jit(solution)/shard_map/ppermute | solution.py:391
  30.9 0.0 copy-done
  30.9 1.6 %shard_map.109 = (f32[2,2,4,4]{3,2,1,0:T(4,128)}, f32[2,2,16,16]{3,2,1,0:T(8,128)}) custom-call(s32[5]{0:T(128)S(1)} %stack.31.flags_ref, f32[40,128]{1,0:T(8,128)S(1)} %get-tuple-element.20.to_near_ref, f32[40,128]{1,0:T(8,128)S(1)} %get-tuple-element.21.to_far_ref, f32[40,128]{1,0:T(8,128)S(1)} %collective-permute-done.4.far_ref, ...), custom_call_target="tpu_custom_call" | custom-call | tf_op jit(solution)/shard_map/pallas_call | solution.py:333
Async XLA Ops:
  1.6 7.9 %collective-permute-start = (bf16[4,2,128,128]{3,2,1,0:T(8,128)(2,1)S(1)}, bf16[4,2,128,128]{3,2,1,0:T(8,128)(2,1)S(1)}, u32[]{:S(2)}, u32[]{:S(2)}) collective-permute-start(bf16[4,2,128,128]{3,2,1,0:T(8,128)(2,1)S(1)} %dynamic-slice_bitcast_fusion), channel_id=1, source_target_pairs={{0,128},{128,0},{1,129},{129,1},{2,130},{130,2},{3,131},{131,3},{4... | collective-permute-start | bytes 786440 | tf_op jit(solution)/shard_map/ppermute | solution.py:371
  11.4 5.7 %collective-permute-start.1 = (f32[8,128]{1,0:T(8,128)S(1)}, f32[8,128]{1,0:T(8,128)S(1)}, u32[]{:S(2)}, u32[]{:S(2)}) collective-permute-start(f32[8,128]{1,0:T(8,128)S(1)} %get-tuple-element.17), channel_id=1, source_target_pairs={{0,128},{128,0},{1,129},{129,1},{2,130},{130,2},{3,131},{131,3},{4... | collective-permute-start | bytes 12296 | tf_op jit(solution)/shard_map/ppermute | solution.py:385
  12.2 6.8 %collective-permute-start.2 = (f32[24,128]{1,0:T(8,128)S(1)}, f32[24,128]{1,0:T(8,128)S(1)}, u32[]{:S(2)}, u32[]{:S(2)}) collective-permute-start(f32[24,128]{1,0:T(8,128)S(1)} %get-tuple-element.16.flows_ref), channel_id=1, source_target_pairs={{0,0},{1,2},{2,1},{3,4},{4,3},{5,6},{6,5},{7,8},{8,7},{9,10},{10,9... | collective-permute-start | bytes 36872 | tf_op jit(solution)/shard_map/ppermute | solution.py:386
  17.7 4.1 %collective-permute-start.3 = (f32[24,128]{1,0:T(8,128)S(1)}, f32[24,128]{1,0:T(8,128)S(1)}, u32[]{:S(2)}, u32[]{:S(2)}) collective-permute-start(f32[24,128]{1,0:T(8,128)S(1)} %shard_map.106.own_ref), channel_id=1, source_target_pairs={{0,1},{1,0},{2,3},{3,2},{4,5},{5,4},{6,7},{7,6},{8,9},{9,8},{10,11... | collective-permute-start | bytes 36872 | tf_op jit(solution)/shard_map/ppermute | solution.py:388
  19.0 11.9 %copy-start = (bf16[96,384]{1,0:T(8,128)(2,1)S(1)}, bf16[96,384]{1,0:T(8,128)(2,1)}, u32[]{:S(2)}) copy-start(bf16[96,384]{1,0:T(8,128)(2,1)} %constant.46.clone.spread_ref) | copy-start | bytes 221188
  22.5 6.1 %collective-permute-start.5 = (f32[40,128]{1,0:T(8,128)S(1)}, f32[40,128]{1,0:T(8,128)S(1)}, u32[]{:S(2)}, u32[]{:S(2)}) collective-permute-start(f32[40,128]{1,0:T(8,128)S(1)} %get-tuple-element.20.to_near_ref), channel_id=1, source_target_pairs={{0,16},{16,0},{32,48},{48,32},{64,80},{80,64},{96,112},{112,96},{1... | collective-permute-start | bytes 61448 | tf_op jit(solution)/shard_map/ppermute | solution.py:392
  25.8 5.1 %collective-permute-start.4 = (f32[40,128]{1,0:T(8,128)S(1)}, f32[40,128]{1,0:T(8,128)S(1)}, u32[]{:S(2)}, u32[]{:S(2)}) collective-permute-start(f32[40,128]{1,0:T(8,128)S(1)} %get-tuple-element.21.to_far_ref), channel_id=1, source_target_pairs={{0,0},{16,32},{32,16},{48,64},{64,48},{80,96},{96,80},{112,112},{1... | collective-permute-start | bytes 61448 | tf_op jit(solution)/shard_map/ppermute | solution.py:391

commit v4 on v3

--- a/solution.py
+++ b/solution.py
@@ -162,24 +162,10 @@
     return jnp.where(on_right, right, left), jnp.concatenate(fields, axis=0)
 
 
-def own_kernel(flags_ref, flows_ref, middle_ref, edge_ref, out_ref):
-    out_ref[0:8, :] = flows_ref[0:8, :] + middle_ref[...] * flags_ref[0].astype(F32)
-    out_ref[8:, :] = edge_ref[...]
-
-
 def far_columns_kernel(flags_ref, own_ref, nodes_ref, far_ref, out_ref):
-    flows, nodes = beside(own_ref[0:8, :], nodes_ref[...], far_ref[...] * flags_ref[2].astype(F32), flags_ref[1] == 1)
+    flows, nodes = beside(own_ref[...], nodes_ref[...], far_ref[...] * flags_ref[2].astype(F32), flags_ref[1] == 1)
     out_ref[0:8, :] = flows
     out_ref[8:, :] = nodes
-
-
-def near_columns_kernel(flags_ref, partial_ref, near_ref, to_near_ref, to_far_ref):
-    flows, nodes = beside(partial_ref[0:8, :], partial_ref[8:, :], near_ref[...], flags_ref[1] == 0)
-    top = jnp.concatenate([flows] + [nodes[16 * f : 16 * f + 8] for f in range(4)], axis=0)
-    bottom = jnp.concatenate([flows] + [nodes[16 * f + 8 : 16 * f + 16] for f in range(4)], axis=0)
-    odd = flags_ref[3] == 1
-    to_near_ref[...] = jnp.where(odd, top, bottom)
-    to_far_ref[...] = jnp.where(odd, bottom, top)
 
 
 def local_kernel(flags_ref, table_hbm, patches_hbm, prior_hbm, start_hbm, weight_hbm, edges_hbm, nodes_hbm, share_hbm,
@@ -251,20 +237,32 @@
 
 
 def nodes_kernel(flags_ref, to_near_ref, to_far_ref, far_ref, near_ref, spread_ref, field_ref, out_ref):
-    odd = flags_ref[3] == 1
-    near, far = near_ref[...], far_ref[...] * flags_ref[4].astype(F32)
+    odd, near_on_right = flags_ref[3] == 1, flags_ref[1] == 0
+    near, far = near_ref[...], far_ref[...]
     above, below = jnp.where(odd, near, far), jnp.where(odd, far, near)
     top = jnp.where(odd, to_near_ref[...], to_far_ref[...])
     bottom = jnp.where(odd, to_far_ref[...], to_near_ref[...])
-
+    blocks = (above, top, bottom, below)
+    flow_lane, lane = lax.broadcasted_iota(jnp.int32, (8, N), 1) % 8, group_lanes(8)
+    flow_side = jnp.where(near_on_right, 6, 0)
+    first = jnp.where(near_on_right, EDGE + 16, 0)
+
+    def flows_of(block):
+        side = jnp.where(near_on_right, pltpu.roll(block[8:16], 4, 1), pltpu.roll(block[8:16], N - 4, 1))
+        return jnp.where((flow_lane >= flow_side) & (flow_lane < flow_side + 2), side, block[0:8])
+
+    def field(at):
+        rows = []
+        for block in blocks:
+            edge = block[48:56]
+            side = jnp.where(near_on_right, pltpu.roll(edge, (EDGE + 16 - EDGE * at) % N, 1), pltpu.roll(edge, -EDGE * at % N, 1))
+            rows.append(jnp.where((lane >= first) & (lane < first + EDGE), side, block[16 + 8 * at : 24 + 8 * at]))
+        return jnp.concatenate(rows, axis=0)
+
+    moved, mixed, patch, share = (field(at) for at in range(4))
+    own_flows = flows_of(top)
     row = lax.broadcasted_iota(jnp.int32, (8, N), 0)
-    window = jnp.where(row < 2, pltpu.roll(above[:8], 4, 0), jnp.where(row < 6, top[:8], pltpu.roll(below[:8], 4, 0)))
-
-    def field(at):
-        part = slice(8 + 8 * at, 16 + 8 * at)
-        return jnp.concatenate([above[part], top[part], bottom[part], below[part]], axis=0)
-
-    moved, mixed, patch, share = (field(at) for at in range(4))
+    window = jnp.where(row < 2, pltpu.roll(flows_of(above), 4, 0), jnp.where(row < 6, own_flows, pltpu.roll(flows_of(below), 4, 0)))
 
     narrow = window[:, : 4 * 8]
     part1 = narrow.astype(BF16)
@@ -310,7 +308,7 @@
     for s in range(2):
         for c in range(2):
             lane = s * 16 + c * 8 + 2
-            field_ref[s, c] = top[2:6, lane : lane + 4]
+            field_ref[s, c] = own_flows[2:6, lane : lane + 4]
             lane = (2 * s + c) * GROUP + EDGE
             out_ref[s, c] = moved[8:24, lane : lane + 16]
 
@@ -363,7 +361,7 @@
     odd, odd_row = gx % 2, gy % 2
     has_far = (gx > 0) & (gx < cols - 1)
     has_far_row = (gy > 0) & (gy < rows - 1)
-    flags = jnp.stack([gz, odd, has_far, odd_row, has_far_row]).astype(jnp.int32)
+    flags = jnp.stack([gz, odd, has_far, odd_row]).astype(jnp.int32)
     table = jnp.asarray(tables())
 
     first_col = 2 * (odd ^ gz)
@@ -384,11 +382,16 @@
     )
     own_middle = lax.ppermute(middle, "gz", [(0, 1), (1, 0)])
     from_far = lax.ppermute(to_far, "gx", far_partner(cols))
-    to_near = call(own_kernel, [flags, to_far, own_middle, near_edge], f32(24, N), flops=1_000_000_000, moved=1_000_000)
-    from_near = lax.ppermute(to_near, "gx", near_partner(cols))
-    partial = call(far_columns_kernel, [flags, to_near, nodes, from_far], f32(72, N), flops=5_000_000_000, moved=2_000_000)
-    to_near, to_far = call(near_columns_kernel, [flags, partial, from_near], [f32(40, N), f32(40, N)])
-    row_far = lax.ppermute(to_far, "gy", far_partner(rows))
+    own = to_far[:8] + own_middle * gz.astype(F32)
+    from_near = lax.ppermute(jnp.concatenate([own, near_edge]), "gx", near_partner(cols))
+    partial = call(far_columns_kernel, [flags, own, nodes, from_far], f32(72, N), flops=5_000_000_000, moved=2_000_000)
+
+    def rows_of(first):
+        return jnp.concatenate([partial[:8], from_near[:8]] + [partial[8 + 16 * f + first :][:8] for f in range(4)] + [from_near[8 + first :][:8]])
+
+    top, bottom = rows_of(0), rows_of(8)
+    to_near, to_far = jnp.where(odd_row == 1, top, bottom), jnp.where(odd_row == 1, bottom, top)
+    row_far = lax.ppermute(to_far, "gy", far_partner(rows)) * has_far_row.astype(F32)
     row_near = lax.ppermute(to_near, "gy", near_partner(rows))
     flow_field, displacement = call(
         nodes_kernel, [flags, to_near, to_far, row_far, row_near, jnp.asarray(spread_table())],

time: 32.7 us -> 31.4 us (0.960)
  the two profiles are of different devices: /device:TPU:165 before, /device:TPU:195 now
where the time goes in v4:
time: 31.4 us; the launch traced here: 31.2 us
  starting transfers between devices  13.7 us (44%)
  Pallas kernels  10.6 us (34%)
  waiting for transfers between devices  5 us (16%)
  local copies, waits for them, and re-layouts  1.01 us (3%)
  between operations  0.81 us (3%)
    pallas_call x4, Pallas kernels, call(): pl.pallas_call(kernel, out_shape=out_shapes, in_specs=[pl.BlockSpec(memor...  10.6 us
    ppermute x1, starting transfers between devices, body(): lax.ppermute(to_far, 'gy', far_partner(rows)) * has_far_row.astype(F32)  5.99 us
    ppermute x1, starting transfers between devices, body(): from_far = lax.ppermute(to_far, 'gx', far_partner(cols))  4.96 us
    ppermute x1, waiting for transfers between devices, body(): lax.ppermute(jnp.concatenate([own, near_edge]), 'gx', near_partner(cols))  1.94 us
    ppermute x1, waiting for transfers between devices, body(): lax.ppermute(to_far, 'gy', far_partner(rows)) * has_far_row.astype(F32)  1.67 us
    ppermute x1, starting transfers between devices, body(): received = lax.ppermute(chunk, 'gz', [(0, 1), (1, 0)])  1.38 us
    ppermute x1, waiting for transfers between devices, body(): from_far = lax.ppermute(to_far, 'gx', far_partner(cols))  1.38 us
    squeeze x1, local copies, waits for them, and re-layouts, body(): lax.dynamic_slice(patches, (1 - gz, 0, first_col, 0, 0), (1, 4, 2, N, N))[0]  0.98 us
  transfers between devices with their start and end apart: 6, of which 3 were waited for; matrix products, arithmetic and copies ran while one was open for 0% of the time, Pallas kernels for 22%

profile of v4, /device:TPU:195, one launch (start us, length us, event | category | flops | bytes accessed | tf_op | source)
XLA Modules:
  0.0 31.2 jit_solution(17923972772751898854)
XLA Ops:
  0.6 1.0 %dynamic-slice_bitcast_fusion = bf16[4,2,128,128]{3,2,1,0:T(8,128)(2,1)S(1)} fusion(bf16[2,4,4,128,128]{4,3,2,1,0:T(8,128)(2,1)} %patches_hbm.1, s32[]{:T(128)S(6)} %select_n.32, s32[]{:T(128)S(6)} %select_n.33), kind=kLoop, calls=%fused_computation | loop fusion | bytes 524296 | tf_op jit(solution)/shard_map/squeeze | solution.py:368
  1.6 1.4 %collective-permute-start = (bf16[4,2,128,128]{3,2,1,0:T(8,128)(2,1)S(1)}, bf16[4,2,128,128]{3,2,1,0:T(8,128)(2,1)S(1)}, u32[]{:S(2)}, u32[]{:S(2)}) collective-permute-start(bf16[4,2,128,128]{3,2,1,0:T(8,128)(2,1)S(1)} %dynamic-slice_bitcast_fusion), channel_id=1, source_target_pairs={{0,128},{128,0},{1,129},{129,1},{2,130},{130,2},{3,131},{131,3},{4... | collective-permute-start | bytes 786440 | tf_op jit(solution)/shard_map/ppermute | solution.py:369
  3.0 0.1 pad_add_fusion.flags_ref
  3.1 6.3 %shard_map.104 = (f32[4,4,128,256]{3,2,1,0:T(8,128)S(1)}, f32[8,128]{1,0:T(8,128)S(1)}, f32[64,128]{1,0:T(8,128)S(1)}, f32[16,128]{1,0:T(8,128)S(1)}, f32[16,128...) custom-call(s32[4]{0:T(128)S(1)} %pad_add_fusion.flags_ref, bf16[6,256,256]{2,1,0:T(8,128)(2,1)} %constant.45.clone.table_hbm, ...), custom_call_target="tpu_custom_call" | custom-call | flops 8000000000 | bytes 4000000 | tf_op jit(solution)/shard_map/pallas_call | solution.py:331
  9.4 0.0 collective-permute-done.recv_ref
  9.4 1.9 %shard_map.105 = (f32[24,128]{1,0:T(8,128)S(1)}, f32[8,128]{1,0:T(8,128)S(1)}) custom-call(s32[4]{0:T(128)S(1)} %pad_add_fusion.flags_ref, bf16[4,2,128,128]{3,2,1,0:T(8,128)(2,1)S(1)} %collective-permute-done.recv_ref, f32[4,4,128,256]{3,2,1,0:T(8,128)S(1)} %get-tuple-element.10.spec_ref, f32[8,128]{1,0:T(8,128)S(1)} %get-tuple-element.11.flows_ref, ...), custom_call_target="tpu_custom_call" | custom-call | flops 2000000000 | bytes 2000000 | tf_op jit(solution)/shard_map/pallas_call | solution.py:331
  11.3 0.8 %collective-permute-start.1 = (f32[8,128]{1,0:T(8,128)S(1)}, f32[8,128]{1,0:T(8,128)S(1)}, u32[]{:S(2)}, u32[]{:S(2)}) collective-permute-start(f32[8,128]{1,0:T(8,128)S(1)} %get-tuple-element.15), channel_id=1, source_target_pairs={{0,128},{128,0},{1,129},{129,1},{2,130},{130,2},{3,131},{131,3},{4... | collective-permute-start | bytes 12296 | tf_op jit(solution)/shard_map/ppermute | solution.py:383
  12.1 5.0 %collective-permute-start.2 = (f32[24,128]{1,0:T(8,128)S(1)}, f32[24,128]{1,0:T(8,128)S(1)}, u32[]{:S(2)}, u32[]{:S(2)}) collective-permute-start(f32[24,128]{1,0:T(8,128)S(1)} %get-tuple-element.14), channel_id=1, source_target_pairs={{0,0},{1,2},{2,1},{3,4},{4,3},{5,6},{6,5},{7,8},{8,7},{9,10},{10,9... | collective-permute-start | bytes 36872 | tf_op jit(solution)/shard_map/ppermute | solution.py:384
  17.1 0.0 collective-permute-done.1
  17.1 0.4 %collective-permute-start.3 = (f32[24,128]{1,0:T(8,128)S(1)}, f32[24,128]{1,0:T(8,128)S(1)}, u32[]{:S(2)}, u32[]{:S(2)}) collective-permute-start(f32[24,128]{1,0:T(8,128)S(1)} %pad_maximum_fusion), channel_id=1, source_target_pairs={{0,1},{1,0},{2,3},{3,2},{4,5},{5,4},{6,7},{7,6},{8,9},{9,8},{10,11... | collective-permute-start | bytes 36872 | tf_op jit(solution)/shard_map/ppermute | solution.py:386
  17.6 1.4 %collective-permute-done.2.far_ref = f32[24,128]{1,0:T(8,128)S(1)} collective-permute-done((f32[24,128]{1,0:T(8,128)S(1)}, f32[24,128]{1,0:T(8,128)S(1)}, u32[]{:S(2)}, u32[]{:S(2)}) %collective-permute-start.2) | collective-permute-done | bytes 12320 | tf_op jit(solution)/shard_map/ppermute | solution.py:384
  19.0 0.0 copy-start
  19.0 0.6 %shard_map.106 = f32[72,128]{1,0:T(8,128)S(1)} custom-call(s32[4]{0:T(128)S(1)} %pad_add_fusion.flags_ref, f32[8,128]{1,0:T(8,128)S(1)} %multiply_add_fusion.own_ref, f32[64,128]{1,0:T(8,128)S(1)} %get-tuple-element.16.nodes_ref, f32[24,128]{1,0:T(8,128)S(1)} %collective-permute-done.2.far_ref), custom_call_target="tpu_custom_call" | custom-call | flops 5000000000 | bytes 2000000 | tf_op jit(solution)/shard_map/pallas_call | solution.py:331
  19.6 1.9 %collective-permute-done.3 = f32[24,128]{1,0:T(8,128)S(1)} collective-permute-done((f32[24,128]{1,0:T(8,128)S(1)}, f32[24,128]{1,0:T(8,128)S(1)}, u32[]{:S(2)}, u32[]{:S(2)}) %collective-permute-start.3) | collective-permute-done | bytes 12320 | tf_op jit(solution)/shard_map/ppermute | solution.py:386
  21.6 6.0 %collective-permute-start.4 = (f32[56,128]{1,0:T(8,128)S(1)}, f32[56,128]{1,0:T(8,128)S(1)}, u32[]{:S(2)}, u32[]{:S(2)}) collective-permute-start(f32[56,128]{1,0:T(8,128)S(1)} %get-tuple-element.18.to_far_ref), channel_id=1, source_target_pairs={{0,0},{16,32},{32,16},{48,64},{64,48},{80,96},{96,80},{112,112},{1... | collective-permute-start | bytes 86024 | tf_op jit(solution)/shard_map/ppermute | solution.py:394
  27.6 0.1 collective-permute-start.5
  27.7 1.7 %collective-permute-done.4 = f32[56,128]{1,0:T(8,128)S(1)} collective-permute-done((f32[56,128]{1,0:T(8,128)S(1)}, f32[56,128]{1,0:T(8,128)S(1)}, u32[]{:S(2)}, u32[]{:S(2)}) %collective-permute-start.4) | collective-permute-done | bytes 28704 | tf_op jit(solution)/shard_map/ppermute | solution.py:394
  29.4 0.0 collective-permute-done.5.near_ref
  29.4 0.0 copy-done
  29.4 1.8 %shard_map.107 = (f32[2,2,4,4]{3,2,1,0:T(4,128)}, f32[2,2,16,16]{3,2,1,0:T(8,128)}) custom-call(s32[4]{0:T(128)S(1)} %pad_add_fusion.flags_ref, f32[56,128]{1,0:T(8,128)S(1)} %get-tuple-element.19.to_near_ref, f32[56,128]{1,0:T(8,128)S(1)} %get-tuple-element.18.to_far_ref, f32[56,128]{1,0:T(8,128)S(1)} %broadcast_multiply_fusion.far_ref, ...), custom_call_target="tpu_custom_call" | custom-call | tf_op jit(solution)/shard_map/pallas_call | solution.py:331
  (13 shorter events, 0.1 us)
Async XLA Ops:
  1.6 7.8 %collective-permute-start = (bf16[4,2,128,128]{3,2,1,0:T(8,128)(2,1)S(1)}, bf16[4,2,128,128]{3,2,1,0:T(8,128)(2,1)S(1)}, u32[]{:S(2)}, u32[]{:S(2)}) collective-permute-start(bf16[4,2,128,128]{3,2,1,0:T(8,128)(2,1)S(1)} %dynamic-slice_bitcast_fusion), channel_id=1, source_target_pairs={{0,128},{128,0},{1,129},{129,1},{2,130},{130,2},{3,131},{131,3},{4... | collective-permute-start | bytes 786440 | tf_op jit(solution)/shard_map/ppermute | solution.py:369
  11.3 5.8 %collective-permute-start.1 = (f32[8,128]{1,0:T(8,128)S(1)}, f32[8,128]{1,0:T(8,128)S(1)}, u32[]{:S(2)}, u32[]{:S(2)}) collective-permute-start(f32[8,128]{1,0:T(8,128)S(1)} %get-tuple-element.15), channel_id=1, source_target_pairs={{0,128},{128,0},{1,129},{129,1},{2,130},{130,2},{3,131},{131,3},{4... | collective-permute-start | bytes 12296 | tf_op jit(solution)/shard_map/ppermute | solution.py:383
  12.1 6.8 %collective-permute-start.2 = (f32[24,128]{1,0:T(8,128)S(1)}, f32[24,128]{1,0:T(8,128)S(1)}, u32[]{:S(2)}, u32[]{:S(2)}) collective-permute-start(f32[24,128]{1,0:T(8,128)S(1)} %get-tuple-element.14), channel_id=1, source_target_pairs={{0,0},{1,2},{2,1},{3,4},{4,3},{5,6},{6,5},{7,8},{8,7},{9,10},{10,9... | collective-permute-start | bytes 36872 | tf_op jit(solution)/shard_map/ppermute | solution.py:384
  17.1 4.4 %collective-permute-start.3 = (f32[24,128]{1,0:T(8,128)S(1)}, f32[24,128]{1,0:T(8,128)S(1)}, u32[]{:S(2)}, u32[]{:S(2)}) collective-permute-start(f32[24,128]{1,0:T(8,128)S(1)} %pad_maximum_fusion), channel_id=1, source_target_pairs={{0,1},{1,0},{2,3},{3,2},{4,5},{5,4},{6,7},{7,6},{8,9},{9,8},{10,11... | collective-permute-start | bytes 36872 | tf_op jit(solution)/shard_map/ppermute | solution.py:386
  19.0 10.5 %copy-start = (bf16[96,384]{1,0:T(8,128)(2,1)S(1)}, bf16[96,384]{1,0:T(8,128)(2,1)}, u32[]{:S(2)}) copy-start(bf16[96,384]{1,0:T(8,128)(2,1)} %constant.46.clone.spread_ref) | copy-start | bytes 221188
  21.6 7.8 %collective-permute-start.4 = (f32[56,128]{1,0:T(8,128)S(1)}, f32[56,128]{1,0:T(8,128)S(1)}, u32[]{:S(2)}, u32[]{:S(2)}) collective-permute-start(f32[56,128]{1,0:T(8,128)S(1)} %get-tuple-element.18.to_far_ref), channel_id=1, source_target_pairs={{0,0},{16,32},{32,16},{48,64},{64,48},{80,96},{96,80},{112,112},{1... | collective-permute-start | bytes 86024 | tf_op jit(solution)/shard_map/ppermute | solution.py:394
  27.6 1.8 %collective-permute-start.5 = (f32[56,128]{1,0:T(8,128)S(1)}, f32[56,128]{1,0:T(8,128)S(1)}, u32[]{:S(2)}, u32[]{:S(2)}) collective-permute-start(f32[56,128]{1,0:T(8,128)S(1)} %get-tuple-element.19.to_near_ref), channel_id=1, source_target_pairs={{0,16},{16,0},{32,48},{48,32},{64,80},{80,64},{96,112},{112,96},{1... | collective-permute-start | bytes 86024 | tf_op jit(solution)/shard_map/ppermute | solution.py:395

commit v5 on v4

--- a/solution.py
+++ b/solution.py
@@ -163,7 +163,7 @@
 
 
 def far_columns_kernel(flags_ref, own_ref, nodes_ref, far_ref, out_ref):
-    flows, nodes = beside(own_ref[...], nodes_ref[...], far_ref[...] * flags_ref[2].astype(F32), flags_ref[1] == 1)
+    flows, nodes = beside(own_ref[...], nodes_ref[...], far_ref[...] * flags_ref[1].astype(F32), flags_ref[0] == 1)
     out_ref[0:8, :] = flows
     out_ref[8:, :] = nodes
 
@@ -171,7 +171,7 @@
 def local_kernel(flags_ref, table_hbm, patches_hbm, prior_hbm, start_hbm, weight_hbm, edges_hbm, nodes_hbm, share_hbm,
                  spec_ref, flows_ref, field_ref, far_edge_ref, near_edge_ref, table_ref, patches_ref, prior_ref, start_ref, weight_ref, edges_ref, nodes_ref, share_ref,
                  before, sums_y, sums_x, sems):
-    at_start, odd = flags_ref[0] == 0, flags_ref[1]
+    at_start, odd = flags_ref[0] == 0, 1 - flags_ref[0]
     pairs = [(table_hbm, table_ref), (patches_hbm, patches_ref), (prior_hbm, prior_ref), (start_hbm, start_ref),
              (weight_hbm, weight_ref), (edges_hbm, edges_ref), (nodes_hbm, nodes_ref), (share_hbm, share_ref)]
     copies = [pltpu.make_async_copy(source, target, sems.at[i]) for i, (source, target) in enumerate(pairs)]
@@ -216,17 +216,17 @@
 
 
 def middle_kernel(flags_ref, recv_ref, spec_ref, flows_ref, edge_ref, table_ref, out_ref, middle_ref, other, sums_y, sums_x):
-    gz, odd = flags_ref[0], flags_ref[1]
+    gz = flags_ref[0]
     forward = [table_ref[i] for i in range(3)]
     inverse = [table_ref[i] for i in range(3, 6)]
-    own = 3 * (1 - gz)
+    own = 2 * (1 - gz)
     for py in range(4):
         other[py] = spectrum(jnp.concatenate([recv_ref[py, 0], recv_ref[py, 1]], axis=1), *forward)
     for py in range(4):
         mine, theirs = spec_ref[own, py], other[py]
         prev, cur = jnp.where(gz == 0, mine, theirs), jnp.where(gz == 0, theirs, mine)
         sums_y[py], sums_x[py] = moments(prev, cur, *inverse)
-    flows = column_flows(sums_y, sums_x, 0, 0, 2 * (1 - gz ^ odd))
+    flows = column_flows(sums_y, sums_x, 0, 0, 2 * (1 - gz))
     middle_ref[...] = flows
     out_ref[0:8, :] = flows_ref[...] + jnp.where(gz == 0, 0.0, flows)
     out_ref[8:, :] = edge_ref[...]
@@ -236,12 +236,12 @@
     return pltpu.roll(values, by % values.shape[0], 0)
 
 
-def nodes_kernel(flags_ref, to_near_ref, to_far_ref, far_ref, near_ref, spread_ref, field_ref, out_ref):
-    odd, near_on_right = flags_ref[3] == 1, flags_ref[1] == 0
-    near, far = near_ref[...], far_ref[...]
-    above, below = jnp.where(odd, near, far), jnp.where(odd, far, near)
-    top = jnp.where(odd, to_near_ref[...], to_far_ref[...])
-    bottom = jnp.where(odd, to_far_ref[...], to_near_ref[...])
+def nodes_kernel(flags_ref, top_ref, bottom_ref, early_ref, late_ref, spread_ref, field_ref, out_ref):
+    near_on_right = flags_ref[0] == 0
+    upward = flags_ref[0] == 1
+    early, late = early_ref[...], late_ref[...]
+    above, below = jnp.where(upward, late, early), jnp.where(upward, early, late)
+    top, bottom = top_ref[...], bottom_ref[...]
     blocks = (above, top, bottom, below)
     flow_lane, lane = lax.broadcasted_iota(jnp.int32, (8, N), 1) % 8, group_lanes(8)
     flow_side = jnp.where(near_on_right, 6, 0)
@@ -343,29 +343,29 @@
     return jax.ShapeDtypeStruct(shape, F32)
 
 
-def near_partner(count):
-    return [(i, i ^ 1) for i in range(count)]
-
-
-def far_partner(count):
+def snake(count, forward):
     pairs = []
-    for i in range(count):
-        other = i + 1 if i % 2 else i - 1
-        pairs.append((i, other if 0 <= other < count else i))
+    for z in range(2):
+        for i in range(count):
+            to = i + 1 if (z == 0) == forward else i - 1
+            pairs.append((z * count + i, z * count + to if 0 <= to < count else (1 - z) * count + i))
     return pairs
 
 
 def body(patches, prior_patches, node_patch, node_weight, edges, flow_weight, start_offset):
     gz, gy, gx = (lax.axis_index(a) for a in ("gz", "gy", "gx"))
     rows, cols = lax.axis_size("gy"), lax.axis_size("gx")
-    odd, odd_row = gx % 2, gy % 2
-    has_far = (gx > 0) & (gx < cols - 1)
-    has_far_row = (gy > 0) & (gy < rows - 1)
-    flags = jnp.stack([gz, odd, has_far, odd_row]).astype(jnp.int32)
+    down = gz == 1
+
+    def heard(place, count):
+        return jnp.where(down, place < count - 1, place > 0), jnp.where(down, place > 0, place < count - 1)
+
+    early_col, late_col = heard(gx, cols)
+    early_row, late_row = (h.astype(F32) for h in heard(gy, rows))
+    flags = jnp.stack([gz, early_col]).astype(jnp.int32)
     table = jnp.asarray(tables())
 
-    first_col = 2 * (odd ^ gz)
-    chunk = lax.dynamic_slice(patches, (1 - gz, 0, first_col, 0, 0), (1, 4, 2, N, N))[0]
+    chunk = lax.dynamic_slice(patches, (1 - gz, 0, 2 * gz, 0, 0), (1, 4, 2, N, N))[0]
     received = lax.ppermute(chunk, "gz", [(0, 1), (1, 0)])
     sums = [pltpu.VMEM((16, 1, N), F32), pltpu.VMEM((16, 1, 2 * N), F32)]
     arrays = [patches, prior_patches, start_offset, flow_weight, edges, node_patch, node_weight]
@@ -381,20 +381,19 @@
         flops=2_000_000_000, moved=2_000_000,
     )
     own_middle = lax.ppermute(middle, "gz", [(0, 1), (1, 0)])
-    from_far = lax.ppermute(to_far, "gx", far_partner(cols))
+    from_far = lax.ppermute(to_far, ("gz", "gx"), snake(cols, True))
     own = to_far[:8] + own_middle * gz.astype(F32)
-    from_near = lax.ppermute(jnp.concatenate([own, near_edge]), "gx", near_partner(cols))
+    from_near = lax.ppermute(jnp.concatenate([own, near_edge]), ("gz", "gx"), snake(cols, False)) * late_col.astype(F32)
     partial = call(far_columns_kernel, [flags, own, nodes, from_far], f32(72, N), flops=5_000_000_000, moved=2_000_000)
 
     def rows_of(first):
         return jnp.concatenate([partial[:8], from_near[:8]] + [partial[8 + 16 * f + first :][:8] for f in range(4)] + [from_near[8 + first :][:8]])
 
     top, bottom = rows_of(0), rows_of(8)
-    to_near, to_far = jnp.where(odd_row == 1, top, bottom), jnp.where(odd_row == 1, bottom, top)
-    row_far = lax.ppermute(to_far, "gy", far_partner(rows)) * has_far_row.astype(F32)
-    row_near = lax.ppermute(to_near, "gy", near_partner(rows))
+    row_early = lax.ppermute(jnp.where(down, top, bottom), ("gz", "gy"), snake(rows, True)) * early_row
+    row_late = lax.ppermute(jnp.where(down, bottom, top), ("gz", "gy"), snake(rows, False)) * late_row
     flow_field, displacement = call(
-        nodes_kernel, [flags, to_near, to_far, row_far, row_near, jnp.asarray(spread_table())],
+        nodes_kernel, [flags, top, bottom, row_early, row_late, jnp.asarray(spread_table())],
         [f32(2, 2, 4, 4), f32(2, 2, 16, 16)])
     return flow_field, displacement
 

time: 31.4 us -> 30.2 us (0.962)
  the two profiles are of different devices: /device:TPU:195 before, /device:TPU:128 now
where the time goes in v5:
time: 30.2 us; the launch traced here: 30 us
  starting transfers between devices  11.9 us (39%)
  Pallas kernels  10.6 us (35%)
  waiting for transfers between devices  5.75 us (19%)
  local copies, waits for them, and re-layouts  1.02 us (3%)
  between operations  0.73 us (2%)
    pallas_call x4, Pallas kernels, call(): pl.pallas_call(kernel, out_shape=out_shapes, in_specs=[pl.BlockSpec(memor...  10.6 us
    ppermute x1, starting transfers between devices, body(): from_far = lax.ppermute(to_far, ('gz', 'gx'), snake(cols, True))  2.9 us
    ppermute x1, starting transfers between devices, body(): lax.ppermute(jnp.where(down, bottom, top), ('gz', 'gy'), snake(rows, False))  2.82 us
    ppermute x1, starting transfers between devices, body(): lax.ppermute(jnp.concatenate([own, near_edge]), ('gz', 'gx'), snake(cols,...  2.81 us
    ppermute x1, waiting for transfers between devices, body(): lax.ppermute(jnp.where(down, top, bottom), ('gz', 'gy'), snake(rows, True))  2.31 us
    ppermute x1, starting transfers between devices, body(): received = lax.ppermute(chunk, 'gz', [(0, 1), (1, 0)])  1.66 us
    ppermute x1, starting transfers between devices, body(): own_middle = lax.ppermute(middle, 'gz', [(0, 1), (1, 0)])  1.66 us
    ppermute x1, waiting for transfers between devices, body(): from_far = lax.ppermute(to_far, ('gz', 'gx'), snake(cols, True))  1.58 us
  transfers between devices with their start and end apart: 6, of which 5 were waited for; matrix products, arithmetic and copies ran while one was open for 0% of the time, Pallas kernels for 23%

profile of v5, /device:TPU:128, one launch (start us, length us, event | category | flops | bytes accessed | tf_op | source)
XLA Modules:
  0.0 30.0 jit_solution(15285092118347527575)
XLA Ops:
  0.6 1.0 %dynamic-slice_bitcast_fusion = bf16[4,2,128,128]{3,2,1,0:T(8,128)(2,1)S(1)} fusion(bf16[2,4,4,128,128]{4,3,2,1,0:T(8,128)(2,1)} %patches_hbm.1, s32[]{:T(128)S(6)} %select_n.32, s32[]{:T(128)S(6)} %select_n.33), kind=kLoop, calls=%fused_computation | loop fusion | bytes 524296 | tf_op jit(solution)/shard_map/squeeze | solution.py:368
  1.6 1.7 %collective-permute-start = (bf16[4,2,128,128]{3,2,1,0:T(8,128)(2,1)S(1)}, bf16[4,2,128,128]{3,2,1,0:T(8,128)(2,1)S(1)}, u32[]{:S(2)}, u32[]{:S(2)}) collective-permute-start(bf16[4,2,128,128]{3,2,1,0:T(8,128)(2,1)S(1)} %dynamic-slice_bitcast_fusion), channel_id=1, source_target_pairs={{0,128},{128,0},{1,129},{129,1},{2,130},{130,2},{3,131},{131,3},{4... | collective-permute-start | bytes 786440 | tf_op jit(solution)/shard_map/ppermute | solution.py:369
  3.3 0.1 pad_add_fusion.flags_ref
  3.4 6.3 %shard_map.104 = (f32[4,4,128,256]{3,2,1,0:T(8,128)S(1)}, f32[8,128]{1,0:T(8,128)S(1)}, f32[64,128]{1,0:T(8,128)S(1)}, f32[16,128]{1,0:T(8,128)S(1)}, f32[16,128...) custom-call(s32[2]{0:T(128)S(1)} %pad_add_fusion.flags_ref, bf16[6,256,256]{2,1,0:T(8,128)(2,1)} %constant.32.clone.table_hbm, ...), custom_call_target="tpu_custom_call" | custom-call | flops 8000000000 | bytes 4000000 | tf_op jit(solution)/shard_map/pallas_call | solution.py:331
  9.7 0.1 collective-permute-done.recv_ref
  9.8 1.8 %shard_map.105 = (f32[24,128]{1,0:T(8,128)S(1)}, f32[8,128]{1,0:T(8,128)S(1)}) custom-call(s32[2]{0:T(128)S(1)} %pad_add_fusion.flags_ref, bf16[4,2,128,128]{3,2,1,0:T(8,128)(2,1)S(1)} %collective-permute-done.recv_ref, f32[4,4,128,256]{3,2,1,0:T(8,128)S(1)} %get-tuple-element.10.spec_ref, f32[8,128]{1,0:T(8,128)S(1)} %get-tuple-element.11.flows_ref, ...), custom_call_target="tpu_custom_call" | custom-call | flops 2000000000 | bytes 2000000 | tf_op jit(solution)/shard_map/pallas_call | solution.py:331
  11.6 1.7 %collective-permute-start.1 = (f32[8,128]{1,0:T(8,128)S(1)}, f32[8,128]{1,0:T(8,128)S(1)}, u32[]{:S(2)}, u32[]{:S(2)}) collective-permute-start(f32[8,128]{1,0:T(8,128)S(1)} %get-tuple-element.15), channel_id=1, source_target_pairs={{0,128},{128,0},{1,129},{129,1},{2,130},{130,2},{3,131},{131,3},{4... | collective-permute-start | bytes 12296 | tf_op jit(solution)/shard_map/ppermute | solution.py:383
  13.3 2.9 %collective-permute-start.2 = (f32[24,128]{1,0:T(8,128)S(1)}, f32[24,128]{1,0:T(8,128)S(1)}, u32[]{:S(2)}, u32[]{:S(2)}) collective-permute-start(f32[24,128]{1,0:T(8,128)S(1)} %get-tuple-element.14), channel_id=1, source_target_pairs={{0,1},{1,2},{2,3},{3,4},{4,5},{5,6},{6,7},{7,8},{8,9},{9,10},{10,1... | collective-permute-start | bytes 36872 | tf_op jit(solution)/shard_map/ppermute | solution.py:384
  16.2 0.0 collective-permute-done.1
  16.2 2.8 %collective-permute-start.3 = (f32[24,128]{1,0:T(8,128)S(1)}, f32[24,128]{1,0:T(8,128)S(1)}, u32[]{:S(2)}, u32[]{:S(2)}) collective-permute-start(f32[24,128]{1,0:T(8,128)S(1)} %pad_maximum_fusion), channel_id=1, source_target_pairs={{0,128},{1,0},{2,1},{3,2},{4,3},{5,4},{6,5},{7,6},{8,7},{9,8},{10,... | collective-permute-start | bytes 36872 | tf_op jit(solution)/shard_map/ppermute | solution.py:386
  19.0 1.6 %collective-permute-done.2.far_ref = f32[24,128]{1,0:T(8,128)S(1)} collective-permute-done((f32[24,128]{1,0:T(8,128)S(1)}, f32[24,128]{1,0:T(8,128)S(1)}, u32[]{:S(2)}, u32[]{:S(2)}) %collective-permute-start.2) | collective-permute-done | bytes 12320 | tf_op jit(solution)/shard_map/ppermute | solution.py:384
  20.6 0.0 copy-start
  20.6 0.6 %shard_map.106 = f32[72,128]{1,0:T(8,128)S(1)} custom-call(s32[2]{0:T(128)S(1)} %pad_add_fusion.flags_ref, f32[8,128]{1,0:T(8,128)S(1)} %multiply_add_fusion.own_ref, f32[64,128]{1,0:T(8,128)S(1)} %get-tuple-element.16.nodes_ref, f32[24,128]{1,0:T(8,128)S(1)} %collective-permute-done.2.far_ref), custom_call_target="tpu_custom_call" | custom-call | flops 5000000000 | bytes 2000000 | tf_op jit(solution)/shard_map/pallas_call | solution.py:331
  21.2 0.2 collective-permute-done.3
  21.6 2.8 %collective-permute-start.5 = (f32[56,128]{1,0:T(8,128)S(1)}, f32[56,128]{1,0:T(8,128)S(1)}, u32[]{:S(2)}, u32[]{:S(2)}) collective-permute-start(f32[56,128]{1,0:T(8,128)S(1)} %get-tuple-element.18), channel_id=1, source_target_pairs={{0,128},{16,0},{32,16},{48,32},{64,48},{80,64},{96,80},{112,96},{1... | collective-permute-start | bytes 86024 | tf_op jit(solution)/shard_map/ppermute | solution.py:394
  24.4 0.0 collective-permute-start.4
  24.4 1.6 %collective-permute-done.5 = f32[56,128]{1,0:T(8,128)S(1)} collective-permute-done((f32[56,128]{1,0:T(8,128)S(1)}, f32[56,128]{1,0:T(8,128)S(1)}, u32[]{:S(2)}, u32[]{:S(2)}) %collective-permute-start.5) | collective-permute-done | bytes 28704 | tf_op jit(solution)/shard_map/ppermute | solution.py:394
  25.9 2.3 %collective-permute-done.4 = f32[56,128]{1,0:T(8,128)S(1)} collective-permute-done((f32[56,128]{1,0:T(8,128)S(1)}, f32[56,128]{1,0:T(8,128)S(1)}, u32[]{:S(2)}, u32[]{:S(2)}) %collective-permute-start.4) | collective-permute-done | bytes 28704 | tf_op jit(solution)/shard_map/ppermute | solution.py:393
  28.3 0.0 copy-done
  28.3 1.8 %shard_map.107 = (f32[2,2,4,4]{3,2,1,0:T(4,128)}, f32[2,2,16,16]{3,2,1,0:T(8,128)}) custom-call(s32[2]{0:T(128)S(1)} %pad_add_fusion.flags_ref, f32[56,128]{1,0:T(8,128)S(1)} %get-tuple-element.27.top_ref, f32[56,128]{1,0:T(8,128)S(1)} %get-tuple-element.26.bottom_ref, f32[56,128]{1,0:T(8,128)S(1)} %broadcast_multiply_fusion.1.early_ref, ...), custom_call_target="tpu_custom_call" | custom-call | tf_op jit(solution)/shard_map/pallas_call | solution.py:331
  (15 shorter events, 0.1 us)
Async XLA Ops:
  1.6 8.1 %collective-permute-start = (bf16[4,2,128,128]{3,2,1,0:T(8,128)(2,1)S(1)}, bf16[4,2,128,128]{3,2,1,0:T(8,128)(2,1)S(1)}, u32[]{:S(2)}, u32[]{:S(2)}) collective-permute-start(bf16[4,2,128,128]{3,2,1,0:T(8,128)(2,1)S(1)} %dynamic-slice_bitcast_fusion), channel_id=1, source_target_pairs={{0,128},{128,0},{1,129},{129,1},{2,130},{130,2},{3,131},{131,3},{4... | collective-permute-start | bytes 786440 | tf_op jit(solution)/shard_map/ppermute | solution.py:369
  11.6 4.6 %collective-permute-start.1 = (f32[8,128]{1,0:T(8,128)S(1)}, f32[8,128]{1,0:T(8,128)S(1)}, u32[]{:S(2)}, u32[]{:S(2)}) collective-permute-start(f32[8,128]{1,0:T(8,128)S(1)} %get-tuple-element.15), channel_id=1, source_target_pairs={{0,128},{128,0},{1,129},{129,1},{2,130},{130,2},{3,131},{131,3},{4... | collective-permute-start | bytes 12296 | tf_op jit(solution)/shard_map/ppermute | solution.py:383
  13.3 7.3 %collective-permute-start.2 = (f32[24,128]{1,0:T(8,128)S(1)}, f32[24,128]{1,0:T(8,128)S(1)}, u32[]{:S(2)}, u32[]{:S(2)}) collective-permute-start(f32[24,128]{1,0:T(8,128)S(1)} %get-tuple-element.14), channel_id=1, source_target_pairs={{0,1},{1,2},{2,3},{3,4},{4,5},{5,6},{6,7},{7,8},{8,9},{9,10},{10,1... | collective-permute-start | bytes 36872 | tf_op jit(solution)/shard_map/ppermute | solution.py:384
  16.2 5.3 %collective-permute-start.3 = (f32[24,128]{1,0:T(8,128)S(1)}, f32[24,128]{1,0:T(8,128)S(1)}, u32[]{:S(2)}, u32[]{:S(2)}) collective-permute-start(f32[24,128]{1,0:T(8,128)S(1)} %pad_maximum_fusion), channel_id=1, source_target_pairs={{0,128},{1,0},{2,1},{3,2},{4,3},{5,4},{6,5},{7,6},{8,7},{9,8},{10,... | collective-permute-start | bytes 36872 | tf_op jit(solution)/shard_map/ppermute | solution.py:386
  20.6 7.7 %copy-start = (bf16[96,384]{1,0:T(8,128)(2,1)S(1)}, bf16[96,384]{1,0:T(8,128)(2,1)}, u32[]{:S(2)}) copy-start(bf16[96,384]{1,0:T(8,128)(2,1)} %constant.33.clone.spread_ref) | copy-start | bytes 221188
  21.6 4.4 %collective-permute-start.5 = (f32[56,128]{1,0:T(8,128)S(1)}, f32[56,128]{1,0:T(8,128)S(1)}, u32[]{:S(2)}, u32[]{:S(2)}) collective-permute-start(f32[56,128]{1,0:T(8,128)S(1)} %get-tuple-element.18), channel_id=1, source_target_pairs={{0,128},{16,0},{32,16},{48,32},{64,48},{80,64},{96,80},{112,96},{1... | collective-permute-start | bytes 86024 | tf_op jit(solution)/shard_map/ppermute | solution.py:394
  24.4 3.9 %collective-permute-start.4 = (f32[56,128]{1,0:T(8,128)S(1)}, f32[56,128]{1,0:T(8,128)S(1)}, u32[]{:S(2)}, u32[]{:S(2)}) collective-permute-start(f32[56,128]{1,0:T(8,128)S(1)} %get-tuple-element.19), channel_id=1, source_target_pairs={{0,16},{16,32},{32,48},{48,64},{64,80},{80,96},{96,112},{112,240},... | collective-permute-start | bytes 86024 | tf_op jit(solution)/shard_map/ppermute | solution.py:393

commit v6 on v5

--- a/solution.py
+++ b/solution.py
@@ -18,6 +18,7 @@
 BF16 = jnp.bfloat16
 GROUP = 32
 EDGE = 3
+MOMENT_ROWS = 80
 VMEM_LIMIT = 24 * 1024 * 1024
 
 
@@ -44,12 +45,16 @@
     back[0:H, :N], back[N : N + H, :N] = basis[:H], basis[H:]
     back[H:N, N:], back[N + H :, N:] = basis[:H], basis[H:]
     offset = ((pixel + H) % N - H).astype(np.float64)
-    moment = (basis * offset[None, :]) @ basis.T
-    stacked = []
-    for left in (root, moment):
-        high, low = split_const(left)
-        stacked.append(np.block([[high, high], [low, low]]))
-    return np.stack([*split_const(wide), stacked[0], stacked[1], *split_const(back)])
+    offset[H] = 0.0
+    odd = np.zeros((MOMENT_ROWS, H))
+    odd[: H + 1] = 2.0 * ((basis * offset[None, :]) @ basis.T)[: H + 1, H:]
+    odd[H, 0] = 0.0
+    high, low = split_const(root)
+    rows = np.block([[high, high], [low, low]])
+    high, low = split_const(odd)
+    moment = np.zeros((2 * N, 2 * N), ml_dtypes.bfloat16)
+    moment[: 2 * MOMENT_ROWS, :N] = np.block([[high, high], [low, low]])
+    return np.stack([*split_const(wide), rows, moment, *split_const(back)])
 
 
 def dot(left, right):
@@ -61,14 +66,10 @@
     return high, (values - high.astype(F32)).astype(BF16)
 
 
-def left_product(stacked, values):
-    high, low = halves(values)
-    both = dot(stacked, jnp.concatenate([high, low], axis=0))
+def spectrum(pixels, wide_high, wide_low, rows):
+    high, low = halves(dot(pixels, wide_high) + dot(pixels, wide_low))
+    both = dot(rows, jnp.concatenate([high, low], axis=0))
     return both[:N] + both[N:]
-
-
-def spectrum(pixels, wide_high, wide_low, rows):
-    return left_product(rows, dot(pixels, wide_high) + dot(pixels, wide_low))
 
 
 def cross(prev, cur):
@@ -104,9 +105,14 @@
 
 def moments(prev, cur, moment, back_high, back_low):
     values = cross(prev, cur)
-    along_y = jnp.sum(values * left_product(moment, values), axis=0, keepdims=True)
+    high, low = halves(values)
+    both = dot(moment[: 2 * MOMENT_ROWS, :N], jnp.concatenate([high[H:], low[H:]], axis=0))
+    both = both[:MOMENT_ROWS] + both[MOMENT_ROWS:]
+    row = lax.broadcasted_iota(jnp.int32, (H, 2 * N), 0)
+    sign = jnp.where(row == 0, math.sqrt(1.0 / N), math.sqrt(2.0 / N) * (1 - 2 * (row % 2)).astype(F32))
+    halfway = jnp.sum(values[:H] * sign, axis=0, keepdims=True) + math.sqrt(1.0 / N) * values[H : H + 1]
+    along_y = jnp.sum(values[:H] * both[:H], axis=0, keepdims=True) + values[H : H + 1] * both[H : H + 1] - H * halfway * halfway
     along_y = along_y[:, :N] + along_y[:, N:]
-    high, low = halves(values)
     pixels = dot(high, back_high) + dot(low, back_high) + dot(high, back_low)
     return along_y, jnp.sum(pixels * pixels, axis=0, keepdims=True)
 
@@ -172,8 +178,11 @@
                  spec_ref, flows_ref, field_ref, far_edge_ref, near_edge_ref, table_ref, patches_ref, prior_ref, start_ref, weight_ref, edges_ref, nodes_ref, share_ref,
                  before, sums_y, sums_x, sems):
     at_start, odd = flags_ref[0] == 0, 1 - flags_ref[0]
-    pairs = [(table_hbm, table_ref), (patches_hbm, patches_ref), (prior_hbm, prior_ref), (start_hbm, start_ref),
-             (weight_hbm, weight_ref), (edges_hbm, edges_ref), (nodes_hbm, nodes_ref), (share_hbm, share_ref)]
+    def piece(source, target, *at):
+        return source.at[at], target.at[at]
+
+    pairs = [piece(table_hbm, table_ref, pl.ds(0, 3)), piece(patches_hbm, patches_ref, 0), piece(patches_hbm, patches_ref, 1), (prior_hbm, prior_ref), piece(table_hbm, table_ref, pl.ds(3, 3)),
+             (start_hbm, start_ref), (weight_hbm, weight_ref), (edges_hbm, edges_ref), (nodes_hbm, nodes_ref), (share_hbm, share_ref)]
     copies = [pltpu.make_async_copy(source, target, sems.at[i]) for i, (source, target) in enumerate(pairs)]
     for copy in copies:
         copy.start()
@@ -181,17 +190,18 @@
     for copy in copies[:2]:
         copy.wait()
     forward = [table_ref[i] for i in range(3)]
-    inverse = [table_ref[i] for i in range(3, 6)]
     units = [(half, py) for half in range(2) for py in range(4)]
 
     def pixels(ref, index, first):
         return jnp.concatenate([ref[(*index, first)], ref[(*index, first + 1)]], axis=1)
 
-    for half, py in units:
-        for section in range(2):
+    for section in range(2):
+        for half, py in units:
             spec_ref[2 * section + half, py] = spectrum(pixels(patches_ref, (section, py), 2 * (half ^ odd)), *forward)
-    for copy in copies[2:]:
-        copy.wait()
+        if section == 0:
+            for copy in copies[2:]:
+                copy.wait()
+    inverse = [table_ref[i] for i in range(3, 6)]
     for unit, (half, py) in enumerate(units):
         before[unit] = spectrum(pixels(prior_ref, (py,), 2 * (half ^ odd)), *forward)
     for unit, (half, py) in enumerate(units):
@@ -301,10 +311,13 @@
     down = over_groups(jnp.where(group == 3, mixed, 0.0))
     left = pltpu.roll(right, 1, 1)
     up = shifted_rows(down, 1)
+    stay = 1.0 - STEP_SIZE * (stiffness + (right + left) + (down + up))
+    pull = STEP_SIZE * stiffness * target
+    right, left, down, up = (STEP_SIZE * spring for spring in (right, left, down, up))
     for _ in range(STEPS):
-        springs = right * (pltpu.roll(moved, N - 1, 1) - moved) + left * (pltpu.roll(moved, 1, 1) - moved)
-        springs = springs + down * (shifted_rows(moved, -1) - moved) + up * (shifted_rows(moved, 1) - moved)
-        moved = moved + STEP_SIZE * (stiffness * (target - moved) + springs)
+        across = right * pltpu.roll(moved, N - 1, 1) + left * pltpu.roll(moved, 1, 1)
+        along = down * shifted_rows(moved, -1) + up * shifted_rows(moved, 1)
+        moved = (stay * moved + pull) + (across + along)
     for s in range(2):
         for c in range(2):
             lane = s * 16 + c * 8 + 2
@@ -372,7 +385,7 @@
     spec, flows, nodes, far_edge, near_edge, table = call(
         local_kernel, [flags],
         [f32(4, 4, N, 2 * N), f32(8, N), f32(64, N), f32(16, N), f32(16, N), jax.ShapeDtypeStruct(table.shape, table.dtype)],
-        [*(pltpu.VMEM(a.shape, a.dtype) for a in arrays), pltpu.VMEM((8, N, 2 * N), F32), *sums, pltpu.SemaphoreType.DMA((8,))],
+        [*(pltpu.VMEM(a.shape, a.dtype) for a in arrays), pltpu.VMEM((8, N, 2 * N), F32), *sums, pltpu.SemaphoreType.DMA((10,))],
         flops=8_000_000_000, moved=4_000_000, from_hbm=[table, *arrays],
     )
     to_far, middle = call(

time: 30.2 us -> 29.9 us (0.990)
  Pallas kernels: 10.6 us -> 9.56 us
  waiting for transfers between devices: 5.75 us -> 6.51 us
    pallas_call x4, Pallas kernels: 10.6 us -> 9.56 us  [call(): pl.pallas_call(kernel, out_shape=out_shapes, in_specs=[pl.BlockSpec(memor...]
    ppermute x1, waiting for transfers between devices: 0.07 us -> 0.83 us  [body(): received = lax.ppermute(chunk, 'gz', [(0, 1), (1, 0)])]
  transfers between devices with their start and end apart: 6 -> 6, of which waited for: 5 -> 5; matrix products, arithmetic and copies ran while one was open for 0% -> 0% of each run, Pallas kernels for 23% -> 21%
where the time goes in v6:
time: 29.9 us; the launch traced here: 29.8 us
  starting transfers between devices  11.9 us (40%)
  Pallas kernels  9.56 us (32%)
  waiting for transfers between devices  6.51 us (22%)
  local copies, waits for them, and re-layouts  1.02 us (3%)
  between operations  0.73 us (2%)
    pallas_call x4, Pallas kernels, call(): pl.pallas_call(kernel, out_shape=out_shapes, in_specs=[pl.BlockSpec(memor...  9.56 us
    ppermute x1, starting transfers between devices, body(): from_far = lax.ppermute(to_far, ('gz', 'gx'), snake(cols, True))  2.9 us
    ppermute x1, starting transfers between devices, body(): lax.ppermute(jnp.where(down, bottom, top), ('gz', 'gy'), snake(rows, False))  2.82 us
    ppermute x1, starting transfers between devices, body(): lax.ppermute(jnp.concatenate([own, near_edge]), ('gz', 'gx'), snake(cols,...  2.81 us
    ppermute x1, waiting for transfers between devices, body(): lax.ppermute(jnp.where(down, top, bottom), ('gz', 'gy'), snake(rows, True))  2.31 us
    ppermute x1, starting transfers between devices, body(): own_middle = lax.ppermute(middle, 'gz', [(0, 1), (1, 0)])  1.66 us
    ppermute x1, starting transfers between devices, body(): received = lax.ppermute(chunk, 'gz', [(0, 1), (1, 0)])  1.66 us
    ppermute x1, waiting for transfers between devices, body(): from_far = lax.ppermute(to_far, ('gz', 'gx'), snake(cols, True))  1.58 us
  transfers between devices with their start and end apart: 6, of which 5 were waited for; matrix products, arithmetic and copies ran while one was open for 0% of the time, Pallas kernels for 21%

profile of v6, /device:TPU:128, one launch (start us, length us, event | category | flops | bytes accessed | tf_op | source)
XLA Modules:
  0.0 29.8 jit_solution(6260206943865956315)
XLA Ops:
  0.6 1.0 %dynamic-slice_bitcast_fusion = bf16[4,2,128,128]{3,2,1,0:T(8,128)(2,1)S(1)} fusion(bf16[2,4,4,128,128]{4,3,2,1,0:T(8,128)(2,1)} %patches_hbm.1, s32[]{:T(128)S(6)} %select_n.32, s32[]{:T(128)S(6)} %select_n.33), kind=kLoop, calls=%fused_computation | loop fusion | bytes 524296 | tf_op jit(solution)/shard_map/squeeze | solution.py:381
  1.6 1.7 %collective-permute-start = (bf16[4,2,128,128]{3,2,1,0:T(8,128)(2,1)S(1)}, bf16[4,2,128,128]{3,2,1,0:T(8,128)(2,1)S(1)}, u32[]{:S(2)}, u32[]{:S(2)}) collective-permute-start(bf16[4,2,128,128]{3,2,1,0:T(8,128)(2,1)S(1)} %dynamic-slice_bitcast_fusion), channel_id=1, source_target_pairs={{0,128},{128,0},{1,129},{129,1},{2,130},{130,2},{3,131},{131,3},{4... | collective-permute-start | bytes 786440 | tf_op jit(solution)/shard_map/ppermute | solution.py:382
  3.3 0.1 pad_add_fusion.flags_ref
  3.4 5.6 %shard_map.104 = (f32[4,4,128,256]{3,2,1,0:T(8,128)S(1)}, f32[8,128]{1,0:T(8,128)S(1)}, f32[64,128]{1,0:T(8,128)S(1)}, f32[16,128]{1,0:T(8,128)S(1)}, f32[16,128...) custom-call(s32[2]{0:T(128)S(1)} %pad_add_fusion.flags_ref, bf16[6,256,256]{2,1,0:T(8,128)(2,1)} %constant.32.clone.table_hbm, ...), custom_call_target="tpu_custom_call" | custom-call | flops 8000000000 | bytes 4000000 | tf_op jit(solution)/shard_map/pallas_call | solution.py:344
  8.9 0.8 %collective-permute-done.recv_ref = bf16[4,2,128,128]{3,2,1,0:T(8,128)(2,1)S(1)} collective-permute-done((bf16[4,2,128,128]{3,2,1,0:T(8,128)(2,1)S(1)}, bf16[4,2,128,128]{3,2,1,0:T(8,128)(2,1)S(1)}, u32[]{:S(2)}, u32[]{:S(2)}) %collective-permute-start) | collective-permute-done | bytes 262176 | tf_op jit(solution)/shard_map/ppermute | solution.py:382
  9.8 1.6 %shard_map.105 = (f32[24,128]{1,0:T(8,128)S(1)}, f32[8,128]{1,0:T(8,128)S(1)}) custom-call(s32[2]{0:T(128)S(1)} %pad_add_fusion.flags_ref, bf16[4,2,128,128]{3,2,1,0:T(8,128)(2,1)S(1)} %collective-permute-done.recv_ref, f32[4,4,128,256]{3,2,1,0:T(8,128)S(1)} %get-tuple-element.10.spec_ref, f32[8,128]{1,0:T(8,128)S(1)} %get-tuple-element.11.flows_ref, ...), custom_call_target="tpu_custom_call" | custom-call | flops 2000000000 | bytes 2000000 | tf_op jit(solution)/shard_map/pallas_call | solution.py:344
  11.4 1.7 %collective-permute-start.1 = (f32[8,128]{1,0:T(8,128)S(1)}, f32[8,128]{1,0:T(8,128)S(1)}, u32[]{:S(2)}, u32[]{:S(2)}) collective-permute-start(f32[8,128]{1,0:T(8,128)S(1)} %get-tuple-element.15), channel_id=1, source_target_pairs={{0,128},{128,0},{1,129},{129,1},{2,130},{130,2},{3,131},{131,3},{4... | collective-permute-start | bytes 12296 | tf_op jit(solution)/shard_map/ppermute | solution.py:396
  13.0 2.9 %collective-permute-start.2 = (f32[24,128]{1,0:T(8,128)S(1)}, f32[24,128]{1,0:T(8,128)S(1)}, u32[]{:S(2)}, u32[]{:S(2)}) collective-permute-start(f32[24,128]{1,0:T(8,128)S(1)} %get-tuple-element.14), channel_id=1, source_target_pairs={{0,1},{1,2},{2,3},{3,4},{4,5},{5,6},{6,7},{7,8},{8,9},{9,10},{10,1... | collective-permute-start | bytes 36872 | tf_op jit(solution)/shard_map/ppermute | solution.py:397
  15.9 0.0 collective-permute-done.1
  15.9 2.8 %collective-permute-start.3 = (f32[24,128]{1,0:T(8,128)S(1)}, f32[24,128]{1,0:T(8,128)S(1)}, u32[]{:S(2)}, u32[]{:S(2)}) collective-permute-start(f32[24,128]{1,0:T(8,128)S(1)} %pad_maximum_fusion), channel_id=1, source_target_pairs={{0,128},{1,0},{2,1},{3,2},{4,3},{5,4},{6,5},{7,6},{8,7},{9,8},{10,... | collective-permute-start | bytes 36872 | tf_op jit(solution)/shard_map/ppermute | solution.py:399
  18.7 1.6 %collective-permute-done.2.far_ref = f32[24,128]{1,0:T(8,128)S(1)} collective-permute-done((f32[24,128]{1,0:T(8,128)S(1)}, f32[24,128]{1,0:T(8,128)S(1)}, u32[]{:S(2)}, u32[]{:S(2)}) %collective-permute-start.2) | collective-permute-done | bytes 12320 | tf_op jit(solution)/shard_map/ppermute | solution.py:397
  20.3 0.0 copy-start
  20.3 0.6 %shard_map.106 = f32[72,128]{1,0:T(8,128)S(1)} custom-call(s32[2]{0:T(128)S(1)} %pad_add_fusion.flags_ref, f32[8,128]{1,0:T(8,128)S(1)} %multiply_add_fusion.own_ref, f32[64,128]{1,0:T(8,128)S(1)} %get-tuple-element.16.nodes_ref, f32[24,128]{1,0:T(8,128)S(1)} %collective-permute-done.2.far_ref), custom_call_target="tpu_custom_call" | custom-call | flops 5000000000 | bytes 2000000 | tf_op jit(solution)/shard_map/pallas_call | solution.py:344
  21.0 0.2 collective-permute-done.3
  21.3 2.8 %collective-permute-start.5 = (f32[56,128]{1,0:T(8,128)S(1)}, f32[56,128]{1,0:T(8,128)S(1)}, u32[]{:S(2)}, u32[]{:S(2)}) collective-permute-start(f32[56,128]{1,0:T(8,128)S(1)} %get-tuple-element.18), channel_id=1, source_target_pairs={{0,128},{16,0},{32,16},{48,32},{64,48},{80,64},{96,80},{112,96},{1... | collective-permute-start | bytes 86024 | tf_op jit(solution)/shard_map/ppermute | solution.py:407
  24.1 0.0 collective-permute-start.4
  24.1 1.6 %collective-permute-done.5 = f32[56,128]{1,0:T(8,128)S(1)} collective-permute-done((f32[56,128]{1,0:T(8,128)S(1)}, f32[56,128]{1,0:T(8,128)S(1)}, u32[]{:S(2)}, u32[]{:S(2)}) %collective-permute-start.5) | collective-permute-done | bytes 28704 | tf_op jit(solution)/shard_map/ppermute | solution.py:407
  25.7 2.3 %collective-permute-done.4 = f32[56,128]{1,0:T(8,128)S(1)} collective-permute-done((f32[56,128]{1,0:T(8,128)S(1)}, f32[56,128]{1,0:T(8,128)S(1)}, u32[]{:S(2)}, u32[]{:S(2)}) %collective-permute-start.4) | collective-permute-done | bytes 28704 | tf_op jit(solution)/shard_map/ppermute | solution.py:406
  28.0 0.0 copy-done
  28.0 1.8 %shard_map.107 = (f32[2,2,4,4]{3,2,1,0:T(4,128)}, f32[2,2,16,16]{3,2,1,0:T(8,128)}) custom-call(s32[2]{0:T(128)S(1)} %pad_add_fusion.flags_ref, f32[56,128]{1,0:T(8,128)S(1)} %get-tuple-element.27.top_ref, f32[56,128]{1,0:T(8,128)S(1)} %get-tuple-element.26.bottom_ref, f32[56,128]{1,0:T(8,128)S(1)} %broadcast_multiply_fusion.1.early_ref, ...), custom_call_target="tpu_custom_call" | custom-call | tf_op jit(solution)/shard_map/pallas_call | solution.py:344
  (15 shorter events, 0.1 us)
Async XLA Ops:
  1.6 8.1 %collective-permute-start = (bf16[4,2,128,128]{3,2,1,0:T(8,128)(2,1)S(1)}, bf16[4,2,128,128]{3,2,1,0:T(8,128)(2,1)S(1)}, u32[]{:S(2)}, u32[]{:S(2)}) collective-permute-start(bf16[4,2,128,128]{3,2,1,0:T(8,128)(2,1)S(1)} %dynamic-slice_bitcast_fusion), channel_id=1, source_target_pairs={{0,128},{128,0},{1,129},{129,1},{2,130},{130,2},{3,131},{131,3},{4... | collective-permute-start | bytes 786440 | tf_op jit(solution)/shard_map/ppermute | solution.py:382
  11.4 4.6 %collective-permute-start.1 = (f32[8,128]{1,0:T(8,128)S(1)}, f32[8,128]{1,0:T(8,128)S(1)}, u32[]{:S(2)}, u32[]{:S(2)}) collective-permute-start(f32[8,128]{1,0:T(8,128)S(1)} %get-tuple-element.15), channel_id=1, source_target_pairs={{0,128},{128,0},{1,129},{129,1},{2,130},{130,2},{3,131},{131,3},{4... | collective-permute-start | bytes 12296 | tf_op jit(solution)/shard_map/ppermute | solution.py:396
  13.0 7.3 %collective-permute-start.2 = (f32[24,128]{1,0:T(8,128)S(1)}, f32[24,128]{1,0:T(8,128)S(1)}, u32[]{:S(2)}, u32[]{:S(2)}) collective-permute-start(f32[24,128]{1,0:T(8,128)S(1)} %get-tuple-element.14), channel_id=1, source_target_pairs={{0,1},{1,2},{2,3},{3,4},{4,5},{5,6},{6,7},{7,8},{8,9},{9,10},{10,1... | collective-permute-start | bytes 36872 | tf_op jit(solution)/shard_map/ppermute | solution.py:397
  15.9 5.3 %collective-permute-start.3 = (f32[24,128]{1,0:T(8,128)S(1)}, f32[24,128]{1,0:T(8,128)S(1)}, u32[]{:S(2)}, u32[]{:S(2)}) collective-permute-start(f32[24,128]{1,0:T(8,128)S(1)} %pad_maximum_fusion), channel_id=1, source_target_pairs={{0,128},{1,0},{2,1},{3,2},{4,3},{5,4},{6,5},{7,6},{8,7},{9,8},{10,... | collective-permute-start | bytes 36872 | tf_op jit(solution)/shard_map/ppermute | solution.py:399
  20.3 7.7 %copy-start = (bf16[96,384]{1,0:T(8,128)(2,1)S(1)}, bf16[96,384]{1,0:T(8,128)(2,1)}, u32[]{:S(2)}) copy-start(bf16[96,384]{1,0:T(8,128)(2,1)} %constant.33.clone.spread_ref) | copy-start | bytes 221188
  21.3 4.4 %collective-permute-start.5 = (f32[56,128]{1,0:T(8,128)S(1)}, f32[56,128]{1,0:T(8,128)S(1)}, u32[]{:S(2)}, u32[]{:S(2)}) collective-permute-start(f32[56,128]{1,0:T(8,128)S(1)} %get-tuple-element.18), channel_id=1, source_target_pairs={{0,128},{16,0},{32,16},{48,32},{64,48},{80,64},{96,80},{112,96},{1... | collective-permute-start | bytes 86024 | tf_op jit(solution)/shard_map/ppermute | solution.py:407
  24.1 3.9 %collective-permute-start.4 = (f32[56,128]{1,0:T(8,128)S(1)}, f32[56,128]{1,0:T(8,128)S(1)}, u32[]{:S(2)}, u32[]{:S(2)}) collective-permute-start(f32[56,128]{1,0:T(8,128)S(1)} %get-tuple-element.19), channel_id=1, source_target_pairs={{0,16},{16,32},{32,48},{48,64},{64,80},{80,96},{96,112},{112,240},... | collective-permute-start | bytes 86024 | tf_op jit(solution)/shard_map/ppermute | solution.py:406

commit v7 on v6

--- a/solution.py
+++ b/solution.py
@@ -120,24 +120,22 @@
 def placed_flows(along_y, power, section, first_col):
     lane = lax.broadcasted_iota(jnp.int32, (8, N), 1)
     offset = ((lane + H) % N - H).astype(F32)
-    pad = jnp.zeros((2, N), F32)
     flows = jnp.zeros((8, N), F32)
-    stacked_y = jnp.concatenate([pad, *along_y, pad], axis=0)
     for side in range(2):
-        columns = jnp.concatenate([pad, *[p[:, side * N : (side + 1) * N] for p in power], pad], axis=0)
-        energy = jnp.sum(columns, axis=1, keepdims=True) * (1.0 / (N * N)) + 1e-6
+        columns = power[:, side * N : (side + 1) * N]
         mine = (lane < H) if side == 0 else (lane >= H)
-        flow_y = jnp.sum(jnp.where(mine, stacked_y, 0.0), axis=1, keepdims=True) * (1.0 / (N * N)) / energy
-        flow_x = jnp.sum(columns * offset, axis=1, keepdims=True) * (1.0 / (N * N)) / energy
+        energy = jnp.sum(columns, axis=1, keepdims=True)
+        sum_y = jnp.sum(jnp.where(mine, along_y, 0.0), axis=1, keepdims=True)
+        sum_x = jnp.sum(columns * offset, axis=1, keepdims=True)
+        scale = (1.0 / (N * N)) / (energy * (1.0 / (N * N)) + 1e-6)
         slot = section * 16 + 2 + first_col + side
-        flows = jnp.where(lane == slot, flow_y, flows)
-        flows = jnp.where(lane == slot + 8, flow_x, flows)
+        flows = jnp.where(lane == slot, sum_y * scale, flows)
+        flows = jnp.where(lane == slot + 8, sum_x * scale, flows)
     return flows
 
 
-def column_flows(sums_y, sums_x, first_unit, section, first_col):
-    units = range(first_unit, first_unit + 4)
-    return placed_flows([sums_y[u] for u in units], [sums_x[u] for u in units], section, first_col)
+def column_flows(sums_y, sums_x, at, section, first_col):
+    return placed_flows(sums_y[at], sums_x[at], section, first_col)
 
 
 def group_lanes(rows):
@@ -187,6 +185,8 @@
     for copy in copies:
         copy.start()
     field_ref[...] = jnp.zeros((64, N), F32)
+    sums_y[...] = jnp.zeros_like(sums_y)
+    sums_x[...] = jnp.zeros_like(sums_x)
     for copy in copies[:2]:
         copy.wait()
     forward = [table_ref[i] for i in range(3)]
@@ -208,10 +208,10 @@
         chain = [before[unit], spec_ref[half, py], spec_ref[2 + half, py]]
         for section in range(2):
             along_y, power = moments(chain[section], chain[section + 1], *inverse)
-            sums_y[8 * section + unit] = along_y
-            sums_x[8 * section + unit] = power
-
-    flows = [sum(column_flows(sums_y, sums_x, 8 * s + 4 * half, s, 2 * (half ^ odd)) for half in range(2)) for s in range(2)]
+            sums_y[2 * section + half, 2 + py : 3 + py, :] = along_y
+            sums_x[2 * section + half, 2 + py : 3 + py, :] = power
+
+    flows = [sum(column_flows(sums_y, sums_x, 2 * s + half, s, 2 * (half ^ odd)) for half in range(2)) for s in range(2)]
     flows_ref[...] = jnp.where(at_start, flows[0], 0.0) + flows[1]
 
     fields = [start_ref[s, c] for s in range(2) for c in range(2)]
@@ -230,12 +230,16 @@
     forward = [table_ref[i] for i in range(3)]
     inverse = [table_ref[i] for i in range(3, 6)]
     own = 2 * (1 - gz)
+    sums_y[0] = jnp.zeros((8, N), F32)
+    sums_x[0] = jnp.zeros((8, 2 * N), F32)
     for py in range(4):
         other[py] = spectrum(jnp.concatenate([recv_ref[py, 0], recv_ref[py, 1]], axis=1), *forward)
     for py in range(4):
         mine, theirs = spec_ref[own, py], other[py]
         prev, cur = jnp.where(gz == 0, mine, theirs), jnp.where(gz == 0, theirs, mine)
-        sums_y[py], sums_x[py] = moments(prev, cur, *inverse)
+        along_y, power = moments(prev, cur, *inverse)
+        sums_y[0, 2 + py : 3 + py, :] = along_y
+        sums_x[0, 2 + py : 3 + py, :] = power
     flows = column_flows(sums_y, sums_x, 0, 0, 2 * (1 - gz))
     middle_ref[...] = flows
     out_ref[0:8, :] = flows_ref[...] + jnp.where(gz == 0, 0.0, flows)
@@ -380,7 +384,7 @@
 
     chunk = lax.dynamic_slice(patches, (1 - gz, 0, 2 * gz, 0, 0), (1, 4, 2, N, N))[0]
     received = lax.ppermute(chunk, "gz", [(0, 1), (1, 0)])
-    sums = [pltpu.VMEM((16, 1, N), F32), pltpu.VMEM((16, 1, 2 * N), F32)]
+    sums = [pltpu.VMEM((4, 8, N), F32), pltpu.VMEM((4, 8, 2 * N), F32)]
     arrays = [patches, prior_patches, start_offset, flow_weight, edges, node_patch, node_weight]
     spec, flows, nodes, far_edge, near_edge, table = call(
         local_kernel, [flags],

time: 29.9 us -> 29.9 us (level)
  no operation moved by 1% of the time
where the time goes in v7:
time: 29.9 us; the launch traced here: 29.8 us
  starting transfers between devices  11.9 us (40%)
  Pallas kernels  9.56 us (32%)
  waiting for transfers between devices  6.52 us (22%)
  local copies, waits for them, and re-layouts  1.02 us (3%)
  between operations  0.73 us (2%)
    pallas_call x4, Pallas kernels, call(): pl.pallas_call(kernel, out_shape=out_shapes, in_specs=[pl.BlockSpec(memor...  9.56 us
    ppermute x1, starting transfers between devices, body(): from_far = lax.ppermute(to_far, ('gz', 'gx'), snake(cols, True))  2.9 us
    ppermute x1, starting transfers between devices, body(): lax.ppermute(jnp.where(down, bottom, top), ('gz', 'gy'), snake(rows, False))  2.82 us
    ppermute x1, starting transfers between devices, body(): lax.ppermute(jnp.concatenate([own, near_edge]), ('gz', 'gx'), snake(cols,...  2.81 us
    ppermute x1, waiting for transfers between devices, body(): lax.ppermute(jnp.where(down, top, bottom), ('gz', 'gy'), snake(rows, True))  2.31 us
    ppermute x1, starting transfers between devices, body(): own_middle = lax.ppermute(middle, 'gz', [(0, 1), (1, 0)])  1.66 us
    ppermute x1, starting transfers between devices, body(): received = lax.ppermute(chunk, 'gz', [(0, 1), (1, 0)])  1.66 us
    ppermute x1, waiting for transfers between devices, body(): from_far = lax.ppermute(to_far, ('gz', 'gx'), snake(cols, True))  1.58 us
  transfers between devices with their start and end apart: 6, of which 5 were waited for; matrix products, arithmetic and copies ran while one was open for 0% of the time, Pallas kernels for 21%

profile of v7, /device:TPU:128, one launch (start us, length us, event | category | flops | bytes accessed | tf_op | source)
XLA Modules:
  0.0 29.8 jit_solution(2823494969561659200)
XLA Ops:
  0.6 1.0 %dynamic-slice_bitcast_fusion = bf16[4,2,128,128]{3,2,1,0:T(8,128)(2,1)S(1)} fusion(bf16[2,4,4,128,128]{4,3,2,1,0:T(8,128)(2,1)} %patches_hbm.1, s32[]{:T(128)S(6)} %select_n.32, s32[]{:T(128)S(6)} %select_n.33), kind=kLoop, calls=%fused_computation | loop fusion | bytes 524296 | tf_op jit(solution)/shard_map/squeeze | solution.py:385
  1.6 1.7 %collective-permute-start = (bf16[4,2,128,128]{3,2,1,0:T(8,128)(2,1)S(1)}, bf16[4,2,128,128]{3,2,1,0:T(8,128)(2,1)S(1)}, u32[]{:S(2)}, u32[]{:S(2)}) collective-permute-start(bf16[4,2,128,128]{3,2,1,0:T(8,128)(2,1)S(1)} %dynamic-slice_bitcast_fusion), channel_id=1, source_target_pairs={{0,128},{128,0},{1,129},{129,1},{2,130},{130,2},{3,131},{131,3},{4... | collective-permute-start | bytes 786440 | tf_op jit(solution)/shard_map/ppermute | solution.py:386
  3.3 0.1 pad_add_fusion.flags_ref
  3.4 5.6 %shard_map.104 = (f32[4,4,128,256]{3,2,1,0:T(8,128)S(1)}, f32[8,128]{1,0:T(8,128)S(1)}, f32[64,128]{1,0:T(8,128)S(1)}, f32[16,128]{1,0:T(8,128)S(1)}, f32[16,128...) custom-call(s32[2]{0:T(128)S(1)} %pad_add_fusion.flags_ref, bf16[6,256,256]{2,1,0:T(8,128)(2,1)} %constant.32.clone.table_hbm, ...), custom_call_target="tpu_custom_call" | custom-call | flops 8000000000 | bytes 4000000 | tf_op jit(solution)/shard_map/pallas_call | solution.py:348
  8.9 0.8 %collective-permute-done.recv_ref = bf16[4,2,128,128]{3,2,1,0:T(8,128)(2,1)S(1)} collective-permute-done((bf16[4,2,128,128]{3,2,1,0:T(8,128)(2,1)S(1)}, bf16[4,2,128,128]{3,2,1,0:T(8,128)(2,1)S(1)}, u32[]{:S(2)}, u32[]{:S(2)}) %collective-permute-start) | collective-permute-done | bytes 262176 | tf_op jit(solution)/shard_map/ppermute | solution.py:386
  9.8 1.6 %shard_map.105 = (f32[24,128]{1,0:T(8,128)S(1)}, f32[8,128]{1,0:T(8,128)S(1)}) custom-call(s32[2]{0:T(128)S(1)} %pad_add_fusion.flags_ref, bf16[4,2,128,128]{3,2,1,0:T(8,128)(2,1)S(1)} %collective-permute-done.recv_ref, f32[4,4,128,256]{3,2,1,0:T(8,128)S(1)} %get-tuple-element.10.spec_ref, f32[8,128]{1,0:T(8,128)S(1)} %get-tuple-element.11.flows_ref, ...), custom_call_target="tpu_custom_call" | custom-call | flops 2000000000 | bytes 2000000 | tf_op jit(solution)/shard_map/pallas_call | solution.py:348
  11.4 1.7 %collective-permute-start.1 = (f32[8,128]{1,0:T(8,128)S(1)}, f32[8,128]{1,0:T(8,128)S(1)}, u32[]{:S(2)}, u32[]{:S(2)}) collective-permute-start(f32[8,128]{1,0:T(8,128)S(1)} %get-tuple-element.15), channel_id=1, source_target_pairs={{0,128},{128,0},{1,129},{129,1},{2,130},{130,2},{3,131},{131,3},{4... | collective-permute-start | bytes 12296 | tf_op jit(solution)/shard_map/ppermute | solution.py:400
  13.0 2.9 %collective-permute-start.2 = (f32[24,128]{1,0:T(8,128)S(1)}, f32[24,128]{1,0:T(8,128)S(1)}, u32[]{:S(2)}, u32[]{:S(2)}) collective-permute-start(f32[24,128]{1,0:T(8,128)S(1)} %get-tuple-element.14), channel_id=1, source_target_pairs={{0,1},{1,2},{2,3},{3,4},{4,5},{5,6},{6,7},{7,8},{8,9},{9,10},{10,1... | collective-permute-start | bytes 36872 | tf_op jit(solution)/shard_map/ppermute | solution.py:401
  15.9 0.0 collective-permute-done.1
  15.9 2.8 %collective-permute-start.3 = (f32[24,128]{1,0:T(8,128)S(1)}, f32[24,128]{1,0:T(8,128)S(1)}, u32[]{:S(2)}, u32[]{:S(2)}) collective-permute-start(f32[24,128]{1,0:T(8,128)S(1)} %pad_maximum_fusion), channel_id=1, source_target_pairs={{0,128},{1,0},{2,1},{3,2},{4,3},{5,4},{6,5},{7,6},{8,7},{9,8},{10,... | collective-permute-start | bytes 36872 | tf_op jit(solution)/shard_map/ppermute | solution.py:403
  18.8 1.6 %collective-permute-done.2.far_ref = f32[24,128]{1,0:T(8,128)S(1)} collective-permute-done((f32[24,128]{1,0:T(8,128)S(1)}, f32[24,128]{1,0:T(8,128)S(1)}, u32[]{:S(2)}, u32[]{:S(2)}) %collective-permute-start.2) | collective-permute-done | bytes 12320 | tf_op jit(solution)/shard_map/ppermute | solution.py:401
  20.3 0.0 copy-start
  20.3 0.6 %shard_map.106 = f32[72,128]{1,0:T(8,128)S(1)} custom-call(s32[2]{0:T(128)S(1)} %pad_add_fusion.flags_ref, f32[8,128]{1,0:T(8,128)S(1)} %multiply_add_fusion.own_ref, f32[64,128]{1,0:T(8,128)S(1)} %get-tuple-element.16.nodes_ref, f32[24,128]{1,0:T(8,128)S(1)} %collective-permute-done.2.far_ref), custom_call_target="tpu_custom_call" | custom-call | flops 5000000000 | bytes 2000000 | tf_op jit(solution)/shard_map/pallas_call | solution.py:348
  21.0 0.2 collective-permute-done.3
  21.3 2.8 %collective-permute-start.5 = (f32[56,128]{1,0:T(8,128)S(1)}, f32[56,128]{1,0:T(8,128)S(1)}, u32[]{:S(2)}, u32[]{:S(2)}) collective-permute-start(f32[56,128]{1,0:T(8,128)S(1)} %get-tuple-element.18), channel_id=1, source_target_pairs={{0,128},{16,0},{32,16},{48,32},{64,48},{80,64},{96,80},{112,96},{1... | collective-permute-start | bytes 86024 | tf_op jit(solution)/shard_map/ppermute | solution.py:411
  24.1 0.0 collective-permute-start.4
  24.1 1.6 %collective-permute-done.5 = f32[56,128]{1,0:T(8,128)S(1)} collective-permute-done((f32[56,128]{1,0:T(8,128)S(1)}, f32[56,128]{1,0:T(8,128)S(1)}, u32[]{:S(2)}, u32[]{:S(2)}) %collective-permute-start.5) | collective-permute-done | bytes 28704 | tf_op jit(solution)/shard_map/ppermute | solution.py:411
  25.7 2.3 %collective-permute-done.4 = f32[56,128]{1,0:T(8,128)S(1)} collective-permute-done((f32[56,128]{1,0:T(8,128)S(1)}, f32[56,128]{1,0:T(8,128)S(1)}, u32[]{:S(2)}, u32[]{:S(2)}) %collective-permute-start.4) | collective-permute-done | bytes 28704 | tf_op jit(solution)/shard_map/ppermute | solution.py:410
  28.0 0.0 copy-done
  28.0 1.8 %shard_map.107 = (f32[2,2,4,4]{3,2,1,0:T(4,128)}, f32[2,2,16,16]{3,2,1,0:T(8,128)}) custom-call(s32[2]{0:T(128)S(1)} %pad_add_fusion.flags_ref, f32[56,128]{1,0:T(8,128)S(1)} %get-tuple-element.27.top_ref, f32[56,128]{1,0:T(8,128)S(1)} %get-tuple-element.26.bottom_ref, f32[56,128]{1,0:T(8,128)S(1)} %broadcast_multiply_fusion.1.early_ref, ...), custom_call_target="tpu_custom_call" | custom-call | tf_op jit(solution)/shard_map/pallas_call | solution.py:348
  (15 shorter events, 0.1 us)
Async XLA Ops:
  1.6 8.1 %collective-permute-start = (bf16[4,2,128,128]{3,2,1,0:T(8,128)(2,1)S(1)}, bf16[4,2,128,128]{3,2,1,0:T(8,128)(2,1)S(1)}, u32[]{:S(2)}, u32[]{:S(2)}) collective-permute-start(bf16[4,2,128,128]{3,2,1,0:T(8,128)(2,1)S(1)} %dynamic-slice_bitcast_fusion), channel_id=1, source_target_pairs={{0,128},{128,0},{1,129},{129,1},{2,130},{130,2},{3,131},{131,3},{4... | collective-permute-start | bytes 786440 | tf_op jit(solution)/shard_map/ppermute | solution.py:386
  11.4 4.6 %collective-permute-start.1 = (f32[8,128]{1,0:T(8,128)S(1)}, f32[8,128]{1,0:T(8,128)S(1)}, u32[]{:S(2)}, u32[]{:S(2)}) collective-permute-start(f32[8,128]{1,0:T(8,128)S(1)} %get-tuple-element.15), channel_id=1, source_target_pairs={{0,128},{128,0},{1,129},{129,1},{2,130},{130,2},{3,131},{131,3},{4... | collective-permute-start | bytes 12296 | tf_op jit(solution)/shard_map/ppermute | solution.py:400
  13.0 7.3 %collective-permute-start.2 = (f32[24,128]{1,0:T(8,128)S(1)}, f32[24,128]{1,0:T(8,128)S(1)}, u32[]{:S(2)}, u32[]{:S(2)}) collective-permute-start(f32[24,128]{1,0:T(8,128)S(1)} %get-tuple-element.14), channel_id=1, source_target_pairs={{0,1},{1,2},{2,3},{3,4},{4,5},{5,6},{6,7},{7,8},{8,9},{9,10},{10,1... | collective-permute-start | bytes 36872 | tf_op jit(solution)/shard_map/ppermute | solution.py:401
  15.9 5.3 %collective-permute-start.3 = (f32[24,128]{1,0:T(8,128)S(1)}, f32[24,128]{1,0:T(8,128)S(1)}, u32[]{:S(2)}, u32[]{:S(2)}) collective-permute-start(f32[24,128]{1,0:T(8,128)S(1)} %pad_maximum_fusion), channel_id=1, source_target_pairs={{0,128},{1,0},{2,1},{3,2},{4,3},{5,4},{6,5},{7,6},{8,7},{9,8},{10,... | collective-permute-start | bytes 36872 | tf_op jit(solution)/shard_map/ppermute | solution.py:403
  20.3 7.7 %copy-start = (bf16[96,384]{1,0:T(8,128)(2,1)S(1)}, bf16[96,384]{1,0:T(8,128)(2,1)}, u32[]{:S(2)}) copy-start(bf16[96,384]{1,0:T(8,128)(2,1)} %constant.33.clone.spread_ref) | copy-start | bytes 221188
  21.3 4.4 %collective-permute-start.5 = (f32[56,128]{1,0:T(8,128)S(1)}, f32[56,128]{1,0:T(8,128)S(1)}, u32[]{:S(2)}, u32[]{:S(2)}) collective-permute-start(f32[56,128]{1,0:T(8,128)S(1)} %get-tuple-element.18), channel_id=1, source_target_pairs={{0,128},{16,0},{32,16},{48,32},{64,48},{80,64},{96,80},{112,96},{1... | collective-permute-start | bytes 86024 | tf_op jit(solution)/shard_map/ppermute | solution.py:411
  24.1 3.9 %collective-permute-start.4 = (f32[56,128]{1,0:T(8,128)S(1)}, f32[56,128]{1,0:T(8,128)S(1)}, u32[]{:S(2)}, u32[]{:S(2)}) collective-permute-start(f32[56,128]{1,0:T(8,128)S(1)} %get-tuple-element.19), channel_id=1, source_target_pairs={{0,16},{16,32},{32,48},{48,64},{64,80},{80,96},{96,112},{112,240},... | collective-permute-start | bytes 86024 | tf_op jit(solution)/shard_map/ppermute | solution.py:410

commit v8 on v7

--- a/solution.py
+++ b/solution.py
@@ -269,7 +269,7 @@
         rows = []
         for block in blocks:
             edge = block[48:56]
-            side = jnp.where(near_on_right, pltpu.roll(edge, (EDGE + 16 - EDGE * at) % N, 1), pltpu.roll(edge, -EDGE * at % N, 1))
+            side = pltpu.roll(edge, jnp.where(near_on_right, (EDGE + 16 - EDGE * at) % N, -EDGE * at % N), 1)
             rows.append(jnp.where((lane >= first) & (lane < first + EDGE), side, block[16 + 8 * at : 24 + 8 * at]))
         return jnp.concatenate(rows, axis=0)
 
@@ -279,11 +279,7 @@
     window = jnp.where(row < 2, pltpu.roll(flows_of(above), 4, 0), jnp.where(row < 6, own_flows, pltpu.roll(flows_of(below), 4, 0)))
 
     narrow = window[:, : 4 * 8]
-    part1 = narrow.astype(BF16)
-    rest = narrow - part1.astype(F32)
-    part2 = rest.astype(BF16)
-    part3 = (rest - part2.astype(F32)).astype(BF16)
-    spread = dot(jnp.concatenate([part1, part2, part3], axis=1), spread_ref[...])
+    spread = dot(jnp.concatenate(halves(narrow), axis=1), spread_ref[...])
     upper = row < 4
     lines = [[jnp.broadcast_to(spread[r : r + 1, b * N : (b + 1) * N], (8, N)) for b in range(3)] for r in range(8)]
 
@@ -332,14 +328,14 @@
 
 @functools.lru_cache(maxsize=None)
 def spread_table():
-    table = np.zeros((3, 32, 3 * N))
+    table = np.zeros((2, 32, 3 * N))
     for b in range(3):
         for lane in range(N):
             group, node = lane // GROUP, lane % GROUP - EDGE
             col = node // 4 + 2 + b - 1
             if 0 <= col < 8 and node < 19:
                 table[:, group * 8 + col, b * N + lane] = 1.0
-    return table.reshape(96, 3 * N).astype(ml_dtypes.bfloat16)
+    return table.reshape(64, 3 * N).astype(ml_dtypes.bfloat16)
 
 
 def call(kernel, inputs, out_shapes, scratch=(), flops=0, moved=0, from_hbm=()):

time: 29.9 us -> 29.9 us (level)
  no operation moved by 1% of the time
where the time goes in v8:
time: 29.9 us; the launch traced here: 29.8 us
  starting transfers between devices  11.9 us (40%)
  Pallas kernels  9.55 us (32%)
  waiting for transfers between devices  6.52 us (22%)
  local copies, waits for them, and re-layouts  1.02 us (3%)
  between operations  0.73 us (2%)
    pallas_call x4, Pallas kernels, call(): pl.pallas_call(kernel, out_shape=out_shapes, in_specs=[pl.BlockSpec(memor...  9.55 us
    ppermute x1, starting transfers between devices, body(): from_far = lax.ppermute(to_far, ('gz', 'gx'), snake(cols, True))  2.9 us
    ppermute x1, starting transfers between devices, body(): lax.ppermute(jnp.where(down, bottom, top), ('gz', 'gy'), snake(rows, False))  2.82 us
    ppermute x1, starting transfers between devices, body(): lax.ppermute(jnp.concatenate([own, near_edge]), ('gz', 'gx'), snake(cols,...  2.81 us
    ppermute x1, waiting for transfers between devices, body(): lax.ppermute(jnp.where(down, top, bottom), ('gz', 'gy'), snake(rows, True))  2.31 us
    ppermute x1, starting transfers between devices, body(): own_middle = lax.ppermute(middle, 'gz', [(0, 1), (1, 0)])  1.66 us
    ppermute x1, starting transfers between devices, body(): received = lax.ppermute(chunk, 'gz', [(0, 1), (1, 0)])  1.66 us
    ppermute x1, waiting for transfers between devices, body(): from_far = lax.ppermute(to_far, ('gz', 'gx'), snake(cols, True))  1.58 us
  transfers between devices with their start and end apart: 6, of which 5 were waited for; matrix products, arithmetic and copies ran while one was open for 0% of the time, Pallas kernels for 21%

profile of v8, /device:TPU:128, one launch (start us, length us, event | category | flops | bytes accessed | tf_op | source)
XLA Modules:
  0.0 29.8 jit_solution(10555453213076571760)
XLA Ops:
  0.6 1.0 %dynamic-slice_bitcast_fusion = bf16[4,2,128,128]{3,2,1,0:T(8,128)(2,1)S(1)} fusion(bf16[2,4,4,128,128]{4,3,2,1,0:T(8,128)(2,1)} %patches_hbm.1, s32[]{:T(128)S(6)} %select_n.32, s32[]{:T(128)S(6)} %select_n.33), kind=kLoop, calls=%fused_computation | loop fusion | bytes 524296 | tf_op jit(solution)/shard_map/squeeze | solution.py:381
  1.6 1.7 %collective-permute-start = (bf16[4,2,128,128]{3,2,1,0:T(8,128)(2,1)S(1)}, bf16[4,2,128,128]{3,2,1,0:T(8,128)(2,1)S(1)}, u32[]{:S(2)}, u32[]{:S(2)}) collective-permute-start(bf16[4,2,128,128]{3,2,1,0:T(8,128)(2,1)S(1)} %dynamic-slice_bitcast_fusion), channel_id=1, source_target_pairs={{0,128},{128,0},{1,129},{129,1},{2,130},{130,2},{3,131},{131,3},{4... | collective-permute-start | bytes 786440 | tf_op jit(solution)/shard_map/ppermute | solution.py:382
  3.3 0.1 pad_add_fusion.flags_ref
  3.4 5.6 %shard_map.104 = (f32[4,4,128,256]{3,2,1,0:T(8,128)S(1)}, f32[8,128]{1,0:T(8,128)S(1)}, f32[64,128]{1,0:T(8,128)S(1)}, f32[16,128]{1,0:T(8,128)S(1)}, f32[16,128...) custom-call(s32[2]{0:T(128)S(1)} %pad_add_fusion.flags_ref, bf16[6,256,256]{2,1,0:T(8,128)(2,1)} %constant.32.clone.table_hbm, ...), custom_call_target="tpu_custom_call" | custom-call | flops 8000000000 | bytes 4000000 | tf_op jit(solution)/shard_map/pallas_call | solution.py:344
  8.9 0.8 %collective-permute-done.recv_ref = bf16[4,2,128,128]{3,2,1,0:T(8,128)(2,1)S(1)} collective-permute-done((bf16[4,2,128,128]{3,2,1,0:T(8,128)(2,1)S(1)}, bf16[4,2,128,128]{3,2,1,0:T(8,128)(2,1)S(1)}, u32[]{:S(2)}, u32[]{:S(2)}) %collective-permute-start) | collective-permute-done | bytes 262176 | tf_op jit(solution)/shard_map/ppermute | solution.py:382
  9.8 1.6 %shard_map.105 = (f32[24,128]{1,0:T(8,128)S(1)}, f32[8,128]{1,0:T(8,128)S(1)}) custom-call(s32[2]{0:T(128)S(1)} %pad_add_fusion.flags_ref, bf16[4,2,128,128]{3,2,1,0:T(8,128)(2,1)S(1)} %collective-permute-done.recv_ref, f32[4,4,128,256]{3,2,1,0:T(8,128)S(1)} %get-tuple-element.10.spec_ref, f32[8,128]{1,0:T(8,128)S(1)} %get-tuple-element.11.flows_ref, ...), custom_call_target="tpu_custom_call" | custom-call | flops 2000000000 | bytes 2000000 | tf_op jit(solution)/shard_map/pallas_call | solution.py:344
  11.4 1.7 %collective-permute-start.1 = (f32[8,128]{1,0:T(8,128)S(1)}, f32[8,128]{1,0:T(8,128)S(1)}, u32[]{:S(2)}, u32[]{:S(2)}) collective-permute-start(f32[8,128]{1,0:T(8,128)S(1)} %get-tuple-element.15), channel_id=1, source_target_pairs={{0,128},{128,0},{1,129},{129,1},{2,130},{130,2},{3,131},{131,3},{4... | collective-permute-start | bytes 12296 | tf_op jit(solution)/shard_map/ppermute | solution.py:396
  13.0 2.9 %collective-permute-start.2 = (f32[24,128]{1,0:T(8,128)S(1)}, f32[24,128]{1,0:T(8,128)S(1)}, u32[]{:S(2)}, u32[]{:S(2)}) collective-permute-start(f32[24,128]{1,0:T(8,128)S(1)} %get-tuple-element.14), channel_id=1, source_target_pairs={{0,1},{1,2},{2,3},{3,4},{4,5},{5,6},{6,7},{7,8},{8,9},{9,10},{10,1... | collective-permute-start | bytes 36872 | tf_op jit(solution)/shard_map/ppermute | solution.py:397
  15.9 0.0 collective-permute-done.1
  15.9 2.8 %collective-permute-start.3 = (f32[24,128]{1,0:T(8,128)S(1)}, f32[24,128]{1,0:T(8,128)S(1)}, u32[]{:S(2)}, u32[]{:S(2)}) collective-permute-start(f32[24,128]{1,0:T(8,128)S(1)} %pad_maximum_fusion), channel_id=1, source_target_pairs={{0,128},{1,0},{2,1},{3,2},{4,3},{5,4},{6,5},{7,6},{8,7},{9,8},{10,... | collective-permute-start | bytes 36872 | tf_op jit(solution)/shard_map/ppermute | solution.py:399
  18.8 1.6 %collective-permute-done.2.far_ref = f32[24,128]{1,0:T(8,128)S(1)} collective-permute-done((f32[24,128]{1,0:T(8,128)S(1)}, f32[24,128]{1,0:T(8,128)S(1)}, u32[]{:S(2)}, u32[]{:S(2)}) %collective-permute-start.2) | collective-permute-done | bytes 12320 | tf_op jit(solution)/shard_map/ppermute | solution.py:397
  20.3 0.0 copy-start
  20.3 0.6 %shard_map.106 = f32[72,128]{1,0:T(8,128)S(1)} custom-call(s32[2]{0:T(128)S(1)} %pad_add_fusion.flags_ref, f32[8,128]{1,0:T(8,128)S(1)} %multiply_add_fusion.own_ref, f32[64,128]{1,0:T(8,128)S(1)} %get-tuple-element.16.nodes_ref, f32[24,128]{1,0:T(8,128)S(1)} %collective-permute-done.2.far_ref), custom_call_target="tpu_custom_call" | custom-call | flops 5000000000 | bytes 2000000 | tf_op jit(solution)/shard_map/pallas_call | solution.py:344
  21.0 0.2 collective-permute-done.3
  21.3 2.8 %collective-permute-start.5 = (f32[56,128]{1,0:T(8,128)S(1)}, f32[56,128]{1,0:T(8,128)S(1)}, u32[]{:S(2)}, u32[]{:S(2)}) collective-permute-start(f32[56,128]{1,0:T(8,128)S(1)} %get-tuple-element.18), channel_id=1, source_target_pairs={{0,128},{16,0},{32,16},{48,32},{64,48},{80,64},{96,80},{112,96},{1... | collective-permute-start | bytes 86024 | tf_op jit(solution)/shard_map/ppermute | solution.py:407
  24.1 0.0 collective-permute-start.4
  24.1 1.6 %collective-permute-done.5 = f32[56,128]{1,0:T(8,128)S(1)} collective-permute-done((f32[56,128]{1,0:T(8,128)S(1)}, f32[56,128]{1,0:T(8,128)S(1)}, u32[]{:S(2)}, u32[]{:S(2)}) %collective-permute-start.5) | collective-permute-done | bytes 28704 | tf_op jit(solution)/shard_map/ppermute | solution.py:407
  25.7 2.3 %collective-permute-done.4 = f32[56,128]{1,0:T(8,128)S(1)} collective-permute-done((f32[56,128]{1,0:T(8,128)S(1)}, f32[56,128]{1,0:T(8,128)S(1)}, u32[]{:S(2)}, u32[]{:S(2)}) %collective-permute-start.4) | collective-permute-done | bytes 28704 | tf_op jit(solution)/shard_map/ppermute | solution.py:406
  28.0 0.0 copy-done
  28.0 1.8 %shard_map.107 = (f32[2,2,4,4]{3,2,1,0:T(4,128)}, f32[2,2,16,16]{3,2,1,0:T(8,128)}) custom-call(s32[2]{0:T(128)S(1)} %pad_add_fusion.flags_ref, f32[56,128]{1,0:T(8,128)S(1)} %get-tuple-element.27.top_ref, f32[56,128]{1,0:T(8,128)S(1)} %get-tuple-element.26.bottom_ref, f32[56,128]{1,0:T(8,128)S(1)} %broadcast_multiply_fusion.1.early_ref, ...), custom_call_target="tpu_custom_call" | custom-call | tf_op jit(solution)/shard_map/pallas_call | solution.py:344
  (15 shorter events, 0.1 us)
Async XLA Ops:
  1.6 8.1 %collective-permute-start = (bf16[4,2,128,128]{3,2,1,0:T(8,128)(2,1)S(1)}, bf16[4,2,128,128]{3,2,1,0:T(8,128)(2,1)S(1)}, u32[]{:S(2)}, u32[]{:S(2)}) collective-permute-start(bf16[4,2,128,128]{3,2,1,0:T(8,128)(2,1)S(1)} %dynamic-slice_bitcast_fusion), channel_id=1, source_target_pairs={{0,128},{128,0},{1,129},{129,1},{2,130},{130,2},{3,131},{131,3},{4... | collective-permute-start | bytes 786440 | tf_op jit(solution)/shard_map/ppermute | solution.py:382
  11.4 4.6 %collective-permute-start.1 = (f32[8,128]{1,0:T(8,128)S(1)}, f32[8,128]{1,0:T(8,128)S(1)}, u32[]{:S(2)}, u32[]{:S(2)}) collective-permute-start(f32[8,128]{1,0:T(8,128)S(1)} %get-tuple-element.15), channel_id=1, source_target_pairs={{0,128},{128,0},{1,129},{129,1},{2,130},{130,2},{3,131},{131,3},{4... | collective-permute-start | bytes 12296 | tf_op jit(solution)/shard_map/ppermute | solution.py:396
  13.0 7.3 %collective-permute-start.2 = (f32[24,128]{1,0:T(8,128)S(1)}, f32[24,128]{1,0:T(8,128)S(1)}, u32[]{:S(2)}, u32[]{:S(2)}) collective-permute-start(f32[24,128]{1,0:T(8,128)S(1)} %get-tuple-element.14), channel_id=1, source_target_pairs={{0,1},{1,2},{2,3},{3,4},{4,5},{5,6},{6,7},{7,8},{8,9},{9,10},{10,1... | collective-permute-start | bytes 36872 | tf_op jit(solution)/shard_map/ppermute | solution.py:397
  15.9 5.3 %collective-permute-start.3 = (f32[24,128]{1,0:T(8,128)S(1)}, f32[24,128]{1,0:T(8,128)S(1)}, u32[]{:S(2)}, u32[]{:S(2)}) collective-permute-start(f32[24,128]{1,0:T(8,128)S(1)} %pad_maximum_fusion), channel_id=1, source_target_pairs={{0,128},{1,0},{2,1},{3,2},{4,3},{5,4},{6,5},{7,6},{8,7},{9,8},{10,... | collective-permute-start | bytes 36872 | tf_op jit(solution)/shard_map/ppermute | solution.py:399
  20.3 7.7 %copy-start = (bf16[64,384]{1,0:T(8,128)(2,1)S(1)}, bf16[64,384]{1,0:T(8,128)(2,1)}, u32[]{:S(2)}) copy-start(bf16[64,384]{1,0:T(8,128)(2,1)} %constant.33.clone.spread_ref) | copy-start | bytes 147460
  21.3 4.4 %collective-permute-start.5 = (f32[56,128]{1,0:T(8,128)S(1)}, f32[56,128]{1,0:T(8,128)S(1)}, u32[]{:S(2)}, u32[]{:S(2)}) collective-permute-start(f32[56,128]{1,0:T(8,128)S(1)} %get-tuple-element.18), channel_id=1, source_target_pairs={{0,128},{16,0},{32,16},{48,32},{64,48},{80,64},{96,80},{112,96},{1... | collective-permute-start | bytes 86024 | tf_op jit(solution)/shard_map/ppermute | solution.py:407
  24.1 3.9 %collective-permute-start.4 = (f32[56,128]{1,0:T(8,128)S(1)}, f32[56,128]{1,0:T(8,128)S(1)}, u32[]{:S(2)}, u32[]{:S(2)}) collective-permute-start(f32[56,128]{1,0:T(8,128)S(1)} %get-tuple-element.19), channel_id=1, source_target_pairs={{0,16},{16,32},{32,48},{48,64},{64,80},{80,96},{96,112},{112,240},... | collective-permute-start | bytes 86024 | tf_op jit(solution)/shard_map/ppermute | solution.py:406
